TPU v7x, 32 devices: a whole 2x2x4 slice. The times are simulated.
32 devices in a mesh: grid: 8 (over z, y), spec: 4 (over x, core).
Axes of the slice: x: 2, y: 2, z: 4, core: 2. Of those that a mesh axis runs over, the one named last changes fastest.
Arguments:
- energy: float32 [36, 36, 32, 128], P('spec', None, 'grid'), may hold values from 0.05 to 1
- nest_energy: float32 [36, 36, 32, 128], P('spec', None, 'grid'), may hold values from 0.05 to 1
- ocean_mask: int32 [32, 128], P('grid'), may hold values 0 or 1
- wind_field: float32 [2, 32, 128], P(None, 'grid'), may hold values from -6 to 6
- rim_cell: int32 [1024, 2], P('grid'), may hold values from 0 to 126, as said below
- rim_dest: int32 [1024, 1], P('grid'), may hold values from 0 to 7; in each aligned block of 128 rows (0 to 127, 128 to 255, ...) at most 32 rows name the same one
- rim_target: int32 [1024], P('grid'), may hold values from 0 to 511
- rim_weight: float32 [1024, 3], P('grid'), may hold values from 0.1 to 0.9
Outputs:
- global_next: float32 [36, 36, 32, 128], P('spec', None, 'grid')
- nest_next: float32 [36, 36, 32, 128], P('spec', None, 'grid')
Inputs may be any that keep to these rules, and one draw needn't show every extreme that they name: `rim_cell`: rows of device g of the grid axis have column 0 between g * 4 and (g + 1) * 4 - 1; column 1 is at most 126. `rim_dest`: the 128 rows of one device name any one nest device at most 32 times, and some device's rows name one exactly 32 times.
All inputs are finite; a program needn't handle non-finite values. No bound on the sum of `ocean_mask` on one device may be relied on, other than what follows from the above.
Results may differ from a plain program's by a relative error of at most 0.003.
Values may be sent and summed in bfloat16 or wider, within the bound.
No kernel may reach another device: no remote copies, remote signals or barrier semaphores. Data moves between devices by JAX's collectives and lax.ppermute only.
A program may use at most 64 MiB of HBM per device.

v0:
```python
import jax
import jax.numpy as jnp
from jax import lax
from jax.sharding import PartitionSpec as P

FREQS = 36
ANGLES = 36


ratio_step = 1.1
speed_coef = 0.054
wind_coef = 0.05
dissip_coef = 0.2
nonlin_coef = 0.12
nest_speedup = 2.0
band_reach = 5


def extended_2(x, sides, width, wrap):
    for axis, dim in sides:
        peers, length = (lax.axis_size(axis), x.shape[dim])
        up = [(i, (i + 1) % peers) for i in range(peers if wrap else peers - 1)]
        down = [(j, i) for i, j in up]
        last = lax.slice_in_dim(x, length - width, length, axis=dim)
        leading = lax.slice_in_dim(x, 0, width, axis=dim)
        before = lax.ppermute(last, axis, up)
        after = lax.ppermute(leading, axis, down)
        x = jnp.concatenate([before, x, after], axis=dim)
    return x


def passed_along(block, axis, distance):
    devices = range(lax.axis_size(axis))
    route = [((i - distance) % len(devices), i) for i in devices]
    return lax.ppermute(block, axis, route)


def freq_ratio(first_band, band_count):
    band_ranks = jnp.asarray(first_band).astype(jnp.float32) + jnp.arange(band_count).astype(
        jnp.float32
    )
    return jnp.power(jnp.float32(ratio_step), band_ranks - FREQS // 2)


def lat_secant(lat_rows):
    lat_degrees = -60.0 + 120.0 * (jnp.arange(lat_rows).astype(jnp.float32) + 0.5) / lat_rows
    return 1.0 / jnp.cos(lat_degrees * (jnp.pi / 180.0))


def headings():
    return 2.0 * jnp.pi * jnp.arange(ANGLES).astype(jnp.float32) / ANGLES


def courant_pair(ratios, lat_scale, speedup):
    group_speed = speedup * speed_coef / ratios
    heading = headings()
    along_lon = (
        group_speed[:, None, None, None]
        * jnp.cos(heading)[None, :, None, None]
        * lat_scale[None, None, None, :]
    )
    along_lat = group_speed[:, None, None, None] * jnp.sin(heading)[None, :, None, None]
    return (along_lon, along_lat)


def advect(padded, along_lon, along_lat):
    center = padded[:, :, 1:-1]
    west_cells = padded[:, :, :-2]
    east_cells = padded[:, :, 2:]
    zeros_row = jnp.zeros_like(center[..., :1])
    south_cells = jnp.concatenate([zeros_row, center[..., :-1]], axis=3)
    north_cells = jnp.concatenate([center[..., 1:], zeros_row], axis=3)
    flux_lon = jnp.maximum(along_lon, 0.0) * (center - west_cells) + jnp.minimum(along_lon, 0.0) * (
        east_cells - center
    )
    flux_lat = jnp.maximum(along_lat, 0.0) * (center - south_cells) + jnp.minimum(
        along_lat, 0.0
    ) * (north_cells - center)
    return center - flux_lon - flux_lat


def nonlinear(banded, ratios_padded):
    band_count = banded.shape[0] - 2 * band_reach
    centre = banded[3 : band_count + 8]
    strength = nonlin_coef * ratios_padded[3 : band_count + 8][:, None, None, None]
    result = jnp.zeros_like(banded[band_reach : band_reach + band_count])
    for mirror in (1, -1):
        upper_pair = jnp.roll(banded[5 : band_count + 10], -3 * mirror, axis=1)
        lower_pair = jnp.roll(banded[0 : band_count + 5], mirror, axis=1)
        transfer = strength * (
            centre * centre * (upper_pair + lower_pair) - 2.0 * centre * upper_pair * lower_pair
        )
        result = (
            result
            - 2.0 * transfer[2 : band_count + 2]
            + jnp.roll(transfer[0:band_count], 3 * mirror, axis=1)
            + jnp.roll(transfer[5 : band_count + 5], -mirror, axis=1)
        )
    return result


def step_sources(advected, banded, ratios, ratios_padded, wind_block, mean_energy):
    heading = headings()
    along_wind = jnp.maximum(
        wind_block[0][None, None] * jnp.cos(heading)[None, :, None, None]
        + wind_block[1][None, None] * jnp.sin(heading)[None, :, None, None],
        0.0,
    )
    wind_gain = wind_coef * ratios[:, None, None, None] * along_wind * advected
    transfer = nonlinear(banded, ratios_padded)
    return (advected + wind_gain + transfer) / (
        1.0 + dissip_coef * (ratios * ratios)[:, None, None, None] * mean_energy[None, None]
    )


def interpolate(spectra_flat, base_cell, east_cell, rim_weight):
    east_share = rim_weight[:, 0]
    north_share = rim_weight[:, 1]
    corner_sw = jnp.take(spectra_flat, base_cell, axis=1)
    corner_nw = jnp.take(spectra_flat, base_cell + 1, axis=1)
    corner_se = jnp.take(spectra_flat, east_cell, axis=1)
    corner_ne = jnp.take(spectra_flat, east_cell + 1, axis=1)
    mixed = (1.0 - east_share) * (1.0 - north_share) * corner_sw + (
        1.0 - east_share
    ) * north_share * corner_nw
    mixed = (
        mixed + east_share * (1.0 - north_share) * corner_se + east_share * north_share * corner_ne
    )
    return mixed.astype(jnp.bfloat16)


def blend(totals, nest_flat, spectra, targets, weights):
    picked = jnp.take(nest_flat, targets, axis=1)
    return totals.at[:, targets].add(weights[None, :] * (spectra.astype(jnp.float32) - picked))


def per_device(
    energy, nest_energy, ocean_mask, wind_field, rim_cell, rim_dest, rim_target, rim_weight
):
    grid_rank = lax.axis_index("grid")
    grid_count = lax.axis_size("grid")
    quarter_count = grid_count // 4
    bands_dev = energy.shape[0]
    lon_dev = energy.shape[2]
    lat_rows = energy.shape[3]
    bin_count = bands_dev * ANGLES
    first_band = lax.axis_index("spec") * bands_dev
    ratios = freq_ratio(first_band, bands_dev)
    global_padded = extended_2(energy, (("grid", 2),), 1, True)
    nest_padded = extended_2(nest_energy, (("grid", 2),), 1, True)
    lower_keep = jnp.logical_and(grid_rank != quarter_count, grid_rank != 3 * quarter_count)
    upper_keep = jnp.logical_and(grid_rank != quarter_count - 1, grid_rank != 3 * quarter_count - 1)
    nest_padded = jnp.concatenate(
        [
            nest_padded[:, :, :1] * lower_keep.astype(jnp.float32),
            nest_padded[:, :, 1:-1],
            nest_padded[:, :, -1:] * upper_keep.astype(jnp.float32),
        ],
        axis=2,
    )
    along_lon, along_lat = courant_pair(ratios, lat_secant(lat_rows), 1.0)
    advected = advect(global_padded, along_lon, along_lat) * ocean_mask.astype(jnp.float32)
    band_weight = 0.1 * ratios
    partial_value = jnp.sum(band_weight[:, None, None, None] * advected, axis=(0, 1))
    total_energy = lax.psum(partial_value, "spec")
    mean_energy = total_energy / (ANGLES * (0.1 * jnp.sum(freq_ratio(0, FREQS))))
    banded = extended_2(advected, (("spec", 0),), band_reach, False)
    ratios_padded = freq_ratio(first_band - band_reach, bands_dev + 2 * band_reach)
    global_next = step_sources(advected, banded, ratios, ratios_padded, wind_field, mean_energy)
    east_column = passed_along(global_next[:, :, :1], "grid", -1)
    extended = jnp.concatenate([global_next, east_column], axis=2).reshape(
        bin_count, (lon_dev + 1) * lat_rows
    )
    local_col = rim_cell[:, 0] - grid_rank * lon_dev
    base_cell = local_col * lat_rows + rim_cell[:, 1]
    east_cell = base_cell + lat_rows
    boundary = interpolate(extended, base_cell, east_cell, rim_weight)
    nest_lon, nest_lat = courant_pair(ratios, jnp.ones((lat_rows,), jnp.float32), nest_speedup)
    nest_flat = advect(nest_padded, nest_lon, nest_lat).reshape(bin_count, lon_dev * lat_rows)
    dest_rows = rim_dest[:, 0]
    relax_rate = rim_weight[:, 2]
    rim_rows = dest_rows.shape[0]
    slot_cap = max(2, (2 * rim_rows + grid_count - 1) // grid_count)
    one_hot = (dest_rows[:, None] == jnp.arange(grid_count, dtype=jnp.int32)[None, :]).astype(
        jnp.int32
    )
    earlier = jnp.cumsum(one_hot, axis=0) - one_hot
    slot_rank = jnp.sum(earlier * one_hot, axis=1)
    position = dest_rows * slot_cap + slot_rank
    packed_spectra = (
        jnp.zeros((bin_count, grid_count * slot_cap), jnp.bfloat16).at[:, position].set(boundary)
    )
    packed_target = jnp.zeros((1, grid_count * slot_cap), jnp.int32).at[0, position].set(rim_target)
    packed_relax = (
        jnp.zeros((1, grid_count * slot_cap), jnp.float32).at[0, position].set(relax_rate)
    )
    spectra, targets, relaxes = (
        lax.all_to_all(packed_spectra, "grid", split_axis=1, concat_axis=1, tiled=True),
        lax.all_to_all(packed_target, "grid", split_axis=1, concat_axis=1, tiled=True),
        lax.all_to_all(
            packed_relax.astype(jnp.bfloat16), "grid", split_axis=1, concat_axis=1, tiled=True
        ).astype(packed_relax.dtype),
    )
    increments = blend(jnp.zeros_like(nest_flat), nest_flat, spectra, targets[0], relaxes[0])
    nest_next = (nest_flat + increments).reshape(bands_dev, ANGLES, lon_dev, lat_rows)
    return (global_next, nest_next)


def solution(mesh):
    in_specs = (
        P("spec", None, "grid", None),
        P("spec", None, "grid", None),
        P("grid", None),
        P(None, "grid", None),
        P("grid", None),
        P("grid", None),
        P("grid"),
        P("grid", None),
    )
    out_specs = (P("spec", None, "grid", None), P("spec", None, "grid", None))
    return jax.shard_map(
        per_device, mesh=mesh, in_specs=in_specs, out_specs=out_specs, check_vma=False
    )
```

profile of v0, /device:TPU:0, one launch (start us, length us, event | category | flops | bytes accessed | tf_op | source)
XLA Modules:
  0.0 93.2 jit_solution(8873416457964179319)
XLA Ops:
  0.6 1.2 %copy.50 = f32[9,36,4,128]{3,1,2,0:T(8,128)S(1)} copy(f32[9,36,4,128]{3,2,1,0:T(4,128)} %param.10) | data formatting | bytes 1327104 | tf_op args[0]
  1.9 3.0 %collective-permute-start = (f32[9,36,1,128]{3,1,2,0:T(8,128)S(1)}, f32[9,36,1,128]{3,1,2,0:T(8,128)S(1)}, u32[]{:S(2)}, u32[]{:S(2)}) collective-permute-start(f32[9,36,1,128]{3,1,2,0:T(8,128)S(1)} %get-tuple-element.27), channel_id=1, source_target_pairs={{0,4},{4,8},{8,12},{12,16},{16,20},{20,24},{24,28},{28,0},{1,5},{5... | collective-permute-start | bytes 497672 | tf_op jit(solution)/shard_map/ppermute | solution.py:26
  4.9 3.1 %collective-permute-start.1 = (f32[9,36,1,128]{3,1,2,0:T(8,128)S(1)}, f32[9,36,1,128]{3,1,2,0:T(8,128)S(1)}, u32[]{:S(2)}, u32[]{:S(2)}) collective-permute-start(f32[9,36,1,128]{3,1,2,0:T(8,128)S(1)} %get-tuple-element.28), channel_id=1, source_target_pairs={{4,0},{8,4},{12,8},{16,12},{20,16},{24,20},{28,24},{0,28},{5,1},{9... | collective-permute-start | bytes 497672 | tf_op jit(solution)/shard_map/ppermute | solution.py:27
  8.0 0.3 fusion.78
  8.3 0.7 copy.69
  9.0 0.7 copy.70
  9.7 4.7 %collective-permute-start.5 = (f32[9,36,1,128]{3,1,2,0:T(8,128)}, f32[9,36,1,128]{3,1,2,0:T(8,128)}, u32[]{:S(2)}, u32[]{:S(2)}) collective-permute-start(f32[9,36,1,128]{3,1,2,0:T(8,128)} %copy.70), channel_id=1, source_target_pairs={{4,0},{8,4},{12,8},{16,12},{20,16},{24,20},{28,24},{0,28},{5,1},{9... | collective-permute-start | bytes 497672 | tf_op jit(solution)/shard_map/ppermute | solution.py:27
  14.5 0.2 reduce_window_sum.11
  14.7 0.2 select_reduce_fusion
  14.9 1.0 %scatter_custom_fusion.1 = f32[256]{0:T(256)S(1)} fusion(s32[128]{0:T(128)S(1)} %fusion.58, f32[128]{0:T(128)S(1)} %slice_bitcast_fusion.2, f32[]{:T(128)} %constant.55.clone.1), kind=kCustom, calls=%fused_computation.143 | custom fusion | bytes 1028 | tf_op jit(solution)/shard_map/scatter | solution.py:195
  15.9 0.7 all_to_all.24
  16.6 3.3 %all-to-all-start.1 = ((bf16[1,8,32]{2,0,1:T(2,128)(2,1)}), bf16[1,8,32]{2,0,1:T(2,128)(2,1)S(1)}, u32[]{:S(2)}, u32[]{:S(2)}) async-start(bf16[1,8,32]{2,0,1:T(2,128)(2,1)} %all_to_all.24), calls=%async_computation.1 | async-start | bytes 8192 | tf_op jit(solution)/shard_map/all_to_all | solution.py:200
  20.0 0.6 broadcast_multiply_fusion.4
  20.6 1.1 %fusion.76 = (f32[9,36,4,127]{3,1,2,0:T(8,128)S(1)}, f32[9,36,4,127]{3,1,2,0:T(8,128)}) fusion(f32[9,36,4,128]{3,1,2,0:T(8,128)S(1)} %copy.50), kind=kLoop, calls=%fused_computation.172 | loop fusion | bytes 2633472 | tf_op jit(solution)/shard_map/slice | solution.py:71
  21.8 0.6 multiply_multiply_fusion
  22.3 0.6 fusion.66
  22.9 1.4 %fusion.77 = (f32[9,36,4,127]{3,2,1,0:T(4,128)}, f32[9,36,4,127]{3,2,1,0:T(4,128)}) fusion(f32[9,36,4,128]{3,2,1,0:T(4,128)S(1)} %copy-done), kind=kLoop, calls=%fused_computation.173 | loop fusion | bytes 2633472 | tf_op jit(solution)/shard_map/slice | solution.py:71
  24.4 0.6 convert_element_type.96
  25.0 0.6 slice_multiply_fusion.2
  25.6 0.6 compare_and_fusion.2
  26.2 0.7 multiply_maximum_fusion.2
  26.9 0.1 multiply_maximum_fusion
  27.1 0.6 pad_clamp_fusion.1
  27.7 0.6 pad_clamp_fusion.3
  28.3 1.1 %scatter_custom_fusion = s32[256]{0:T(256)S(1)} fusion(s32[128]{0:T(128)S(1)} %fusion.58, s32[128]{0:T(128)} %param.16, s32[]{:T(128)} %constant.70.clone.1), kind=kCustom, calls=%fused_computation.145 | custom fusion | bytes 1536 | tf_op jit(solution)/shard_map/scatter | solution.py:193
  29.4 0.7 all_to_all.18
  30.0 0.6 power_reduce_fusion
  31.2 5.9 %all-to-all-start = ((s32[1,8,32]{2,0,1:T(1,128)}), s32[1,8,32]{2,0,1:T(1,128)S(1)}, u32[]{:S(2)}, u32[]{:S(2)}) async-start(s32[1,8,32]{2,0,1:T(1,128)} %all_to_all.18), calls=%async_computation | async-start | bytes 8192 | tf_op jit(solution)/shard_map/all_to_all | solution.py:199
  37.2 0.7 reshape.370
  37.9 5.8 %all-to-all-done = s32[1,8,32]{2,0,1:T(1,128)S(1)} async-done(((s32[1,8,32]{2,0,1:T(1,128)}), s32[1,8,32]{2,0,1:T(1,128)S(1)}, u32[]{:S(2)}, u32[]{:S(2)}) %all-to-all-start) | async-done | bytes 1056 | tf_op jit(solution)/shard_map/all_to_all | solution.py:199
  43.6 0.5 broadcast.647
  44.1 0.6 reduce.9
  44.9 0.5 compare_and_fusion.4
  45.4 0.7 copy-done.3
  46.1 2.4 %multiply_reduce_fusion = (f32[4,128]{1,0:T(4,128)}, f32[9,36,4,128]{3,1,2,0:T(8,128)S(1)}) fusion(f32[9]{0:T(128)} %broadcast_multiply_fusion.4, f32[4,128]{1,0:T(4,128)} %convert_element_type.96, f32[9,36,4,128]{3,1,2,0:T(8,128)S(1)} %copy.50, f32[9,36,4,127]{3,1,2,0:T(8,128)} %get-tuple-element.30, f32[9,36]{1,0:T(8,128)S(1)} %get-tuple-element.56, ...), kind=kLoop, calls=%fused_computation.56 | loop fusion | flops 2819584 | bytes 3314116 | tf_op jit(solution)/shard_map/reduce_sum | solution.py:164
  48.6 1.3 %collective-permute-start.2 = (f32[5,36,4,128]{3,1,2,0:T(8,128)S(1)}, f32[5,36,4,128]{3,1,2,0:T(8,128)S(1)}, u32[]{:S(2)}, u32[]{:S(2)}) collective-permute-start(f32[5,36,4,128]{3,1,2,0:T(8,128)S(1)} %get-tuple-element.25), channel_id=1, source_target_pairs={{0,1},{1,2},{2,3},{4,5},{5,6},{6,7},{8,9},{9,10},{10,11},{12,13},{... | collective-permute-start | bytes 1105928 | tf_op jit(solution)/shard_map/ppermute | solution.py:26
  49.9 1.3 %collective-permute-start.3 = (f32[5,36,4,128]{3,1,2,0:T(8,128)S(1)}, f32[5,36,4,128]{3,1,2,0:T(8,128)S(1)}, u32[]{:S(2)}, u32[]{:S(2)}) collective-permute-start(f32[5,36,4,128]{3,1,2,0:T(8,128)S(1)} %get-tuple-element.26), channel_id=1, source_target_pairs={{1,0},{2,1},{3,2},{5,4},{6,5},{7,6},{9,8},{10,9},{11,10},{13,12},{... | collective-permute-start | bytes 1105928 | tf_op jit(solution)/shard_map/ppermute | solution.py:27
  51.2 9.1 %psum.7 = f32[4,128]{1,0:T(4,128)S(1)} all-reduce(f32[4,128]{1,0:T(4,128)S(1)} %copy-done.8), channel_id=1, replica_groups=mesh['grid'=8,'spec'=4] {'spec'}, use_global_device_ids=true, to_apply=%region_1.0 | all-reduce | flops 512 | bytes 4096 | tf_op jit(solution)/shard_map/psum | solution.py:165
  60.5 0.1 fusion.2
  60.7 0.2 fusion.1
  60.9 0.4 copy-done.27
  61.3 0.8 subtract_multiply_fusion.1
  62.4 0.5 copy-done.26
  62.9 0.7 fusion.8
  63.6 0.6 collective-permute-start.6
  64.3 0.9 %broadcast_multiply_fusion.1 = f32[9,36,1,128]{3,1,2,0:T(8,128)S(1)} fusion(f32[9,36,1,128]{3,1,2,0:T(8,128)} %collective-permute-done.4, f32[]{:T(128)S(6)} %convert_element_type.99), kind=kLoop, calls=%fused_computation.99 | loop fusion | flops 41472 | bytes 331780 | tf_op jit(solution)/shard_map/mul | solution.py:155
  65.2 4.9 %collective-permute-done.6 = f32[9,36,1,128]{3,1,2,0:T(8,128)S(1)} collective-permute-done((f32[9,36,1,128]{3,1,2,0:T(8,128)S(1)}, f32[9,36,1,128]{3,1,2,0:T(8,128)S(1)}, u32[]{:S(2)}, u32[]{:S(2)}) %collective-permute-start.6) | collective-permute-done | bytes 165920 | tf_op jit(solution)/shard_map/ppermute | solution.py:35
  70.2 0.2 copy.60
  70.5 0.2 copy.72
  70.8 0.3 copy.61
  71.1 0.2 copy-done.4
  71.5 3.2 %scatter_custom_fusion.2 = bf16[324,256]{0,1:T(8,128)(2,1)} fusion(s32[128]{0:T(128)} %copy-done.28, f32[]{:T(128)} %constant.35.clone.1, f32[128]{0:T(128)S(1)} %copy-done.17, f32[128]{0:T(128)S(1)} %copy-done.16, f32[128]{0:T(128)S(1)} %copy-done.15, f32[128]{0:T(128)S(1)} %copy-done.14, bf16[]{:T(256)} %constant.30.clone.1, ...), kind=kCustom, calls=%fused_computation.87 | custom fusion | flops 497664 | bytes 4119552 | tf_op jit(solution)/shard_map/scatter | solution.py:191
  74.7 4.7 %all-to-all-start.2 = ((bf16[324,8,32]{0,2,1:T(8,128)(2,1)}), bf16[324,8,32]{0,2,1:T(8,128)(2,1)S(1)}, u32[]{:S(2)}, u32[]{:S(2)}) async-start(bf16[324,8,32]{0,2,1:T(8,128)(2,1)} %bitcast.15), calls=%async_computation.2 | async-start | bytes 393216 | tf_op jit(solution)/shard_map/all_to_all | solution.py:198
  79.4 0.9 %broadcast_multiply_fusion = f32[9,36,1,128]{3,1,2,0:T(8,128)S(1)} fusion(f32[9,36,1,128]{3,1,2,0:T(8,128)} %collective-permute-done.5, f32[]{:T(128)S(6)} %convert_element_type.100), kind=kLoop, calls=%fused_computation.98 | loop fusion | flops 41472 | bytes 331780 | tf_op jit(solution)/shard_map/mul | solution.py:157
  80.3 0.2 copy.56
  80.5 0.2 copy.58
  80.7 2.1 %fusion.27 = f32[9,36,4,128]{3,2,1,0:T(4,128)S(1)} fusion(f32[9,36,4,128]{3,2,1,0:T(4,128)S(1)} %copy-done, f32[9,36,1,128]{3,2,1,0:T(1,128)S(1)} %copy.58, f32[9,36,1,128]{3,2,1,0:T(1,128)S(1)} %copy.56, f32[9,36,4,127]{3,2,1,0:T(4,128)S(1)} %copy-done.2, f32[9,36,4,127]{3,2,1,0:T(4,128)S(1)} %copy-done.1, f32[9,36]{1,0:T(8,128)S(1)} %get-tuple-element.58, ...), kind=kLoop, calls=%fused_computation.62 | loop fusion | flops 2322432 | bytes 2980800 | tf_op jit(solution)/shard_map/sub | solution.py:79
  82.8 0.1 pad.66
  83.0 0.3 copy.66
  83.2 1.0 %copy.68 = f32[9,36,4,128]{3,2,1,0:T(4,128)} copy(f32[9,36,4,128]{3,1,2,0:T(8,128)S(1)} %fusion.8) | data formatting | bytes 1327104
  84.3 4.1 %all-to-all-done.2 = bf16[324,8,32]{0,2,1:T(8,128)(2,1)S(1)} async-done(((bf16[324,8,32]{0,2,1:T(8,128)(2,1)}), bf16[324,8,32]{0,2,1:T(8,128)(2,1)S(1)}, u32[]{:S(2)}, u32[]{:S(2)}) %all-to-all-start.2) | async-done | bytes 165920 | tf_op jit(solution)/shard_map/all_to_all | solution.py:198
  88.4 3.5 %scatter_custom_fusion.3 = f32[324,512]{0,1:T(8,128)S(1)} fusion(f32[324,512]{0,1:T(8,128)S(1)} %copy.66, s32[256]{0:T(256)} %bitcast.116, bf16[324,256]{0,1:T(8,128)(2,1)S(1)} %bitcast.113, f32[]{:T(128)} %constant.35.clone.1, f32[256]{0:T(256)S(1)} %copy-done.9, pred[256]{0:T(512)(128)(4,1)S(1)} %copy-done.25, s32[1024]{0:T(1024)S(1)} %pad_clamp_fusion), kind=kCustom, calls=%fused_computation.69 | custom fusion | flops 414720 | bytes 1498880 | tf_op jit(solution)/shard_map/scatter-add | solution.py:134
  91.9 0.2 copy.67
  92.1 1.1 %reshape.369 = f32[9,36,4,128]{3,2,1,0:T(4,128)} reshape(f32[324,512]{1,0:T(8,128)S(1)} %copy.67) | data formatting | bytes 1327104 | tf_op jit(solution)/shard_map/reshape | solution.py:205
  (95 shorter events, 1.4 us)
Async XLA Ops:
  0.6 7.4 %copy-start = (f32[9,36,4,128]{3,2,1,0:T(4,128)S(1)}, f32[9,36,4,128]{3,2,1,0:T(4,128)}, u32[]{:S(2)}) copy-start(f32[9,36,4,128]{3,2,1,0:T(4,128)} %param.11) | copy-start | bytes 1990660
  1.9 12.6 %copy-start.12 = (s32[128,1]{0,1:T(1,128)S(1)}, s32[128,1]{0,1:T(1,128)}, u32[]{:S(2)}) copy-start(s32[128,1]{0,1:T(1,128)} %param.15) | copy-start | bytes 1540
  1.9 13.0 %copy-start.23 = (f32[128,3]{0,1:T(4,128)S(1)}, f32[128,3]{0,1:T(4,128)}, u32[]{:S(2)}) copy-start(f32[128,3]{0,1:T(4,128)} %param.17) | copy-start | bytes 4612
  1.9 43.5 %collective-permute-start = (f32[9,36,1,128]{3,1,2,0:T(8,128)S(1)}, f32[9,36,1,128]{3,1,2,0:T(8,128)S(1)}, u32[]{:S(2)}, u32[]{:S(2)}) collective-permute-start(f32[9,36,1,128]{3,1,2,0:T(8,128)S(1)} %get-tuple-element.27), channel_id=1, source_target_pairs={{0,4},{4,8},{8,12},{12,16},{16,20},{20,24},{24,28},{28,0},{1,5},{5... | collective-permute-start | bytes 497672 | tf_op jit(solution)/shard_map/ppermute | solution.py:26
  4.9 40.5 %collective-permute-start.1 = (f32[9,36,1,128]{3,1,2,0:T(8,128)S(1)}, f32[9,36,1,128]{3,1,2,0:T(8,128)S(1)}, u32[]{:S(2)}, u32[]{:S(2)}) collective-permute-start(f32[9,36,1,128]{3,1,2,0:T(8,128)S(1)} %get-tuple-element.28), channel_id=1, source_target_pairs={{4,0},{8,4},{12,8},{16,12},{20,16},{24,20},{28,24},{0,28},{5,1},{9... | collective-permute-start | bytes 497672 | tf_op jit(solution)/shard_map/ppermute | solution.py:27
  9.0 55.3 %collective-permute-start.4 = (f32[9,36,1,128]{3,1,2,0:T(8,128)}, f32[9,36,1,128]{3,1,2,0:T(8,128)}, u32[]{:S(2)}, u32[]{:S(2)}) collective-permute-start(f32[9,36,1,128]{3,1,2,0:T(8,128)} %copy.69), channel_id=1, source_target_pairs={{0,4},{4,8},{8,12},{12,16},{16,20},{20,24},{24,28},{28,0},{1,5},{5... | collective-permute-start | bytes 497672 | tf_op jit(solution)/shard_map/ppermute | solution.py:26
  9.7 69.7 %collective-permute-start.5 = (f32[9,36,1,128]{3,1,2,0:T(8,128)}, f32[9,36,1,128]{3,1,2,0:T(8,128)}, u32[]{:S(2)}, u32[]{:S(2)}) collective-permute-start(f32[9,36,1,128]{3,1,2,0:T(8,128)} %copy.70), channel_id=1, source_target_pairs={{4,0},{8,4},{12,8},{16,12},{20,16},{24,20},{28,24},{0,28},{5,1},{9... | collective-permute-start | bytes 497672 | tf_op jit(solution)/shard_map/ppermute | solution.py:27
  14.9 13.4 %copy-start.28 = (s32[128]{0:T(128)}, s32[128]{0:T(128)S(1)}, u32[]{:S(2)}) copy-start(s32[128]{0:T(128)S(1)} %fusion.58) | copy-start | bytes 1540
  16.6 14.7 %all-to-all-start.1 = ((bf16[1,8,32]{2,0,1:T(2,128)(2,1)}), bf16[1,8,32]{2,0,1:T(2,128)(2,1)S(1)}, u32[]{:S(2)}, u32[]{:S(2)}) async-start(bf16[1,8,32]{2,0,1:T(2,128)(2,1)} %all_to_all.24), calls=%async_computation.1 | async-start | bytes 8192 | tf_op jit(solution)/shard_map/all_to_all | solution.py:200
  22.9 1.4 %copy-start.13 = (s32[4,128]{1,0:T(4,128)S(1)}, s32[4,128]{1,0:T(4,128)}, u32[]{:S(2)}) copy-start(s32[4,128]{1,0:T(4,128)} %param.12) | copy-start | bytes 6148
  22.9 2.6 %copy-start.11 = (f32[2,4,128]{2,1,0:T(4,128)S(1)}, f32[2,4,128]{2,1,0:T(4,128)}, u32[]{:S(2)}) copy-start(f32[2,4,128]{2,1,0:T(4,128)} %param.13) | copy-start | bytes 12292
  22.9 2.6 %copy-start.22 = (s32[128,2]{0,1:T(2,128)S(1)}, s32[128,2]{0,1:T(2,128)}, u32[]{:S(2)}) copy-start(s32[128,2]{0,1:T(2,128)} %param.14) | copy-start | bytes 3076
  31.2 12.4 %all-to-all-start = ((s32[1,8,32]{2,0,1:T(1,128)}), s32[1,8,32]{2,0,1:T(1,128)S(1)}, u32[]{:S(2)}, u32[]{:S(2)}) async-start(s32[1,8,32]{2,0,1:T(1,128)} %all_to_all.18), calls=%async_computation | async-start | bytes 8192 | tf_op jit(solution)/shard_map/all_to_all | solution.py:199
  44.8 0.6 copy-start.10
  45.4 0.7 copy-start.3
  48.5 2.7 %copy-start.8 = (f32[4,128]{1,0:T(4,128)S(1)}, f32[4,128]{1,0:T(4,128)}, u32[]{:S(2)}) copy-start(f32[4,128]{1,0:T(4,128)} %get-tuple-element.17) | copy-start | bytes 6148
  48.5 11.8 %copy-start.24 = (f32[9]{0:T(128)S(1)}, f32[9]{0:T(128)}, u32[]{:S(2)}) copy-start(f32[9]{0:T(128)} %get-tuple-element.60) | copy-start | bytes 112
  48.6 12.1 %collective-permute-start.2 = (f32[5,36,4,128]{3,1,2,0:T(8,128)S(1)}, f32[5,36,4,128]{3,1,2,0:T(8,128)S(1)}, u32[]{:S(2)}, u32[]{:S(2)}) collective-permute-start(f32[5,36,4,128]{3,1,2,0:T(8,128)S(1)} %get-tuple-element.25), channel_id=1, source_target_pairs={{0,1},{1,2},{2,3},{4,5},{5,6},{6,7},{8,9},{9,10},{10,11},{12,13},{... | collective-permute-start | bytes 1105928 | tf_op jit(solution)/shard_map/ppermute | solution.py:26
  49.9 10.5 %collective-permute-start.3 = (f32[5,36,4,128]{3,1,2,0:T(8,128)S(1)}, f32[5,36,4,128]{3,1,2,0:T(8,128)S(1)}, u32[]{:S(2)}, u32[]{:S(2)}) collective-permute-start(f32[5,36,4,128]{3,1,2,0:T(8,128)S(1)} %get-tuple-element.26), channel_id=1, source_target_pairs={{1,0},{2,1},{3,2},{5,4},{6,5},{7,6},{9,8},{10,9},{11,10},{13,12},{... | collective-permute-start | bytes 1105928 | tf_op jit(solution)/shard_map/ppermute | solution.py:27
  60.7 0.6 copy-start.27
  62.3 0.6 copy-start.26
  63.6 6.5 %collective-permute-start.6 = (f32[9,36,1,128]{3,1,2,0:T(8,128)S(1)}, f32[9,36,1,128]{3,1,2,0:T(8,128)S(1)}, u32[]{:S(2)}, u32[]{:S(2)}) collective-permute-start(f32[9,36,1,128]{3,1,2,0:T(8,128)S(1)} %slice.248), channel_id=1, source_target_pairs={{4,0},{8,4},{12,8},{16,12},{20,16},{24,20},{28,24},{0,28},{5,1},{9... | collective-permute-start | bytes 497672 | tf_op jit(solution)/shard_map/ppermute | solution.py:35
  70.7 0.7 copy-start.4
  70.7 0.7 copy-start.5
  70.7 0.7 copy-start.6
  70.7 0.7 copy-start.7
  70.7 0.7 copy-start.14
  70.7 0.7 copy-start.15
  70.8 0.7 copy-start.16
  70.8 0.7 copy-start.17
  70.8 0.7 copy-start.18
  70.8 0.7 copy-start.19
  70.8 0.7 copy-start.20
  70.8 0.7 copy-start.21
  74.7 6.0 %copy-start.1 = (f32[9,36,4,127]{3,2,1,0:T(4,128)S(1)}, f32[9,36,4,127]{3,2,1,0:T(4,128)}, u32[]{:S(2)}) copy-start(f32[9,36,4,127]{3,2,1,0:T(4,128)} %get-tuple-element.31) | copy-start | bytes 1975108
  74.7 6.0 %copy-start.2 = (f32[9,36,4,127]{3,2,1,0:T(4,128)S(1)}, f32[9,36,4,127]{3,2,1,0:T(4,128)}, u32[]{:S(2)}) copy-start(f32[9,36,4,127]{3,2,1,0:T(4,128)} %get-tuple-element.32) | copy-start | bytes 1975108
  74.7 13.7 %all-to-all-start.2 = ((bf16[324,8,32]{0,2,1:T(8,128)(2,1)}), bf16[324,8,32]{0,2,1:T(8,128)(2,1)S(1)}, u32[]{:S(2)}, u32[]{:S(2)}) async-start(bf16[324,8,32]{0,2,1:T(8,128)(2,1)} %bitcast.15), calls=%async_computation.2 | async-start | bytes 393216 | tf_op jit(solution)/shard_map/all_to_all | solution.py:198
  83.0 5.4 %copy-start.9 = (f32[256]{0:T(256)S(1)}, f32[256]{0:T(256)}, u32[]{:S(2)}) copy-start(f32[256]{0:T(256)} %reshape.370) | copy-start | bytes 3076
  83.0 5.4 %copy-start.25 = (pred[256]{0:T(512)(128)(4,1)S(1)}, pred[256]{0:T(512)(128)(4,1)}, u32[]{:S(2)}) copy-start(pred[256]{0:T(512)(128)(4,1)} %compare_and_fusion.4) | copy-start | bytes 772
where the time goes:
time: 93.7 us; the launch traced here: 93.2 us
  starting transfers between devices  28.1 us (30%)
  other arithmetic  23 us (25%)
  local copies, waits for them, and re-layouts  16.4 us (18%)
  waiting for transfers between devices  14.8 us (16%)
  blocking collectives  9.11 us (10%)
  between operations  1.83 us (2%)
    ppermute x3, starting transfers between devices, extended_2(): after = lax.ppermute(leading, axis, down)  9.12 us
    psum x1, blocking collectives, per_device(): total_energy = lax.psum(partial_value, 'spec')  9.11 us
    unnamed x66, local copies, waits for them, and re-layouts  5.98 us
    all_to_all x1, starting transfers between devices, per_device(): lax.all_to_all(packed_target, 'grid', split_axis=1, concat_axis=1, tiled=...  5.94 us
    all_to_all x1, waiting for transfers between devices, per_device(): lax.all_to_all(packed_target, 'grid', split_axis=1, concat_axis=1, tiled=...  5.76 us
    ppermute x1, waiting for transfers between devices, passed_along(): return lax.ppermute(block, axis, route)  4.88 us
    all_to_all x1, starting transfers between devices, per_device(): lax.all_to_all(packed_spectra, 'grid', split_axis=1, concat_axis=1, tiled...  4.69 us
    ppermute x3, starting transfers between devices, extended_2(): before = lax.ppermute(last, axis, up)  4.34 us
  transfers between devices with their start and end apart: 10, of which 3 were waited for; matrix products, arithmetic and copies ran while one was open for 32% of the time, Pallas kernels for 0%

commit v1 on v0

v1 whole, which is shorter than its diff:
```python
import functools

import jax
import jax.numpy as jnp
import numpy as np
from jax import lax
from jax.experimental import pallas as pl
from jax.experimental.pallas import tpu as pltpu
from jax.sharding import PartitionSpec as P

ratio_step = 1.1
speed_coef = 0.054
wind_coef = 0.05
dissip_coef = 0.2
nonlin_coef = 0.12
nest_speedup = 2.0
reach = 5

VREG = 8
BF16 = jnp.bfloat16
F32 = jnp.float32


class Sizes:
    def __init__(self, mesh, energy, rim_rows):
        self.grid = mesh.shape["grid"]
        self.spec = mesh.shape["spec"]
        self.bands, self.angles, self.cols, self.lat = energy.shape
        self.freqs = self.bands * self.spec
        self.bins = self.bands * self.angles
        self.ring = self.angles * self.cols
        self.rows = self.bins * self.cols
        self.vregs = self.ring // VREG
        self.rim = rim_rows
        self.cap = max(2, (2 * rim_rows + self.grid - 1) // self.grid)
        self.slots = self.grid * self.cap
        self.lanes = (self.bins + 4 + 127) // 128 * 128
        self.msg_rows = (self.bins + 8 + 15) // 16 * 16
        self.edge_rows = reach * self.ring
        self.band_rows = self.edge_rows + 16
        self.half = self.angles // 2
        self.quarter = self.angles // 4


def ratio_table(sz):
    ranks = np.arange(-reach, sz.freqs + reach, dtype=np.float64) - sz.freqs // 2
    return (ratio_step**ranks).astype(np.float32)


def angle_table(sz):
    heading = 2.0 * np.pi * np.arange(sz.angles) / sz.angles
    table = np.zeros((sz.ring + VREG, sz.lat), np.float32)
    table[: sz.ring, 0] = np.repeat(np.cos(heading), sz.cols)
    table[: sz.ring, 1] = np.repeat(np.sin(heading), sz.cols)
    degrees = -60.0 + 120.0 * (np.arange(sz.lat) + 0.5) / sz.lat
    table[sz.ring :] = 1.0 / np.cos(degrees * (np.pi / 180.0))
    return table


def from_west(sz, angle):
    return angle < sz.quarter or angle >= 3 * sz.quarter


def split2(x):
    high = x.astype(BF16).astype(F32)
    return high, x - high


def pack_kernel(sz, energy, nest, cell, dest, weight, east_msg, west_msg, tmp):
    q = sz.quarter
    for msg, col, mine in ((east_msg, sz.cols - 1, True), (west_msg, 0, False)):
        for k in range(sz.bands):
            for part in range(4):
                own = (part in (0, 3)) == mine
                src = energy if own else nest
                angle = part * q if own else ((part + 2) % 4) * q
                row = (k * sz.angles + angle) * sz.cols + col
                tmp[pl.ds(k * sz.angles + part * q, q), :] = src[pl.ds(row, q, stride=sz.cols), :]
        if mine:
            last = cell[0:1, :] - lax.axis_index("grid") * sz.cols == sz.cols - 1
            lat = jnp.where(last, cell[1:2, :], -1).astype(F32)
            ex, ny = weight[0:1, :], weight[1:2, :]
            south, north = split2(ex * (1.0 - ny)), split2(ex * ny)
            info = [dest[...].astype(F32), lat, south[0], south[1], north[0], north[1]]
            for i, line in enumerate(info):
                tmp[pl.ds(sz.bins + i, 1), :] = line
            rest = sz.msg_rows - sz.bins - len(info)
            tmp[pl.ds(sz.bins + len(info), rest), :] = jnp.zeros((rest, sz.lat), F32)
        else:
            rest = sz.msg_rows - sz.bins
            tmp[pl.ds(sz.bins, rest), :] = jnp.zeros((rest, sz.lat), F32)
        msg[...] = tmp[...].astype(BF16)


def spread_halo(sz, from_w, from_e, halo):
    halo[pl.ds(0, sz.msg_rows, stride=sz.cols), :] = from_w[...].astype(F32)
    halo[pl.ds(sz.cols - 1, sz.msg_rows, stride=sz.cols), :] = from_e[...].astype(F32)


def fill_coefficients(sz, table, secant, centre, lon, lat):
    lane = lax.broadcasted_iota(jnp.int32, (VREG, sz.lat), 1)
    sec = table[pl.ds(sz.ring, VREG), :]
    for v in range(sz.vregs):
        rows = table[pl.ds(v * VREG, VREG), :]
        along = jnp.broadcast_to(jnp.abs(rows[:, 0:1]), (VREG, sz.lat))
        across = jnp.broadcast_to(jnp.abs(rows[:, 1:2]), (VREG, sz.lat))
        if secant:
            along = along * sec
        edge = 0 if v * VREG < sz.half * sz.cols else sz.lat - 1
        centre[pl.ds(v * VREG, VREG), :] = along + across
        lon[pl.ds(v * VREG, VREG), :] = along
        lat[pl.ds(v * VREG, VREG), :] = jnp.where(lane == edge, 0.0, across)


def transported(sz, field, halo, k, v, coefficients, speed, shift, keep=None):
    sub = lax.broadcasted_iota(jnp.int32, (VREG, sz.lat), 0)
    base = pl.multiple_of(k * sz.ring, VREG)
    x = field[pl.ds(base + v * VREG, VREG), :]
    edge = halo[pl.ds(base + (v * VREG + shift) % sz.ring, VREG), :]
    first = v * VREG // sz.cols
    per = VREG // sz.cols
    wests = [from_west(sz, first + i) for i in range(per)]
    col = sub % sz.cols
    if all(wests):
        near, at_edge = pltpu.roll(x, 1, 0), col == 0
    elif not any(wests):
        near, at_edge = pltpu.roll(x, VREG - 1, 0), col == sz.cols - 1
    else:
        west = sub < 0
        for i in range(per):
            if wests[i]:
                west = west | ((sub >= i * sz.cols) & (sub < (i + 1) * sz.cols))
        near = jnp.where(west, pltpu.roll(x, 1, 0), pltpu.roll(x, VREG - 1, 0))
        at_edge = jnp.where(west, col, sz.cols - 1 - col) == 0
    if keep is not None:
        edge = edge * jnp.where(col == 0, keep[0], keep[1])
    near = jnp.where(at_edge, edge, near)
    beside = pltpu.roll(x, 1 if v * VREG < sz.half * sz.cols else sz.lat - 1, 1)
    centre, lon, lat = (c[pl.ds(v * VREG, VREG), :] for c in coefficients)
    return x - speed * (centre * x - lon * near - lat * beside)


def advect_kernel(
    sz, table, ratios, energy, from_w, from_e, mask, adv, msg_a, msg_b, part, halo, centre, lon, lat
):
    spec_rank = lax.axis_index("spec")
    spread_halo(sz, from_w, from_e, halo)
    fill_coefficients(sz, table, True, centre, lon, lat)
    sea4 = mask[...].astype(F32)
    sea = jnp.concatenate([sea4] * (VREG // sz.cols), axis=0)

    def band(k, total):
        ratio = ratios[spec_rank * sz.bands + reach + k]
        speed = ratios[sz.freqs + 2 * reach + spec_rank * sz.bands + reach + k]
        base = pl.multiple_of(k * sz.ring, VREG)
        line = jnp.zeros((VREG, sz.lat), F32)
        for v in range(sz.vregs):
            out = sea * transported(sz, energy, halo, k, v, (centre, lon, lat), speed, 0)
            adv[pl.ds(base + v * VREG, VREG), :] = out
            line = line + out
        return total + line * (0.1 * ratio)

    total = lax.fori_loop(0, sz.bands, band, jnp.zeros((VREG, sz.lat), F32))
    mine = total[0 : sz.cols]
    for i in range(1, VREG // sz.cols):
        mine = mine + total[i * sz.cols : (i + 1) * sz.cols]
    part[...] = mine
    even = lax.rem(spec_rank, 2) == 0
    top = (sz.bands - reach) * sz.ring
    first_a = pl.multiple_of(jnp.where(even, top, 0), VREG)
    first_b = pl.multiple_of(jnp.where(even, 0, top), VREG)
    msg_a[pl.ds(0, sz.edge_rows), :] = adv[pl.ds(first_a, sz.edge_rows), :].astype(BF16)
    msg_b[...] = adv[pl.ds(first_b, sz.edge_rows), :].astype(BF16)
    high, rest = split2(mine)
    middle, low = split2(rest)
    pieces = jnp.concatenate([high, middle, low, jnp.zeros_like(mine)], axis=0)
    msg_a[pl.ds(sz.edge_rows, 4 * sz.cols), :] = pieces.astype(BF16)


def slot_matrix(sz, dest):
    device = lax.broadcasted_iota(jnp.int32, (sz.grid, sz.rim), 0).astype(F32)
    hot = jnp.where(device == dest, 1.0, 0.0)
    before = lax.broadcasted_iota(jnp.int32, (sz.rim, sz.rim), 0)
    after = lax.broadcasted_iota(jnp.int32, (sz.rim, sz.rim), 1)
    earlier = jnp.dot(
        hot.astype(BF16), jnp.where(before < after, 1.0, 0.0).astype(BF16), preferred_element_type=F32
    )
    rank = jnp.sum(hot * earlier, axis=0, keepdims=True)
    place = dest * sz.cap + rank
    slot = lax.broadcasted_iota(jnp.int32, (sz.slots, sz.rim), 0).astype(F32)
    return jnp.where(slot == place, 1.0, 0.0).astype(BF16)


def dot_lanes(a, b):
    return lax.dot_general(a, b, (((1,), (1,)), ((), ())), preferred_element_type=F32)


def side_kernel(
    sz, table, ratios, nest, from_w, from_e, cell, dest, target, weight, nest_adv, mix, halo, centre, lon, lat
):
    spec_rank, grid_rank = lax.axis_index("spec"), lax.axis_index("grid")
    quarter = sz.grid // 4
    keep_w = jnp.where((grid_rank != quarter) & (grid_rank != 3 * quarter), 1.0, 0.0).astype(F32)
    keep_e = jnp.where((grid_rank != quarter - 1) & (grid_rank != 3 * quarter - 1), 1.0, 0.0).astype(F32)
    spread_halo(sz, from_w, from_e, halo)
    fill_coefficients(sz, table, False, centre, lon, lat)

    def band(k, carry):
        speed = nest_speedup * ratios[sz.freqs + 2 * reach + spec_rank * sz.bands + reach + k]
        base = pl.multiple_of(k * sz.ring, VREG)
        for v in range(sz.vregs):
            nest_adv[pl.ds(base + v * VREG, VREG), :] = transported(
                sz, nest, halo, k, v, (centre, lon, lat), speed, sz.half * sz.cols, (keep_w, keep_e)
            )
        return carry

    lax.fori_loop(0, sz.bands, band, 0)

    row = lax.broadcasted_iota(jnp.int32, (sz.lat, sz.rim), 0)
    hot = slot_matrix(sz, dest[...].astype(F32))
    col = cell[0:1, :] - grid_rank * sz.cols
    south_row = cell[1:2, :]
    ex, ny = weight[0:1, :], weight[1:2, :]
    for c in range(sz.cols):
        share = jnp.where(col == c, 1.0 - ex, 0.0) + jnp.where(col + 1 == c, ex, 0.0)
        south, north = share * (1.0 - ny), share * ny
        corner = jnp.where(row == south_row, south, 0.0) + jnp.where(row == south_row + 1, north, 0.0)
        mix[:, c * sz.lat : (c + 1) * sz.lat] = dot_lanes(hot, corner.astype(BF16)).astype(BF16)
    info = from_w[pl.ds(sz.bins // 16 * 16, 16), :].astype(F32)
    off = sz.bins % 16
    their_dest, their_row = info[off : off + 1], info[off + 1 : off + 2]
    south = info[off + 2 : off + 3] + info[off + 3 : off + 4]
    north = info[off + 4 : off + 5] + info[off + 5 : off + 6]
    their_hot = slot_matrix(sz, their_dest)
    valid = their_row >= 0.0
    rowf = row.astype(F32)
    corner = jnp.where(valid & (rowf == their_row), south, 0.0) + jnp.where(
        valid & (rowf == their_row + 1.0), north, 0.0
    )
    n = sz.cols * sz.lat
    mix[:, n : n + sz.lat] = dot_lanes(their_hot, corner.astype(BF16)).astype(BF16)
    at = sz.bins % 128
    line = lax.broadcasted_iota(jnp.int32, (128, sz.rim), 0)
    t = target[...]
    t_col = t // sz.lat
    about = jnp.where(line == at, t_col.astype(F32), 0.0)
    about = about + jnp.where(line == at + 1, (t - t_col * sz.lat).astype(F32), 0.0)
    rate, rest = split2(weight[2:3, :])
    about = about + jnp.where(line == at + 2, rate, 0.0) + jnp.where(line == at + 3, rest, 0.0)
    n = n + sz.lat
    mix[:, n : n + 128] = dot_lanes(hot, about.astype(BF16)).astype(BF16)


def source_kernel(
    sz, table, ratios, adv, recv_a, recv_b, pair, other, wind, mix, out, msg, plain, turned, plus, minus, wide
):
    spec_rank = lax.axis_index("spec")
    first = spec_rank * sz.bands
    nv = sz.vregs
    low = lax.broadcasted_iota(jnp.int32, (VREG, sz.lat), 0) < VREG // 2
    turn = VREG // 2

    def put(slot, load):
        vals = [load(v) for v in range(nv)]
        for v in range(nv):
            plain[slot, pl.ds(v * VREG, VREG), :] = vals[v]
            nxt = pltpu.roll(jnp.where(low, vals[(v + 1) % nv], vals[v]), turn, 0)
            turned[slot, pl.ds((v + 2) * VREG, VREG), :] = nxt
            if v >= nv - 2:
                turned[slot, pl.ds((v + 2 - nv) * VREG, VREG), :] = nxt
            if v == 0:
                turned[slot, pl.ds((nv + 2) * VREG, VREG), :] = nxt

    even = lax.rem(spec_rank, 2) == 0
    base_a = jnp.where(even, sz.bands + reach, 0)
    base_b = jnp.where(even, 0, sz.bands + reach)

    def own(k, carry):
        base = pl.multiple_of(k * sz.ring, VREG)
        put(k + reach, lambda v: adv[pl.ds(base + v * VREG, VREG), :])
        return carry

    def halo(k, carry):
        base = pl.multiple_of(k * sz.ring, 16)
        a = recv_a[pl.ds(base, sz.ring), :].astype(F32)
        put(base_a + k, lambda v: a[v * VREG : (v + 1) * VREG])
        b = recv_b[pl.ds(base, sz.ring), :].astype(F32)
        put(base_b + k, lambda v: b[v * VREG : (v + 1) * VREG])
        return carry

    lax.fori_loop(0, sz.bands, own, 0)
    lax.fori_loop(0, reach, halo, 0)

    def strengths(n, carry):
        strength = nonlin_coef * ratios[first + n + 3]
        for v in range(nv):
            c = plain[n + 3, pl.ds(v * VREG, VREG), :]
            sc = strength * c
            for ref, up_row, down_row in ((plus, v + 3, v + 1), (minus, v, v + 2)):
                up = turned[n + 5, pl.ds(up_row * VREG, VREG), :]
                down = turned[n, pl.ds(down_row * VREG, VREG), :]
                delta = sc * (c * (up + down) - 2.0 * (up * down))
                ref[n, pl.ds((v + 1) * VREG, VREG), :] = delta
                if v == nv - 1:
                    ref[n, pl.ds(0, VREG), :] = delta
                if v < 2:
                    ref[n, pl.ds((nv + 1 + v) * VREG, VREG), :] = delta
        return carry

    lax.fori_loop(0, sz.bands + reach, strengths, 0)

    per = VREG // sz.cols
    east = jnp.concatenate([wind[0]] * per, axis=0)
    north = jnp.concatenate([wind[1]] * per, axis=0)
    for v in range(nv):
        rows = table[pl.ds(v * VREG, VREG), :]
        along = rows[:, 0:1] * east + rows[:, 1:2] * north
        wide[pl.ds(v * VREG, VREG), :] = wind_coef * jnp.maximum(along, 0.0)
    total_weight = float(sz.angles * 0.1 * np.sum(ratio_table(sz)[reach:-reach].astype(np.float64)))
    mean4 = (pair[...] + other[...]) * (1.0 / total_weight)
    mean = jnp.concatenate([mean4] * per, axis=0)

    def result(k, carry):
        ratio = ratios[first + reach + k]
        scale = 1.0 / (1.0 + (dissip_coef * ratio * ratio) * mean)
        base = pl.multiple_of(k * sz.ring, VREG)

        def side(v):
            return (
                plus[k, pl.ds(v * VREG, VREG), :]
                + minus[k, pl.ds((v + 3) * VREG, VREG), :]
                + plus[k + 5, pl.ds((v + 2) * VREG, VREG), :]
                + minus[k + 5, pl.ds((v + 1) * VREG, VREG), :]
            )

        before = side(nv - 1)
        for v in range(nv):
            now = side(v)
            moved = pltpu.roll(jnp.where(low, now, before), turn, 0)
            before = now
            here = pl.ds((v + 1) * VREG, VREG)
            transfer = moved - 2.0 * (plus[k + 2, here, :] + minus[k + 2, here, :])
            a = adv[pl.ds(base + v * VREG, VREG), :]
            gain = ratio * wide[pl.ds(v * VREG, VREG), :]
            out[pl.ds(base + v * VREG, VREG), :] = (a + gain * a + transfer) * scale
        return carry

    lax.fori_loop(0, sz.bands, result, 0)

    pad = jnp.zeros((sz.lanes - sz.bins, sz.lat), BF16)
    columns = [
        jnp.concatenate([out[pl.ds(c, sz.bins, stride=sz.cols), :].astype(BF16), pad], axis=0)
        for c in range(sz.cols)
    ]
    n = sz.cols * sz.lat
    spectra = dot_lanes(mix[:, 0:n], jnp.concatenate(columns, axis=1))
    about = mix[:, n + sz.lat : n + sz.lat + 128].astype(F32)
    msg[:, 0 : sz.lanes - 128] = spectra[:, : sz.lanes - 128].astype(BF16)
    msg[:, sz.lanes - 128 : sz.lanes] = (spectra[:, sz.lanes - 128 :] + about).astype(BF16)
    msg[:, sz.lanes :] = dot_lanes(mix[:, n : n + sz.lat], columns[0]).astype(BF16)


def blend_kernel(sz, recv, nest_adv, out):
    east = recv[:, sz.lanes :].astype(F32)
    east = jnp.concatenate([east[sz.cap :], east[: sz.cap]], axis=0)
    own = recv[:, : sz.lanes].astype(F32)
    spectra = (own + east).astype(BF16)
    at = sz.bins - (sz.lanes - 128)
    about = own[:, sz.lanes - 128 :]
    t_col, t_row, rate = about[:, at : at + 1], about[:, at + 1 : at + 2], about[:, at + 2 : at + 3]
    lane = lax.broadcasted_iota(jnp.int32, (sz.slots, sz.lat), 1).astype(F32)
    hit = jnp.where(lane == t_row, rate, 0.0)
    for c in range(sz.cols):
        relax = jnp.where(t_col == float(c), hit, 0.0)
        kept = 1.0 - jnp.sum(relax, axis=0, keepdims=True)
        added = lax.dot_general(
            spectra, relax.astype(BF16), (((0,), (0,)), ((), ())), preferred_element_type=F32
        )
        here = pl.ds(c, sz.bins, stride=sz.cols)
        out[here, :] = nest_adv[here, :] * kept + added[: sz.bins]


def kernel_call(body, out_shape, n_in, smem=(), scratch=(), flops=0, moved=0, name=None):
    specs = [
        pl.BlockSpec(memory_space=pltpu.SMEM if i in smem else pltpu.VMEM) for i in range(n_in)
    ]
    return pl.pallas_call(
        body,
        out_shape=out_shape,
        in_specs=specs,
        out_specs=jax.tree.map(lambda _: pl.BlockSpec(memory_space=pltpu.VMEM), out_shape),
        scratch_shapes=list(scratch),
        compiler_params=pltpu.CompilerParams(vmem_limit_bytes=20 * 2**20),
        cost_estimate=pl.CostEstimate(flops=flops, bytes_accessed=moved, transcendentals=0),
        name=name,
    )


def per_device(
    mesh, energy, nest_energy, ocean_mask, wind_field, rim_cell, rim_dest, rim_target, rim_weight
):
    sz = Sizes(mesh, energy, rim_dest.shape[0])
    shape = jax.ShapeDtypeStruct
    field = shape((sz.rows, sz.lat), F32)
    vmem = pltpu.VMEM
    ratio = ratio_table(sz)
    ratios = jnp.asarray(np.concatenate([ratio, speed_coef / ratio]).astype(np.float32))
    table = jnp.asarray(angle_table(sz))
    energy = energy.reshape(sz.rows, sz.lat)
    nest = nest_energy.reshape(sz.rows, sz.lat)
    cell, dest, weight = rim_cell.T, rim_dest.T, rim_weight.T
    target = rim_target.reshape(1, sz.rim)

    edge = shape((sz.msg_rows, sz.lat), BF16)
    east_msg, west_msg = kernel_call(
        functools.partial(pack_kernel, sz),
        (edge, edge),
        5,
        scratch=[vmem((sz.msg_rows, sz.lat), F32)],
        name="pack",
    )(energy, nest, cell, dest, weight)
    up = [(i, (i + 1) % sz.grid) for i in range(sz.grid)]
    from_w = lax.ppermute(east_msg, "grid", up)
    from_e = lax.ppermute(west_msg, "grid", [(j, i) for i, j in up])

    coefficient = [vmem((sz.ring, sz.lat), F32)] * 3
    halo = vmem((sz.msg_rows * sz.cols, sz.lat), F32)
    adv, msg_a, msg_b, part = kernel_call(
        functools.partial(advect_kernel, sz),
        (
            field,
            shape((sz.band_rows, sz.lat), BF16),
            shape((sz.edge_rows, sz.lat), BF16),
            shape((sz.cols, sz.lat), F32),
        ),
        6,
        smem=(1,),
        scratch=[halo] + coefficient,
        name="advect",
    )(table, ratios, energy, from_w, from_e, ocean_mask)

    recv_a = lax.ppermute(msg_a, "spec", [(i, i ^ 1) for i in range(sz.spec)])
    across = [(i, i + 1) for i in range(1, sz.spec - 1, 2)]
    recv_b = lax.ppermute(msg_b, "spec", across + [(j, i) for i, j in across])
    pieces = recv_a[sz.edge_rows : sz.edge_rows + 3 * sz.cols].astype(F32)
    pair = part + pieces.reshape(3, sz.cols, sz.lat).sum(axis=0)
    other = jnp.zeros_like(pair)
    step = 2
    while step < sz.spec:
        pair = pair + other
        other = lax.ppermute(pair, "spec", [(i, i ^ step) for i in range(sz.spec)])
        step *= 2

    nest_adv, mix = kernel_call(
        functools.partial(side_kernel, sz),
        (field, shape((sz.slots, (sz.cols + 1) * sz.lat + 128), BF16)),
        9,
        smem=(1,),
        scratch=[halo] + coefficient,
        flops=10**9,
        moved=2 * 10**6,
        name="side",
    )(table, ratios, nest, from_w, from_e, cell, dest, target, weight)

    padded = sz.bands + 2 * reach
    global_next, msg = kernel_call(
        functools.partial(source_kernel, sz),
        (field, shape((sz.slots, 2 * sz.lanes), BF16)),
        9,
        smem=(1,),
        scratch=[
            vmem((padded, sz.ring, sz.lat), F32),
            vmem((padded, sz.ring + 3 * VREG, sz.lat), F32),
            vmem((sz.bands + reach, sz.ring + 3 * VREG, sz.lat), F32),
            vmem((sz.bands + reach, sz.ring + 3 * VREG, sz.lat), F32),
            vmem((sz.ring, sz.lat), F32),
        ],
        name="sources",
    )(table, ratios, adv, recv_a, recv_b, pair, other, wind_field, mix)

    recv = lax.all_to_all(msg, "grid", split_axis=0, concat_axis=0, tiled=True)
    nest_next = kernel_call(functools.partial(blend_kernel, sz), field, 2, name="blend")(recv, nest_adv)
    full = (sz.bands, sz.angles, sz.cols, sz.lat)
    return global_next.reshape(full), nest_next.reshape(full)


def solution(mesh):
    in_specs = (
        P("spec", None, "grid", None),
        P("spec", None, "grid", None),
        P("grid", None),
        P(None, "grid", None),
        P("grid", None),
        P("grid", None),
        P("grid"),
        P("grid", None),
    )
    out_specs = (P("spec", None, "grid", None), P("spec", None, "grid", None))
    return jax.shard_map(
        functools.partial(per_device, mesh),
        mesh=mesh,
        in_specs=in_specs,
        out_specs=out_specs,
        check_vma=False,
    )
```

time: 93.7 us -> 43.8 us (0.47)
  other arithmetic: 23 us -> 0.03 us
  starting transfers between devices: 28.1 us -> 9.58 us
  local copies, waits for them, and re-layouts: 16.4 us -> 2.89 us
  waiting for transfers between devices: 14.8 us -> 5.35 us
  blocking collectives: 9.11 us -> 17.1 us
  Pallas kernels: 0 us -> 7.88 us
  between operations: 1.83 us -> 0.72 us
    all_to_all x0 -> x1, blocking collectives: none -> 17.1 us  [per_device(): recv = lax.all_to_all(msg, 'grid', split_axis=0, concat_axis=0, tiled=True)]
    all_to_all x3 -> x0, starting transfers between devices: 14 us -> none  [the longest x1 5.94 us: per_device(): lax.all_to_all(packed_target, 'grid', split_axis=1, concat_axis=1, tiled=...]
    all_to_all x3 -> x0, waiting for transfers between devices: 9.9 us -> none  [the longest x1 5.76 us: per_device(): lax.all_to_all(packed_target, 'grid', split_axis=1, concat_axis=1, tiled=...]
    psum x1 -> x0, blocking collectives: 9.11 us -> none  [per_device(): total_energy = lax.psum(partial_value, 'spec')]
    pallas_call x0 -> x5, Pallas kernels: none -> 7.88 us  [the longest x1 2.77 us: per_device(): kernel_call(functools.partial(source_kernel, sz), (field, shape((sz.slots...]
    mul x7 -> x0, other arithmetic: 5.07 us -> none  [the longest x1 0.94 us: per_device(): nest_padded[:, :, -1:] * upper_keep.astype(jnp.float32)]
    ppermute x7 -> x5, starting transfers between devices: 14.1 us -> 9.58 us  [the longest x1 3.1 us: per_device(): from_e = lax.ppermute(west_msg, 'grid', [(j, i) for i, j in up])]
    scatter-add x1 -> x0, other arithmetic: 3.47 us -> none  [blend(): totals.at[:, targets]]
  transfers between devices with their start and end apart: 10 -> 5, of which waited for: 3 -> 4; matrix products, arithmetic and copies ran while one was open for 32% -> 0% of each run, Pallas kernels for 0% -> 5%
where the time goes in v1:
time: 43.8 us; the launch traced here: 43.5 us
  blocking collectives  17.1 us (39%)
  starting transfers between devices  9.58 us (22%)
  Pallas kernels  7.88 us (18%)
  waiting for transfers between devices  5.35 us (12%)
  local copies, waits for them, and re-layouts  2.89 us (7%)
  between operations  0.72 us (2%)
    all_to_all x1, blocking collectives, per_device(): recv = lax.all_to_all(msg, 'grid', split_axis=0, concat_axis=0, tiled=True)  17.1 us
    ppermute x1, starting transfers between devices, per_device(): from_e = lax.ppermute(west_msg, 'grid', [(j, i) for i, j in up])  3.1 us
    ppermute x1, starting transfers between devices, per_device(): from_w = lax.ppermute(east_msg, 'grid', up)  3.02 us
    unnamed x22, local copies, waits for them, and re-layouts  2.88 us
    pallas_call x1, Pallas kernels, per_device(): kernel_call(functools.partial(source_kernel, sz), (field, shape((sz.slots...  2.77 us
    ppermute x1, starting transfers between devices, per_device(): other = lax.ppermute(pair, 'spec', [(i, i ^ step) for i in range(sz.spec)])  2.71 us
    ppermute x1, waiting for transfers between devices, per_device(): from_w = lax.ppermute(east_msg, 'grid', up)  2.57 us
    pallas_call x1, Pallas kernels, per_device(): kernel_call(functools.partial(side_kernel, sz), (field, shape((sz.slots,...  1.99 us
  transfers between devices with their start and end apart: 5, of which 4 were waited for; matrix products, arithmetic and copies ran while one was open for 0% of the time, Pallas kernels for 5%

profile of v1, /device:TPU:0, one launch (start us, length us, event | category | flops | bytes accessed | tf_op | source)
XLA Modules:
  0.0 43.5 jit_solution(4256083496286366274)
XLA Ops:
  0.6 0.0 copy-start.6
  0.6 0.0 copy-start.8
  0.7 0.0 copy-start.9
  0.7 0.7 %copy-done.6 = f32[128,3]{0,1:T(4,128)S(1)} copy-done((f32[128,3]{0,1:T(4,128)S(1)}, f32[128,3]{0,1:T(4,128)}, u32[]{:S(2)}) %copy-start.6) | copy-done | bytes 1560
  1.3 0.0 copy-done.8
  1.3 0.0 copy-done.9
  1.3 0.0 copy-start
  1.3 1.1 %copy-done = f32[9,36,4,128]{3,2,1,0:T(4,128)S(1)} copy-done((f32[9,36,4,128]{3,2,1,0:T(4,128)S(1)}, f32[9,36,4,128]{3,2,1,0:T(4,128)}, u32[]{:S(2)}) %copy-start) | copy-done | bytes 663576
  2.4 0.0 copy-start.1
  2.4 1.1 %copy-done.1 = f32[9,36,4,128]{3,2,1,0:T(4,128)S(1)} copy-done((f32[9,36,4,128]{3,2,1,0:T(4,128)S(1)}, f32[9,36,4,128]{3,2,1,0:T(4,128)}, u32[]{:S(2)}) %copy-start.1) | copy-done | bytes 663576
  3.5 0.0 copy-start.3
  3.5 0.0 copy-start.5
  3.5 0.0 copy-start.7
  3.5 0.1 pack.1
  3.6 0.0 copy-start.2
  3.6 3.0 %collective-permute-start = (bf16[336,128]{1,0:T(8,128)(2,1)S(1)}, bf16[336,128]{1,0:T(8,128)(2,1)S(1)}, u32[]{:S(2)}, u32[]{:S(2)}) collective-permute-start(bf16[336,128]{1,0:T(8,128)(2,1)S(1)} %get-tuple-element.12), channel_id=1, source_target_pairs={{0,4},{4,8},{8,12},{12,16},{16,20},{20,24},{24,28},{28,0},{1,5},{5... | collective-permute-start | bytes 258056 | tf_op jit(solution)/shard_map/ppermute | solution.py:423
  6.7 3.1 %collective-permute-start.1 = (bf16[336,128]{1,0:T(8,128)(2,1)S(1)}, bf16[336,128]{1,0:T(8,128)(2,1)S(1)}, u32[]{:S(2)}, u32[]{:S(2)}) collective-permute-start(bf16[336,128]{1,0:T(8,128)(2,1)S(1)} %get-tuple-element.13), channel_id=1, source_target_pairs={{4,0},{8,4},{12,8},{16,12},{20,16},{24,20},{28,24},{0,28},{5,1},{9... | collective-permute-start | bytes 258056 | tf_op jit(solution)/shard_map/ppermute | solution.py:424
  9.8 2.6 %collective-permute-done.from_w = bf16[336,128]{1,0:T(8,128)(2,1)S(1)} collective-permute-done((bf16[336,128]{1,0:T(8,128)(2,1)S(1)}, bf16[336,128]{1,0:T(8,128)(2,1)S(1)}, u32[]{:S(2)}, u32[]{:S(2)}) %collective-permute-start) | collective-permute-done | bytes 86048 | tf_op jit(solution)/shard_map/ppermute | solution.py:423
  12.3 0.7 %collective-permute-done.1.from_e = bf16[336,128]{1,0:T(8,128)(2,1)S(1)} collective-permute-done((bf16[336,128]{1,0:T(8,128)(2,1)S(1)}, bf16[336,128]{1,0:T(8,128)(2,1)S(1)}, u32[]{:S(2)}, u32[]{:S(2)}) %collective-permute-start.1) | collective-permute-done | bytes 86048 | tf_op jit(solution)/shard_map/ppermute | solution.py:424
  13.0 0.0 copy-done.3
  13.0 0.0 copy-done.5
  13.0 0.0 copy-done.7
  13.0 1.6 %advect.1 = (f32[1296,128]{1,0:T(8,128)S(1)}, bf16[736,128]{1,0:T(8,128)(2,1)S(1)}, bf16[720,128]{1,0:T(8,128)(2,1)S(1)}, f32[4,128]{1,0:T(4,128)S(1)}) custom-call(f32[152,128]{1,0:T(8,128)S(1)} %copy-done.3, f32[92]{0:T(128)S(1)} %copy-done.7, f32[1296,128]{1,0:T(8,128)S(1)} %bitcast.11, bf16[336,128]{1,0:T(8,128)(2,1)S(1)} %collective-permute-done.from_w, ...), custom_call_target="tpu_custom_call" | custom-call | tf_op jit(solution)/shard_map/advect/pallas_call | solution.py:428
  14.6 0.1 collective-permute-start.2
  14.7 0.7 %collective-permute-start.3 = (bf16[720,128]{1,0:T(8,128)(2,1)S(1)}, bf16[720,128]{1,0:T(8,128)(2,1)S(1)}, u32[]{:S(2)}, u32[]{:S(2)}) collective-permute-start(bf16[720,128]{1,0:T(8,128)(2,1)S(1)} %get-tuple-element.16), channel_id=1, source_target_pairs={{1,2},{2,1},{5,6},{6,5},{9,10},{10,9},{13,14},{14,13},{17,18},{18,... | collective-permute-start | bytes 552968 | tf_op jit(solution)/shard_map/ppermute | solution.py:444
  15.4 0.7 %collective-permute-done.2.recv_a = bf16[736,128]{1,0:T(8,128)(2,1)S(1)} collective-permute-done((bf16[736,128]{1,0:T(8,128)(2,1)S(1)}, bf16[736,128]{1,0:T(8,128)(2,1)S(1)}, u32[]{:S(2)}, u32[]{:S(2)}) %collective-permute-start.2) | collective-permute-done | bytes 188448 | tf_op jit(solution)/shard_map/ppermute | solution.py:442
  16.1 0.0 copy-start.10
  16.1 2.7 %collective-permute-start.4 = (f32[4,128]{1,0:T(4,128)S(1)}, f32[4,128]{1,0:T(4,128)S(1)}, u32[]{:S(2)}, u32[]{:S(2)}) collective-permute-start(f32[4,128]{1,0:T(4,128)S(1)} %add.3.pair), channel_id=1, source_target_pairs={{0,2},{1,3},{2,0},{3,1},{4,6},{5,7},{6,4},{7,5},{8,10},{9,11},{10,... | collective-permute-start | bytes 6152 | tf_op jit(solution)/shard_map/ppermute | solution.py:451
  18.8 0.0 copy-done.2
  18.8 0.0 copy-done.10
  18.9 0.0 copy-start.4
  18.9 2.0 %side.1 = (f32[1296,128]{1,0:T(8,128)S(1)}, bf16[256,768]{1,0:T(8,128)(2,1)S(1)}) custom-call(f32[152,128]{1,0:T(8,128)S(1)} %copy-done.3, f32[92]{0:T(128)S(1)} %copy-done.7, f32[1296,128]{1,0:T(8,128)S(1)} %bitcast.14, bf16[336,128]{1,0:T(8,128)(2,1)S(1)} %collective-permute-done.from_w, bf16[336,128]{1,0:T(8,128)(2,1)S(1)} %collective-permute-done.1.from_e, ...), custom_call_target="tpu_custom_call" | custom-call | flops 1000000000 | bytes 2000000 | tf_op jit(solution)/shard_map/side/pallas_call | solution.py:454
  20.8 0.0 collective-permute-done.3.recv_b
  20.9 1.4 %collective-permute-done.4.other = f32[4,128]{1,0:T(4,128)S(1)} collective-permute-done((f32[4,128]{1,0:T(4,128)S(1)}, f32[4,128]{1,0:T(4,128)S(1)}, u32[]{:S(2)}, u32[]{:S(2)}) %collective-permute-start.4) | collective-permute-done | bytes 2080 | tf_op jit(solution)/shard_map/ppermute | solution.py:451
  22.2 0.0 copy-done.4
  22.2 2.8 %sources.1 = (f32[1296,128]{1,0:T(8,128)}, bf16[256,768]{1,0:T(8,128)(2,1)S(1)}) custom-call(f32[152,128]{1,0:T(8,128)S(1)} %copy-done.3, f32[92]{0:T(128)S(1)} %copy-done.7, f32[1296,128]{1,0:T(8,128)S(1)} %get-tuple-element.14.adv, bf16[736,128]{1,0:T(8,128)(2,1)S(1)} %collective-permute-done.2.recv_a, bf16[720,128]{1,0:T(8,128)(2,1)S(1)} %collective-permute-done.3.recv_b, ...), custom_call_target="tpu_custom_call" | custom-call | tf_op jit(solution)/shard_map/sources/pallas_call | solution.py:466
  25.0 17.1 %all_to_all.11 = bf16[8,32,768]{2,1,0:T(8,128)(2,1)S(1)} all-to-all(bf16[8,32,768]{2,1,0:T(8,128)(2,1)S(1)} %bitcast.15), channel_id=1, replica_groups=mesh['grid'=8,'spec'=4] {'grid'}, dimensions={0} | all-to-all | bytes 786432 | tf_op jit(solution)/shard_map/all_to_all | solution.py:481
  42.1 1.4 %blend.1 = f32[1296,128]{1,0:T(8,128)} custom-call(bf16[256,768]{1,0:T(8,128)(2,1)S(1)} %bitcast.12, f32[1296,128]{1,0:T(8,128)S(1)} %get-tuple-element.21.nest_adv), custom_call_target="tpu_custom_call" | custom-call | tf_op jit(solution)/shard_map/blend/pallas_call | solution.py:482
  (4 shorter events, 0.0 us)
Async XLA Ops:
  0.6 0.7 %copy-start.6 = (f32[128,3]{0,1:T(4,128)S(1)}, f32[128,3]{0,1:T(4,128)}, u32[]{:S(2)}) copy-start(f32[128,3]{0,1:T(4,128)} %param.17) | copy-start | bytes 4612
  0.6 0.7 %copy-start.8 = (s32[128,2]{0,1:T(2,128)S(1)}, s32[128,2]{0,1:T(2,128)}, u32[]{:S(2)}) copy-start(s32[128,2]{0,1:T(2,128)} %param.14) | copy-start | bytes 3076
  0.7 0.7 %copy-start.9 = (s32[128,1]{0,1:T(1,128)S(1)}, s32[128,1]{0,1:T(1,128)}, u32[]{:S(2)}) copy-start(s32[128,1]{0,1:T(1,128)} %param.15) | copy-start | bytes 1540
  1.3 1.1 %copy-start = (f32[9,36,4,128]{3,2,1,0:T(4,128)S(1)}, f32[9,36,4,128]{3,2,1,0:T(4,128)}, u32[]{:S(2)}) copy-start(f32[9,36,4,128]{3,2,1,0:T(4,128)} %param.10) | copy-start | bytes 1990660
  2.4 1.1 %copy-start.1 = (f32[9,36,4,128]{3,2,1,0:T(4,128)S(1)}, f32[9,36,4,128]{3,2,1,0:T(4,128)}, u32[]{:S(2)}) copy-start(f32[9,36,4,128]{3,2,1,0:T(4,128)} %param.11) | copy-start | bytes 1990660
  3.5 9.5 %copy-start.3 = (f32[152,128]{1,0:T(8,128)S(1)}, f32[152,128]{1,0:T(8,128)}, u32[]{:S(2)}) copy-start(f32[152,128]{1,0:T(8,128)} %constant.7.clone.table) | copy-start | bytes 233476
  3.5 9.5 %copy-start.5 = (s32[4,128]{1,0:T(4,128)S(1)}, s32[4,128]{1,0:T(4,128)}, u32[]{:S(2)}) copy-start(s32[4,128]{1,0:T(4,128)} %mask.1) | copy-start | bytes 6148
  3.5 9.5 %copy-start.7 = (f32[92]{0:T(128)S(1)}, f32[92]{0:T(128)}, u32[]{:S(2)}) copy-start(f32[92]{0:T(128)} %constant.6.clone.ratios) | copy-start | bytes 1108
  3.6 15.2 %copy-start.2 = (f32[9,36,4,128]{3,2,1,0:T(4,128)S(1)}, f32[9,36,4,128]{3,2,1,0:T(4,128)}, u32[]{:S(2)}) copy-start(f32[9,36,4,128]{3,2,1,0:T(4,128)} %param.11) | copy-start | bytes 1990660
  3.6 8.7 %collective-permute-start = (bf16[336,128]{1,0:T(8,128)(2,1)S(1)}, bf16[336,128]{1,0:T(8,128)(2,1)S(1)}, u32[]{:S(2)}, u32[]{:S(2)}) collective-permute-start(bf16[336,128]{1,0:T(8,128)(2,1)S(1)} %get-tuple-element.12), channel_id=1, source_target_pairs={{0,4},{4,8},{8,12},{12,16},{16,20},{20,24},{24,28},{28,0},{1,5},{5... | collective-permute-start | bytes 258056 | tf_op jit(solution)/shard_map/ppermute | solution.py:423
  6.7 6.3 %collective-permute-start.1 = (bf16[336,128]{1,0:T(8,128)(2,1)S(1)}, bf16[336,128]{1,0:T(8,128)(2,1)S(1)}, u32[]{:S(2)}, u32[]{:S(2)}) collective-permute-start(bf16[336,128]{1,0:T(8,128)(2,1)S(1)} %get-tuple-element.13), channel_id=1, source_target_pairs={{4,0},{8,4},{12,8},{16,12},{20,16},{24,20},{28,24},{0,28},{5,1},{9... | collective-permute-start | bytes 258056 | tf_op jit(solution)/shard_map/ppermute | solution.py:424
  14.6 1.5 %collective-permute-start.2 = (bf16[736,128]{1,0:T(8,128)(2,1)S(1)}, bf16[736,128]{1,0:T(8,128)(2,1)S(1)}, u32[]{:S(2)}, u32[]{:S(2)}) collective-permute-start(bf16[736,128]{1,0:T(8,128)(2,1)S(1)} %get-tuple-element.15), channel_id=1, source_target_pairs={{0,1},{1,0},{2,3},{3,2},{4,5},{5,4},{6,7},{7,6},{8,9},{9,8},{10,11... | collective-permute-start | bytes 565256 | tf_op jit(solution)/shard_map/ppermute | solution.py:442
  14.7 6.2 %collective-permute-start.3 = (bf16[720,128]{1,0:T(8,128)(2,1)S(1)}, bf16[720,128]{1,0:T(8,128)(2,1)S(1)}, u32[]{:S(2)}, u32[]{:S(2)}) collective-permute-start(bf16[720,128]{1,0:T(8,128)(2,1)S(1)} %get-tuple-element.16), channel_id=1, source_target_pairs={{1,2},{2,1},{5,6},{6,5},{9,10},{10,9},{13,14},{14,13},{17,18},{18,... | collective-permute-start | bytes 552968 | tf_op jit(solution)/shard_map/ppermute | solution.py:444
  16.1 2.7 %copy-start.10 = (s32[128]{0:T(128)S(1)}, s32[128]{0:T(128)}, u32[]{:S(2)}) copy-start(s32[128]{0:T(128)} %param.16) | copy-start | bytes 1540
  16.1 6.1 %collective-permute-start.4 = (f32[4,128]{1,0:T(4,128)S(1)}, f32[4,128]{1,0:T(4,128)S(1)}, u32[]{:S(2)}, u32[]{:S(2)}) collective-permute-start(f32[4,128]{1,0:T(4,128)S(1)} %add.3.pair), channel_id=1, source_target_pairs={{0,2},{1,3},{2,0},{3,1},{4,6},{5,7},{6,4},{7,5},{8,10},{9,11},{10,... | collective-permute-start | bytes 6152 | tf_op jit(solution)/shard_map/ppermute | solution.py:451
  18.9 3.4 %copy-start.4 = (f32[2,4,128]{2,1,0:T(4,128)S(1)}, f32[2,4,128]{2,1,0:T(4,128)}, u32[]{:S(2)}) copy-start(f32[2,4,128]{2,1,0:T(4,128)} %wind.1) | copy-start | bytes 12292

commit v2 on v1

v2 whole, which is shorter than its diff:
```python
import functools

import jax
import jax.numpy as jnp
import numpy as np
from jax import lax
from jax.experimental import pallas as pl
from jax.experimental.pallas import tpu as pltpu
from jax.sharding import PartitionSpec as P

ratio_step = 1.1
speed_coef = 0.054
wind_coef = 0.05
dissip_coef = 0.2
nonlin_coef = 0.12
nest_speedup = 2.0
reach = 5

VREG = 8
BF16 = jnp.bfloat16
F32 = jnp.float32


class Sizes:
    def __init__(self, mesh, energy, rim_rows):
        self.grid = mesh.shape["grid"]
        self.spec = mesh.shape["spec"]
        self.bands, self.angles, self.cols, self.lat = energy.shape
        self.freqs = self.bands * self.spec
        self.bins = self.bands * self.angles
        self.ring = self.angles * self.cols
        self.rows = self.bins * self.cols
        self.vregs = self.ring // VREG
        self.rim = rim_rows
        self.cap = max(2, (2 * rim_rows + self.grid - 1) // self.grid)
        self.slots = self.grid * self.cap
        self.lanes = (self.bins + 3 + 127) // 128 * 128
        self.half = self.angles // 2
        self.quarter = self.angles // 4
        self.side = (self.angles + VREG - 1) // VREG * VREG
        self.frame = self.side + 2 * VREG
        self.thin = self.bands * self.half
        self.thin_rows = (2 * self.thin + 15) // 16 * 16
        self.thick = (self.angles + self.half + VREG - 1) // VREG * VREG
        self.info = self.bands * self.thick
        self.thick_nest = (self.info + 7 + VREG - 1) // VREG * VREG
        self.thick_rows = (self.thick_nest + self.thin + 15) // 16 * 16
        self.edge_rows = reach * self.ring
        self.rim_band = (2 * self.half + VREG - 1) // VREG * VREG
        self.far_band = self.rim_band + self.side
        self.sum_row = reach * self.far_band
        self.fix_rows = (self.sum_row + 3 * VREG + 15) // 16 * 16


def band_ratio(sz, band, inverse=False):
    rank = lax.axis_index("spec")
    ratio = F32(0.0)
    for s in range(sz.spec):
        power = ratio_step ** (s * sz.bands + band - sz.freqs // 2)
        ratio = jnp.where(rank == s, F32(1.0 / power if inverse else power), ratio)
    return ratio


def over_bands(count, ratio, body, inverse=False):
    step = F32(1.0 / ratio_step if inverse else ratio_step)

    def turn(i, r):
        body(i, r)
        return r * step

    lax.fori_loop(0, count, turn, ratio)


def angle_table(sz):
    heading = 2.0 * np.pi * np.arange(sz.angles) / sz.angles
    table = np.zeros((sz.ring + VREG + sz.side, sz.lat), np.float32)
    table[sz.ring + VREG :][: sz.angles, 0] = np.cos(heading)
    table[sz.ring + VREG :][: sz.angles, 1] = np.sin(heading)
    table[: sz.ring, 0] = np.repeat(np.cos(heading), sz.cols)
    table[: sz.ring, 1] = np.repeat(np.sin(heading), sz.cols)
    degrees = -60.0 + 120.0 * (np.arange(sz.lat) + 0.5) / sz.lat
    table[sz.ring : sz.ring + VREG] = 1.0 / np.cos(degrees * (np.pi / 180.0))
    return table


def from_west(sz, angle):
    return angle < sz.quarter or angle >= 3 * sz.quarter


def split3(x):
    high = x.astype(BF16).astype(F32)
    middle = (x - high).astype(BF16).astype(F32)
    return [high, middle, x - high - middle]


def upwind(sz, v):
    sub = lax.broadcasted_iota(jnp.int32, (VREG, sz.lat), 0)
    first, per = v * VREG // sz.cols, VREG // sz.cols
    wests = [from_west(sz, first + i) for i in range(per)]
    west = sub < 0
    for i in range(per):
        if wests[i]:
            west = west | ((sub >= i * sz.cols) & (sub < (i + 1) * sz.cols))
    return wests, west, sub % sz.cols


def west_half(sz):
    return ((3 * sz.quarter, sz.angles - 3 * sz.quarter), (0, sz.quarter))


def fetch(pairs, sems):
    copies = [pltpu.make_async_copy(a, b, sems.at[i]) for i, (a, b) in enumerate(pairs)]
    for c in copies:
        c.start()
    return copies


def far_band(sz):
    return jnp.where(lax.rem(lax.axis_index("spec"), 2) == 0, 0, sz.bands - reach)


def pack_kernel(
    sz, table, energy, nest, mask, wind,
    thin, thick, moves, nest_moves, s_moves, gain, sea,
    table_v, field, nest_field, mask_v, wind_v, tmp_thin, tmp_thick, sems,
):
    pairs = [(table, table_v), (mask, mask_v), (wind, wind_v)]
    for source, target in ((energy, field), (nest, nest_field)):
        for k in range(sz.bands):
            band = pl.ds(k * sz.ring, sz.ring)
            pairs.append((source.at[band], target.at[band]))
    copies = [pltpu.make_async_copy(a, b, sems.at[i]) for i, (a, b) in enumerate(pairs)]
    for copy in copies:
        copy.start()
    rest = sz.thin_rows - 2 * sz.thin
    if rest:
        tmp_thin[pl.ds(2 * sz.thin, rest), :] = jnp.zeros((rest, sz.lat), F32)
    tmp_thick[...] = jnp.zeros_like(tmp_thick)
    for copy in copies[:3]:
        copy.wait()
    info = [mask_v[0:1, :].astype(F32)] + split3(wind_v[0, 0:1, :]) + split3(wind_v[1, 0:1, :])
    for i, line in enumerate(info):
        tmp_thick[pl.ds(sz.info + i, 1), :] = line
    per = VREG // sz.cols
    sea[...] = jnp.concatenate([mask_v[...].astype(F32)] * per, axis=0)
    east_wind = jnp.concatenate([wind_v[0]] * per, axis=0)
    north_wind = jnp.concatenate([wind_v[1]] * per, axis=0)
    fill_moves(sz, 0, table_v, sz.cols, (moves, nest_moves))
    fill_moves(sz, sz.ring + VREG, table_v, 1, (s_moves, None))
    for v in range(sz.vregs):
        rows = table_v[pl.ds(v * VREG, VREG), :]
        along = rows[:, 0:1] * east_wind + rows[:, 1:2] * north_wind
        gain[pl.ds(v * VREG, VREG), :] = wind_coef * jnp.maximum(along, 0.0)
    for v in range(sz.side // VREG):
        rows = table_v[pl.ds(sz.ring + VREG + v * VREG, VREG), :]
        for i in range(2):
            s_moves[3 + i, pl.ds(v * VREG, VREG), :] = jnp.broadcast_to(rows[:, i : i + 1], (VREG, sz.lat))

    def west(source, row, at):
        for first, count in west_half(sz):
            start = row + first * sz.cols + sz.cols - 1
            tmp_thin[pl.ds(at, count), :] = source[pl.ds(start, count, stride=sz.cols), :]
            at += count

    def east(source, row, at):
        start = row + sz.quarter * sz.cols
        tmp_thick[pl.ds(at, sz.half), :] = source[pl.ds(start, sz.half, stride=sz.cols), :]

    for k in range(sz.bands):
        copies[k + 3].wait()
        row = k * sz.ring
        west(field, row, k * sz.half)
        at = k * sz.thick
        tmp_thick[pl.ds(at, sz.angles), :] = field[pl.ds(row, sz.angles, stride=sz.cols), :]
        east(field, row + 1, at + sz.angles)
    for k in range(sz.bands):
        copies[k + 3 + sz.bands].wait()
        row = k * sz.ring
        west(nest_field, row, sz.thin + k * sz.half)
        east(nest_field, row, sz.thick_nest + k * sz.half)
    thin[...] = tmp_thin[...].astype(BF16)
    thick[...] = tmp_thick[...].astype(BF16)


def raw_kernel(sz, energy, raw_a, raw_b):
    for raw, first in ((raw_a, sz.bands - reach - far_band(sz)), (raw_b, far_band(sz))):
        raw[...] = energy[pl.ds(pl.multiple_of(first * sz.ring, VREG), sz.edge_rows), :].astype(BF16)


def spread_halo(sz, wide_w, first_w, wide_e, stride_e, first_e, halo):
    for k in range(sz.bands):
        at = first_w + k * sz.half
        for first, count in west_half(sz):
            start = k * sz.ring + first * sz.cols
            halo[pl.ds(start, count, stride=sz.cols), :] = wide_w[pl.ds(at, count), :]
            at += count
        start = k * sz.ring + (sz.quarter + 1) * sz.cols - 1
        halo[pl.ds(start, sz.half, stride=sz.cols), :] = wide_e[pl.ds(k * stride_e + first_e, sz.half), :]


def fill_moves(sz, rows, table, cols, targets):
    lane = lax.broadcasted_iota(jnp.int32, (VREG, sz.lat), 1)
    sub = lax.broadcasted_iota(jnp.int32, (VREG, sz.lat), 0)
    sec = table[pl.ds(sz.ring, VREG), :]
    for v in range(targets[0].shape[1] // VREG):
        line = table[pl.ds(rows + v * VREG, VREG), :]
        along = jnp.broadcast_to(jnp.abs(line[:, 0:1]), (VREG, sz.lat))
        across = jnp.broadcast_to(jnp.abs(line[:, 1:2]), (VREG, sz.lat))
        edge = lane == jnp.where(sub < sz.half * cols - v * VREG, 0, sz.lat - 1)
        here = pl.ds(v * VREG, VREG)
        for target, by in zip(targets, (along * sec, along)):
            if target is not None:
                target[0, here, :] = by + across
                target[1, here, :] = by
                target[2, here, :] = jnp.where(edge, 0.0, across)


def beside(sz, x, turn):
    if turn >= VREG:
        return pltpu.roll(x, 1, 1)
    if turn <= 0:
        return pltpu.roll(x, sz.lat - 1, 1)
    sub = lax.broadcasted_iota(jnp.int32, (VREG, sz.lat), 0)
    return jnp.where(sub < turn, pltpu.roll(x, 1, 1), pltpu.roll(x, sz.lat - 1, 1))


def transported(sz, field, halo, base, v, moves, speed):
    here = pl.ds(v * VREG, VREG)
    x = field[pl.ds(base + v * VREG, VREG), :]
    wests, west, col = upwind(sz, v)
    if all(wests):
        near, at_edge = pltpu.roll(x, 1, 0), col == 0
    elif not any(wests):
        near, at_edge = pltpu.roll(x, VREG - 1, 0), col == sz.cols - 1
    else:
        near = jnp.where(west, pltpu.roll(x, 1, 0), pltpu.roll(x, VREG - 1, 0))
        at_edge = jnp.where(west, col, sz.cols - 1 - col) == 0
    edge = 0.0 if halo is None else halo[pl.ds(base + v * VREG, VREG), :]
    near = jnp.where(at_edge, edge, near)
    south = sz.half * sz.cols - v * VREG
    return x - speed * (moves[0, here, :] * x - moves[1, here, :] * near - moves[2, here, :] * beside(sz, x, south))


def advect_kernel(
    sz, energy, from_w, from_e, moves, s_moves, sea, adv, side, msg_a, msg_b, part,
    wide_w, wide_e, halo, s_near, totals, fix,
):
    wide_w[...] = from_w[...].astype(F32)
    wide_e[...] = from_e[...].astype(F32)
    spread_halo(sz, wide_w, 0, wide_e, sz.thick, sz.quarter, halo)
    for k in range(sz.bands):
        for first, count in west_half(sz):
            start = k * sz.ring + first * sz.cols + sz.cols - 1
            s_near[pl.ds(k * sz.side + first, count), :] = energy[pl.ds(start, count, stride=sz.cols), :]
        there = pl.ds(k * sz.thick + sz.angles, sz.half)
        s_near[pl.ds(k * sz.side + sz.quarter, sz.half), :] = wide_e[there, :]
        if sz.side > sz.angles:
            rest = sz.side - sz.angles
            s_near[pl.ds(k * sz.side + sz.angles, rest), :] = jnp.zeros((rest, sz.lat), F32)
    s_sea = wide_e[pl.ds(sz.info, 1), :]
    sub = lax.broadcasted_iota(jnp.int32, (VREG, sz.lat), 0)
    totals[...] = jnp.zeros_like(totals)

    def band(k, inverse):
        speed = speed_coef * inverse
        base = pl.multiple_of(k * sz.ring, VREG)
        line = jnp.zeros((VREG, sz.lat), F32)
        for v in range(sz.vregs):
            out = sea[...] * transported(sz, energy, halo, base, v, moves, speed)
            adv[pl.ds(base + v * VREG, VREG), :] = out
            line = line + out
        s_line = jnp.zeros((VREG, sz.lat), F32)
        s_base = pl.multiple_of(k * sz.side, VREG)
        from_base = pl.multiple_of(k * sz.thick, VREG)
        for v in range(sz.side // VREG):
            here = pl.ds(v * VREG, VREG)
            x = wide_e[pl.ds(from_base + v * VREG, VREG), :]
            near = s_near[pl.ds(s_base + v * VREG, VREG), :]
            move = s_moves[0, here, :] * x - s_moves[1, here, :] * near
            move = move - s_moves[2, here, :] * beside(sz, x, sz.half - v * VREG)
            out = s_sea * (x - speed * move)
            side[pl.ds(s_base + v * VREG, VREG), :] = out
            s_line = s_line + jnp.where(sub < sz.angles - v * VREG, out, 0.0)
        totals[0] = totals[0] * F32(1.0 / ratio_step) + line
        totals[1] = totals[1] * F32(1.0 / ratio_step) + s_line

    over_bands(sz.bands, band_ratio(sz, 0, True), band, True)
    weight = 0.1 * band_ratio(sz, sz.bands - 1)
    total, s_total = totals[0] * weight, totals[1] * weight
    sums = total[0 : sz.cols]
    for i in range(1, VREG // sz.cols):
        sums = sums + total[i * sz.cols : (i + 1) * sz.cols]
    s_sum = jnp.sum(s_total, axis=0, keepdims=True)
    sums = jnp.concatenate([sums, s_sum, jnp.zeros((VREG - sz.cols - 1, sz.lat), F32)], axis=0)
    part[...] = sums
    fix[...] = jnp.zeros_like(fix)
    fix[pl.ds(sz.sum_row, 3 * VREG), :] = jnp.concatenate(split3(sums), axis=0)
    for msg, start in ((msg_a, sz.bands - reach - far_band(sz)), (msg_b, far_band(sz))):
        for k in range(reach):
            band_row = pl.multiple_of((start + k) * sz.ring, VREG)
            at = k * sz.far_band
            for first, count in west_half(sz):
                fix[pl.ds(at, count), :] = adv[pl.ds(band_row + first * sz.cols, count, stride=sz.cols), :]
                at += count
            last = band_row + (sz.quarter + 1) * sz.cols - 1
            fix[pl.ds(at, sz.half), :] = adv[pl.ds(last, sz.half, stride=sz.cols), :]
            s_row = pl.multiple_of((start + k) * sz.side, VREG)
            fix[pl.ds(k * sz.far_band + sz.rim_band, sz.side), :] = side[pl.ds(s_row, sz.side), :]
        msg[...] = fix[...].astype(BF16) if msg is msg_a else jnp.concatenate([fix[...], fix[0:16, :]], axis=0).astype(BF16)


def nest_kernel(sz, nest, moves, out):
    def band(k, inverse):
        base = pl.multiple_of(k * sz.ring, VREG)
        for v in range(sz.vregs):
            moved = transported(sz, nest, None, base, v, moves, nest_speedup * speed_coef * inverse)
            out[pl.ds(base + v * VREG, VREG), :] = moved

    over_bands(sz.bands, band_ratio(sz, 0, True), band, True)


def nest_edge_kernel(sz, inner, from_w, from_e, moves, out, wide_w, wide_e):
    grid_rank = lax.axis_index("grid")
    quarter = sz.grid // 4
    keep_w = jnp.where((grid_rank != quarter) & (grid_rank != 3 * quarter), 1.0, 0.0).astype(F32)
    keep_e = jnp.where((grid_rank != quarter - 1) & (grid_rank != 3 * quarter - 1), 1.0, 0.0).astype(F32)
    wide_w[...] = from_w[...].astype(F32)
    wide_e[...] = from_e[...].astype(F32)
    for k in range(sz.bands):
        speed = nest_speedup * speed_coef * band_ratio(sz, k, True)

        def add(first, count, col, wide, at, keep):
            rows = pl.ds(k * sz.ring + first * sz.cols + col, count, stride=sz.cols)
            by = moves[1, pl.ds(first * sz.cols, count, stride=sz.cols), :] * (speed * keep)
            out[rows, :] = out[rows, :] + by * wide[pl.ds(at, count), :]

        at = sz.thin + k * sz.half
        for first, count in west_half(sz):
            add(first, count, 0, wide_w, at, keep_w)
            at += count
        add(sz.quarter, sz.half, sz.cols - 1, wide_e, sz.thick_nest + k * sz.half, keep_e)


def dot_lanes(a, b):
    return lax.dot_general(a, b, (((1,), (1,)), ((), ())), preferred_element_type=F32)


def rim_kernel(sz, cell, dest, target, weight, mix):
    device = lax.broadcasted_iota(jnp.int32, (sz.grid, sz.rim), 0)
    hot = jnp.where(device == dest[...], 1.0, 0.0)
    before = lax.broadcasted_iota(jnp.int32, (sz.rim, sz.rim), 0)
    after = lax.broadcasted_iota(jnp.int32, (sz.rim, sz.rim), 1)
    earlier = jnp.dot(
        hot.astype(BF16), jnp.where(before < after, 1.0, 0.0).astype(BF16), preferred_element_type=F32
    )
    rank = jnp.sum(hot * earlier, axis=0, keepdims=True)
    place = dest[...] * sz.cap + rank.astype(jnp.int32)
    slot = lax.broadcasted_iota(jnp.int32, (sz.slots, sz.rim), 0)
    takes = jnp.where(slot == place, 1.0, 0.0).astype(BF16)
    row = lax.broadcasted_iota(jnp.int32, (sz.lat, sz.rim), 0)
    col = cell[0:1, :] - lax.axis_index("grid") * sz.cols
    south_row = cell[1:2, :]
    ex, ny = weight[0:1, :], weight[1:2, :]
    for c in range(sz.cols + 1):
        share = jnp.where(col == c, 1.0 - ex, 0.0) + jnp.where(col + 1 == c, ex, 0.0)
        south, north = share * (1.0 - ny), share * ny
        corner = jnp.where(row == south_row, south, 0.0) + jnp.where(row == south_row + 1, north, 0.0)
        mix[:, c * sz.lat : (c + 1) * sz.lat] = dot_lanes(takes, corner.astype(BF16)).astype(BF16)
    at = sz.bins - (sz.lanes - 128)
    line = lax.broadcasted_iota(jnp.int32, (128, sz.rim), 0)
    t = target[...]
    t_col = t // sz.lat
    about = jnp.where(line == at, t_col.astype(F32), 0.0)
    about = about + jnp.where(line == at + 1, (t - t_col * sz.lat).astype(F32), 0.0)
    about = about + jnp.where(line == at + 2, weight[2:3, :], 0.0)
    n = (sz.cols + 1) * sz.lat
    mix[:, n : n + 128] = dot_lanes(takes, about.astype(BF16)).astype(BF16)


def low_rows(sz):
    return lax.broadcasted_iota(jnp.int32, (VREG, sz.lat), 0) < VREG // 2


def put(sz, plain, turned, slot, vals):
    nv, low = sz.vregs, low_rows(sz)
    for v in range(nv):
        if plain is not None:
            plain[slot, pl.ds(v * VREG, VREG), :] = vals[v]
        nxt = pltpu.roll(jnp.where(low, vals[(v + 1) % nv], vals[v]), VREG // 2, 0)
        turned[slot, pl.ds((v + 2) * VREG, VREG), :] = nxt
        if v >= nv - 2:
            turned[slot, pl.ds((v + 2 - nv) * VREG, VREG), :] = nxt
        if v == 0:
            turned[slot, pl.ds((nv + 2) * VREG, VREG), :] = nxt


def close(sz, ref, slot):
    ref[slot, pl.ds(VREG - 3, 3), :] = ref[slot, pl.ds(VREG + sz.angles - 3, 3), :]
    ref[slot, pl.ds(VREG + sz.angles, 3), :] = ref[slot, pl.ds(VREG, 3), :]


def s_put(sz, s_plain, slot, load):
    for v in range(sz.side // VREG):
        s_plain[slot, pl.ds((v + 1) * VREG, VREG), :] = load(v)
    close(sz, s_plain, slot)


def exchange(sc, c, up, down):
    return sc * (c * (up + down) - 2.0 * (up * down))


def strengths(sz, ratio, n, plain, turned, plus, minus, s_plain, s_plus, s_minus):
    nv = sz.vregs
    strength = nonlin_coef * ratio
    for v in range(nv):
        c = plain[n + 3, pl.ds(v * VREG, VREG), :]
        sc = strength * c
        for ref, up_row, down_row in ((plus, v + 3, v + 1), (minus, v, v + 2)):
            up = turned[n + 5, pl.ds(up_row * VREG, VREG), :]
            down = turned[n, pl.ds(down_row * VREG, VREG), :]
            delta = exchange(sc, c, up, down)
            ref[n, pl.ds((v + 1) * VREG, VREG), :] = delta
            if v == nv - 1:
                ref[n, pl.ds(0, VREG), :] = delta
            if v < 2:
                ref[n, pl.ds((nv + 1 + v) * VREG, VREG), :] = delta
    for v in range(sz.side // VREG):
        row = (v + 1) * VREG
        c = s_plain[n + 3, pl.ds(row, VREG), :]
        sc = strength * c
        for ref, s in ((s_plus, 1), (s_minus, -1)):
            up = s_plain[n + 5, pl.ds(row + 3 * s, VREG), :]
            down = s_plain[n, pl.ds(row - s, VREG), :]
            ref[n, pl.ds(row, VREG), :] = exchange(sc, c, up, down)
    close(sz, s_plus, n)
    close(sz, s_minus, n)


def is_even():
    return lax.rem(lax.axis_index("spec"), 2) == 0


def complete(sz, slot, fix, k, plain, turned, s_plain, real=None):
    at = k * sz.far_band
    for start, count in west_half(sz):
        plain[slot, pl.ds(start * sz.cols, count, stride=sz.cols), :] = fix[pl.ds(at, count), :]
        at += count
    last = (sz.quarter + 1) * sz.cols - 1
    plain[slot, pl.ds(last, sz.half, stride=sz.cols), :] = fix[pl.ds(at, sz.half), :]
    at = k * sz.far_band + sz.rim_band
    s_put(sz, s_plain, slot, lambda v: fix[pl.ds(at + v * VREG, VREG), :])


def turn_halo(sz, base, plain, turned, real=None):
    def halo(k, carry):
        vals = [plain[base + k, pl.ds(v * VREG, VREG), :] for v in range(sz.vregs)]
        put(sz, None if real is None else plain, turned, base + k, vals if real is None else [x * real for x in vals])
        return carry

    lax.fori_loop(0, reach, halo, 0)


def inner_kernel(
    sz, adv, side, recv_a, raw_a, raw_b, moves, sea, plain, turned, plus, minus, s_plain, s_plus, s_minus, wide, fix
):
    base_a = jnp.where(is_even(), sz.bands + reach, 0)
    base_b = sz.bands + reach - base_a
    below, above = band_ratio(sz, -reach, True), band_ratio(sz, sz.bands, True)

    def own(k, carry):
        base = pl.multiple_of(k * sz.ring, VREG)
        put(sz, plain, turned, k + reach, [adv[pl.ds(base + v * VREG, VREG), :] for v in range(sz.vregs)])
        s_base = pl.multiple_of(k * sz.side, VREG)
        s_put(sz, s_plain, k + reach, lambda v: side[pl.ds(s_base + v * VREG, VREG), :])
        return carry

    lax.fori_loop(0, sz.bands, own, 0)

    for raw, first, inverse in (
        (raw_a, base_a, jnp.where(is_even(), above, below)),
        (raw_b, base_b, jnp.where(is_even(), below, above)),
    ):
        wide[...] = raw[...].astype(F32)

        def transport(k, r, first=first):
            base = pl.multiple_of(k * sz.ring, VREG)
            for v in range(sz.vregs):
                moved = transported(sz, wide, None, base, v, moves, speed_coef * r)
                plain[first + k, pl.ds(v * VREG, VREG), :] = sea[...] * moved

        over_bands(reach, inverse, transport, True)

    fix[...] = recv_a[...].astype(F32)
    for k in range(reach):
        complete(sz, base_a + k, fix, k, plain, turned, s_plain)
    turn_halo(sz, base_a, plain, turned)

    arrays = (plain, turned, plus, minus, s_plain, s_plus, s_minus)
    start = jnp.where(is_even(), reach, 0)
    ratio = jnp.where(is_even(), band_ratio(sz, 3), band_ratio(sz, 3 - reach))
    over_bands(sz.bands, ratio, lambda i, r: strengths(sz, r, start + i, *arrays))


def source_kernel(
    sz, adv, side, recv_b, pair, other, gain, s_moves, from_e, mix,
    plain_in, turned_in, plus_in, minus_in, s_plain_in, s_plus_in, s_minus_in,
    out, msg, plain, turned, plus, minus, s_plain, s_plus, s_minus, s_out, fix,
):
    spec_rank = lax.axis_index("spec")
    nv, ns = sz.vregs, sz.side // VREG
    low, turn = low_rows(sz), VREG // 2
    base_b = jnp.where(is_even(), 0, sz.bands + reach)
    real_b = jnp.where((spec_rank == 0) | (spec_rank == sz.spec - 1), 0.0, 1.0).astype(F32)
    fix[...] = recv_b[...].astype(F32) * real_b
    for k in range(reach):
        complete(sz, base_b + k, fix, k, plain, turned, s_plain)
    turn_halo(sz, base_b, plain, turned, real_b)
    arrays = (plain, turned, plus, minus, s_plain, s_plus, s_minus)
    begin = jnp.where(is_even(), 0, sz.bands)
    ratio = jnp.where(is_even(), band_ratio(sz, 3 - reach), band_ratio(sz, sz.bands + 3 - reach))
    over_bands(reach, ratio, lambda i, r: strengths(sz, r, begin + i, *arrays))

    info = from_e[pl.ds(sz.info // 16 * 16, 32), :].astype(F32)
    at = sz.info % 16 + 1
    s_east = info[at : at + 1] + info[at + 1 : at + 2] + info[at + 2 : at + 3]
    s_north = info[at + 3 : at + 4] + info[at + 4 : at + 5] + info[at + 5 : at + 6]
    total_weight = sz.angles * 0.1 * sum(ratio_step ** (k - sz.freqs // 2) for k in range(sz.freqs))
    means = (pair[...] + other[...]) * (1.0 / total_weight)
    mean = jnp.concatenate([means[0 : sz.cols]] * (VREG // sz.cols), axis=0)
    s_mean = means[sz.cols : sz.cols + 1]

    def result(k, ratio):
        scale = 1.0 / (1.0 + (dissip_coef * ratio * ratio) * mean)
        base = pl.multiple_of(k * sz.ring, VREG)

        def moved_in(v):
            return (
                plus[k, pl.ds(v * VREG, VREG), :]
                + minus[k, pl.ds((v + 3) * VREG, VREG), :]
                + plus[k + 5, pl.ds((v + 2) * VREG, VREG), :]
                + minus[k + 5, pl.ds((v + 1) * VREG, VREG), :]
            )

        before = moved_in(nv - 1)
        for v in range(nv):
            now = moved_in(v)
            moved = pltpu.roll(jnp.where(low, now, before), turn, 0)
            before = now
            here = pl.ds((v + 1) * VREG, VREG)
            transfer = moved - 2.0 * (plus[k + 2, here, :] + minus[k + 2, here, :])
            a = adv[pl.ds(base + v * VREG, VREG), :]
            grown = ratio * gain[pl.ds(v * VREG, VREG), :]
            out[pl.ds(base + v * VREG, VREG), :] = (a + grown * a + transfer) * scale

    over_bands(sz.bands, band_ratio(sz, 0), result)

    s_gain = []
    for v in range(ns):
        here = pl.ds(v * VREG, VREG)
        along = s_moves[3, here, :] * s_east + s_moves[4, here, :] * s_north
        s_gain.append(wind_coef * jnp.maximum(along, 0.0))
    for k in range(sz.bands):
        ratio = band_ratio(sz, k)
        scale = 1.0 / (1.0 + (dissip_coef * ratio * ratio) * s_mean)
        for v in range(ns):
            row = (v + 1) * VREG
            here = pl.ds(row, VREG)
            transfer = (
                s_plus[k, pl.ds(row - 3, VREG), :]
                + s_minus[k, pl.ds(row + 3, VREG), :]
                + s_plus[k + 5, pl.ds(row + 1, VREG), :]
                + s_minus[k + 5, pl.ds(row - 1, VREG), :]
                - 2.0 * (s_plus[k + 2, here, :] + s_minus[k + 2, here, :])
            )
            a = side[pl.ds(k * sz.side + v * VREG, VREG), :]
            s_out[pl.ds(k * sz.angles + v * VREG, VREG), :] = (a + (ratio * s_gain[v]) * a + transfer) * scale

    pad = jnp.zeros((sz.lanes - sz.bins, sz.lat), BF16)
    columns = [out[pl.ds(c, sz.bins, stride=sz.cols), :] for c in range(sz.cols)]
    columns.append(s_out[pl.ds(0, sz.bins), :])
    columns = [jnp.concatenate([c.astype(BF16), pad], axis=0) for c in columns]
    n = (sz.cols + 1) * sz.lat
    spectra = dot_lanes(mix[:, 0:n], jnp.concatenate(columns, axis=1))
    about = mix[:, n : n + 128].astype(F32)
    msg[:, 0 : sz.lanes - 128] = spectra[:, : sz.lanes - 128].astype(BF16)
    msg[:, sz.lanes - 128 : sz.lanes] = (spectra[:, sz.lanes - 128 :] + about).astype(BF16)


def blend_kernel(sz, recv, nest_adv, out):
    spectra = recv[...]
    at = sz.bins - (sz.lanes - 128)
    about = spectra[:, sz.lanes - 128 :].astype(F32)
    t_col, t_row, rate = about[:, at : at + 1], about[:, at + 1 : at + 2], about[:, at + 2 : at + 3]
    lane = lax.broadcasted_iota(jnp.int32, (sz.slots, sz.lat), 1).astype(F32)
    hit = jnp.where(lane == t_row, rate, 0.0)
    for c in range(sz.cols):
        relax = jnp.where(t_col == float(c), hit, 0.0)
        kept = 1.0 - jnp.sum(relax, axis=0, keepdims=True)
        added = lax.dot_general(
            spectra, relax.astype(BF16), (((0,), (0,)), ((), ())), preferred_element_type=F32
        )
        here = pl.ds(c, sz.bins, stride=sz.cols)
        out[here, :] = nest_adv[here, :] * kept + added[: sz.bins]


def kernel_call(body, out_shape, n_in, hbm=(), scratch=(), aliases=None, flops=0, name=None):
    return pl.pallas_call(
        body,
        out_shape=out_shape,
        in_specs=[pl.BlockSpec(memory_space=pltpu.HBM if i in hbm else pltpu.VMEM) for i in range(n_in)],
        out_specs=jax.tree.map(lambda _: pl.BlockSpec(memory_space=pltpu.VMEM), out_shape),
        scratch_shapes=list(scratch),
        input_output_aliases=aliases or {},
        compiler_params=pltpu.CompilerParams(vmem_limit_bytes=20 * 2**20),
        cost_estimate=pl.CostEstimate(flops=flops, bytes_accessed=0, transcendentals=0) if flops else None,
        name=name,
    )


def per_device(
    mesh, energy, nest_energy, ocean_mask, wind_field, rim_cell, rim_dest, rim_target, rim_weight
):
    sz = Sizes(mesh, energy, rim_dest.shape[0])

    def array(*shape, dtype=F32):
        return jax.ShapeDtypeStruct(shape + (sz.lat,), dtype)

    def vmem(*shape):
        return pltpu.VMEM(shape + (sz.lat,), F32)

    def half(rows):
        return array(rows, dtype=BF16)

    field = array(sz.rows)
    table = jnp.asarray(angle_table(sz))
    energy = energy.reshape(sz.rows, sz.lat)
    nest = nest_energy.reshape(sz.rows, sz.lat)
    up = [(i, (i + 1) % sz.grid) for i in range(sz.grid)]
    down = [(j, i) for i, j in up]
    across = [(i, (i + 1 if i % 2 else i - 1) % sz.spec) for i in range(sz.spec)]
    near_rows = [vmem(sz.thin_rows), vmem(sz.thick_rows)]

    stay = functools.partial(pltpu.with_memory_space_constraint, memory_space=pltpu.HBM)
    thin, thick, moves, nest_moves, s_moves, gain, sea = kernel_call(
        functools.partial(pack_kernel, sz),
        (
            half(sz.thin_rows),
            half(sz.thick_rows),
            array(3, sz.ring),
            array(3, sz.ring),
            array(5, sz.side),
            array(sz.ring),
            array(VREG),
        ),
        5,
        hbm=range(5),
        scratch=[
            vmem(*table.shape[:1]),
            vmem(sz.rows),
            vmem(sz.rows),
            pltpu.VMEM(ocean_mask.shape, ocean_mask.dtype),
            pltpu.VMEM(wind_field.shape, F32),
        ]
        + near_rows
        + [pltpu.SemaphoreType.DMA((2 * sz.bands + 3,))],
        name="pack",
    )(stay(table), stay(energy), stay(nest), stay(ocean_mask), stay(wind_field))
    from_e = lax.ppermute(thick, "grid", down)
    from_w = lax.ppermute(thin, "grid", up)

    energy, sea = lax.optimization_barrier((energy, sea))
    raw_a, raw_b = kernel_call(
        functools.partial(raw_kernel, sz), (half(sz.edge_rows), half(sz.edge_rows)), 1, name="raw"
    )(energy)
    pairs = [(i, i ^ 1) for i in range(sz.spec)]
    recv_raw_b = lax.ppermute(raw_b, "spec", [(i, j) for i, j in across if abs(i - j) == 1])
    recv_raw_a = lax.ppermute(raw_a, "spec", pairs)
    rim = (rim_cell.T, rim_dest.T, rim_target.reshape(1, sz.rim), rim_weight.T)
    rim, raw_a = lax.optimization_barrier((rim, raw_a))
    mix = kernel_call(
        functools.partial(rim_kernel, sz),
        jax.ShapeDtypeStruct((sz.slots, (sz.cols + 1) * sz.lat + 128), BF16),
        4,
        name="rim",
    )(*rim)
    nest, raw_a = lax.optimization_barrier((nest, raw_a))
    nest_inner = kernel_call(functools.partial(nest_kernel, sz), field, 2, flops=3 * 10**10, name="nest")(nest, nest_moves)
    from_e, from_w, recv_raw_a, recv_raw_b, mix, nest_inner = lax.optimization_barrier(
        (from_e, from_w, recv_raw_a, recv_raw_b, mix, nest_inner)
    )

    adv, side, msg_a, msg_b, part = kernel_call(
        functools.partial(advect_kernel, sz),
        (field, array(sz.bands * sz.side), half(sz.fix_rows), half(sz.fix_rows + 16), array(VREG)),
        6,
        scratch=near_rows
        + [
            vmem(sz.rows),
            vmem(sz.bands * sz.side),
            vmem(2, VREG),
            vmem(sz.fix_rows),
        ],
        name="advect",
    )(energy, from_w, from_e, moves, s_moves, sea)

    recv_a = lax.ppermute(msg_a, "spec", pairs)
    recv_b = lax.ppermute(msg_b, "spec", across)
    pieces = recv_a[sz.sum_row : sz.sum_row + 3 * VREG].astype(F32)
    pair = part + pieces.reshape(3, VREG, sz.lat).sum(axis=0)
    other = jnp.zeros_like(pair)
    step = 2
    while step < sz.spec:
        pair = pair + other
        other = lax.ppermute(pair, "spec", [(i, i ^ step) for i in range(sz.spec)])
        step *= 2

    nest_adv = kernel_call(
        functools.partial(nest_edge_kernel, sz),
        field,
        4,
        scratch=near_rows,
        aliases={0: 0},
        name="nest_edge",
    )(nest_inner, from_w, from_e, nest_moves)

    padded, centres, turns = sz.bands + 2 * reach, sz.bands + reach, sz.ring + 3 * VREG
    arrays = (
        array(padded, sz.ring),
        array(padded, turns),
        array(centres, turns),
        array(centres, turns),
        array(padded, sz.frame),
        array(centres, sz.frame),
        array(centres, sz.frame),
    )
    inner = kernel_call(
        functools.partial(inner_kernel, sz),
        arrays,
        7,
        scratch=[vmem(sz.edge_rows), vmem(sz.fix_rows)],
        name="inner",
    )(adv, side, recv_a, recv_raw_a, recv_raw_b, moves, sea)
    nest_adv, recv_b = lax.optimization_barrier((nest_adv, recv_b))
    global_next, msg, *_ = kernel_call(
        functools.partial(source_kernel, sz),
        (field, jax.ShapeDtypeStruct((sz.slots, sz.lanes), BF16)) + arrays,
        9 + len(arrays),
        scratch=[vmem(sz.bins + VREG), vmem(sz.fix_rows + 16)],
        aliases={9 + i: 2 + i for i in range(len(arrays))},
        name="sources",
    )(adv, side, recv_b, pair, other, gain, s_moves, from_e, mix, *inner)

    recv = lax.all_to_all(msg, "grid", split_axis=0, concat_axis=0, tiled=True)
    nest_next = kernel_call(functools.partial(blend_kernel, sz), field, 2, name="blend")(recv, nest_adv)
    full = (sz.bands, sz.angles, sz.cols, sz.lat)
    return global_next.reshape(full), nest_next.reshape(full)


def solution(mesh):
    in_specs = (
        P("spec", None, "grid", None),
        P("spec", None, "grid", None),
        P("grid", None),
        P(None, "grid", None),
        P("grid", None),
        P("grid", None),
        P("grid"),
        P("grid", None),
    )
    out_specs = (P("spec", None, "grid", None), P("spec", None, "grid", None))
    return jax.shard_map(
        functools.partial(per_device, mesh),
        mesh=mesh,
        in_specs=in_specs,
        out_specs=out_specs,
        check_vma=False,
    )
```

time: 43.8 us -> 36.5 us (0.83)
  blocking collectives: 17.1 us -> 11.1 us
  starting transfers between devices: 9.58 us -> 14.6 us
  waiting for transfers between devices: 5.35 us -> 0.82 us
  local copies, waits for them, and re-layouts: 2.89 us -> 0.03 us
  Pallas kernels: 7.88 us -> 9.01 us
    ppermute x4 -> x6, starting transfers between devices: 6.87 us -> 13.4 us  [the longest x1 3.1 us: per_device(): from_e = lax.ppermute(thick, 'grid', down)]
    all_to_all x1, blocking collectives: 17.1 us -> 11.1 us  [per_device(): recv = lax.all_to_all(msg, 'grid', split_axis=0, concat_axis=0, tiled=True)]
    ppermute x4 -> x6, waiting for transfers between devices: 3.96 us -> 0.47 us  [the longest x1 0.46 us: per_device(): recv_b = lax.ppermute(msg_b, 'spec', across)]
    unnamed x22 -> x12, local copies, waits for them, and re-layouts: 2.88 us -> 0.03 us
    ppermute x1, starting transfers between devices: 2.71 us -> 1.19 us  [per_device(): other = lax.ppermute(pair, 'spec', [(i, i ^ step) for i in range(sz.spec)])]
    pallas_call x4 -> x8, Pallas kernels: 6.46 us -> 7.6 us  [the longest x1 1.75 us: per_device(): kernel_call(functools.partial(source_kernel, sz), (field, jax.ShapeDtypeS...]
    ppermute x1, waiting for transfers between devices: 1.38 us -> 0.35 us  [per_device(): other = lax.ppermute(pair, 'spec', [(i, i ^ step) for i in range(sz.spec)])]
  transfers between devices with their start and end apart: 5 -> 7, of which waited for: 4 -> 2; matrix products, arithmetic and copies ran while one was open for 0% -> 0% of each run, Pallas kernels for 5% -> 8%
where the time goes in v2:
time: 36.5 us; the launch traced here: 36.3 us
  starting transfers between devices  14.6 us (40%)
  blocking collectives  11.1 us (30%)
  Pallas kernels  9.01 us (25%)
  waiting for transfers between devices  0.82 us (2%)
  between operations  0.77 us (2%)
    all_to_all x1, blocking collectives, per_device(): recv = lax.all_to_all(msg, 'grid', split_axis=0, concat_axis=0, tiled=True)  11.1 us
    ppermute x1, starting transfers between devices, per_device(): from_e = lax.ppermute(thick, 'grid', down)  3.1 us
    ppermute x1, starting transfers between devices, per_device(): from_w = lax.ppermute(thin, 'grid', up)  3.02 us
    ppermute x1, starting transfers between devices, per_device(): recv_raw_a = lax.ppermute(raw_a, 'spec', pairs)  3.01 us
    ppermute x1, starting transfers between devices, per_device(): recv_a = lax.ppermute(msg_a, 'spec', pairs)  1.86 us
    pallas_call x1, Pallas kernels, per_device(): kernel_call(functools.partial(source_kernel, sz), (field, jax.ShapeDtypeS...  1.75 us
    ppermute x1, starting transfers between devices, per_device(): recv_b = lax.ppermute(msg_b, 'spec', across)  1.75 us
    pallas_call x1, Pallas kernels, per_device(): kernel_call(functools.partial(pack_kernel, sz), (half(sz.thin_rows), half...  1.74 us
  transfers between devices with their start and end apart: 7, of which 2 were waited for; matrix products, arithmetic and copies ran while one was open for 0% of the time, Pallas kernels for 8%

profile of v2, /device:TPU:0, one launch (start us, length us, event | category | flops | bytes accessed | tf_op | source)
XLA Modules:
  0.0 36.3 jit_solution(13963706037215607703)
XLA Ops:
  0.6 0.0 copy-start.1
  0.6 0.0 copy-start
  0.7 1.7 %pack.1 = (bf16[336,128]{1,0:T(8,128)(2,1)S(1)}, bf16[688,128]{1,0:T(8,128)(2,1)S(1)}, f32[3,144,128]{2,1,0:T(8,128)S(1)}, f32[3,144,128]{2,1,0:T(8,128)S(1)}, f...) custom-call(f32[192,128]{1,0:T(8,128)} %constant.4.clone.table, f32[1296,128]{1,0:T(8,128)} %bitcast.15, ...), custom_call_target="tpu_custom_call" | custom-call | tf_op jit(solution)/shard_map/pack/pallas_call | solution.py:644
  2.4 3.0 %collective-permute-start.1 = (bf16[336,128]{1,0:T(8,128)(2,1)S(1)}, bf16[336,128]{1,0:T(8,128)(2,1)S(1)}, u32[]{:S(2)}, u32[]{:S(2)}) collective-permute-start(bf16[336,128]{1,0:T(8,128)(2,1)S(1)} %get-tuple-element.42), channel_id=1, source_target_pairs={{0,4},{4,8},{8,12},{12,16},{16,20},{20,24},{24,28},{28,0},{1,5},{5... | collective-permute-start | bytes 258056 | tf_op jit(solution)/shard_map/ppermute | solution.py:669
  5.4 3.1 %collective-permute-start = (bf16[688,128]{1,0:T(8,128)(2,1)S(1)}, bf16[688,128]{1,0:T(8,128)(2,1)S(1)}, u32[]{:S(2)}, u32[]{:S(2)}) collective-permute-start(bf16[688,128]{1,0:T(8,128)(2,1)S(1)} %get-tuple-element.41), channel_id=1, source_target_pairs={{4,0},{8,4},{12,8},{16,12},{20,16},{24,20},{28,24},{0,28},{5,1},{9... | collective-permute-start | bytes 528392 | tf_op jit(solution)/shard_map/ppermute | solution.py:668
  8.5 0.0 copy-done
  8.6 0.7 %collective-permute-start.3 = (bf16[720,128]{1,0:T(8,128)(2,1)S(1)}, bf16[720,128]{1,0:T(8,128)(2,1)S(1)}, u32[]{:S(2)}, u32[]{:S(2)}) collective-permute-start(bf16[720,128]{1,0:T(8,128)(2,1)S(1)} %get-tuple-element.44), channel_id=1, source_target_pairs={{1,2},{2,1},{5,6},{6,5},{9,10},{10,9},{13,14},{14,13},{17,18},{18,... | collective-permute-start | bytes 552968 | tf_op jit(solution)/shard_map/ppermute | solution.py:676
  9.2 3.0 %collective-permute-start.2 = (bf16[720,128]{1,0:T(8,128)(2,1)S(1)}, bf16[720,128]{1,0:T(8,128)(2,1)S(1)}, u32[]{:S(2)}, u32[]{:S(2)}) collective-permute-start(bf16[720,128]{1,0:T(8,128)(2,1)S(1)} %get-tuple-element.43), channel_id=1, source_target_pairs={{0,1},{1,0},{2,3},{3,2},{4,5},{5,4},{6,7},{7,6},{8,9},{9,8},{10,11... | collective-permute-start | bytes 552968 | tf_op jit(solution)/shard_map/ppermute | solution.py:677
  12.3 0.0 copy-done.1
  12.3 0.0 copy-start.2
  12.3 0.0 copy-start.3
  12.3 0.0 copy-start.4
  12.3 0.0 copy-start.5
  12.3 0.8 %nest.1.inner = f32[1296,128]{1,0:T(8,128)S(1)} custom-call(f32[1296,128]{1,0:T(8,128)S(1)} %bitcast.20, f32[3,144,128]{2,1,0:T(8,128)S(1)} %get-tuple-element.49.moves), custom_call_target="tpu_custom_call" | custom-call | flops 30000001024 | tf_op jit(solution)/shard_map/nest/pallas_call | solution.py:687
  13.1 0.0 copy-done.2
  13.1 0.0 copy-done.3
  13.1 0.0 copy-done.4
  13.1 0.0 copy-done.5
  13.2 0.4 %rim.1.mix = bf16[256,768]{1,0:T(8,128)(2,1)S(1)} custom-call(s32[2,128]{1,0:T(2,128)S(1)} %bitcast.23, s32[1,128]{1,0:T(1,128)S(1)} %bitcast.24, s32[1,128]{1,0:T(1,128)S(1)} %bitcast.25, f32[3,128]{1,0:T(4,128)S(1)} %bitcast.22), custom_call_target="tpu_custom_call" | custom-call | tf_op jit(solution)/shard_map/rim/pallas_call | solution.py:680
  13.6 0.0 collective-permute-done.1.from_w
  13.6 0.0 collective-permute-done.from_e
  13.6 0.0 collective-permute-done.3.raw_b
  13.6 0.0 collective-permute-done.2.raw_a
  13.6 1.1 %advect.1 = (f32[1296,128]{1,0:T(8,128)S(1)}, f32[360,128]{1,0:T(8,128)S(1)}, bf16[432,128]{1,0:T(8,128)(2,1)S(1)}, bf16[448,128]{1,0:T(8,128)(2,1)S(1)}, f32[8,128]{1,0:T(8,128)S(1)}) custom-call(f32[1296,128]{1,0:T(8,128)S(1)} %bitcast.17, bf16[336,128]{1,0:T(8,128)(2,1)S(1)} %collective-permute-done.1.from_w, ...), custom_call_target="tpu_custom_call" | custom-call | tf_op jit(solution)/shard_map/advect/pallas_call | solution.py:692
  14.7 1.9 %collective-permute-start.5 = (bf16[432,128]{1,0:T(8,128)(2,1)S(1)}, bf16[432,128]{1,0:T(8,128)(2,1)S(1)}, u32[]{:S(2)}, u32[]{:S(2)}) collective-permute-start(bf16[432,128]{1,0:T(8,128)(2,1)S(1)} %get-tuple-element.61), channel_id=1, source_target_pairs={{0,1},{1,0},{2,3},{3,2},{4,5},{5,4},{6,7},{7,6},{8,9},{9,8},{10,11... | collective-permute-start | bytes 331784 | tf_op jit(solution)/shard_map/ppermute | solution.py:706
  16.5 1.7 %collective-permute-start.4 = (bf16[448,128]{1,0:T(8,128)(2,1)S(1)}, bf16[448,128]{1,0:T(8,128)(2,1)S(1)}, u32[]{:S(2)}, u32[]{:S(2)}) collective-permute-start(bf16[448,128]{1,0:T(8,128)(2,1)S(1)} %get-tuple-element.58), channel_id=1, source_target_pairs={{0,3},{1,2},{2,1},{3,0},{4,7},{5,6},{6,5},{7,4},{8,11},{9,10},{10,... | collective-permute-start | bytes 344072 | tf_op jit(solution)/shard_map/ppermute | solution.py:707
  18.3 0.0 collective-permute-done.5.recv_a
  18.3 1.2 %collective-permute-start.6 = (f32[8,128]{1,0:T(8,128)S(1)}, f32[8,128]{1,0:T(8,128)S(1)}, u32[]{:S(2)}, u32[]{:S(2)}) collective-permute-start(f32[8,128]{1,0:T(8,128)S(1)} %add.3.pair), channel_id=1, source_target_pairs={{0,2},{1,3},{2,0},{3,1},{4,6},{5,7},{6,4},{7,5},{8,10},{9,11},{10,... | collective-permute-start | bytes 12296 | tf_op jit(solution)/shard_map/ppermute | solution.py:714
  19.5 0.1 nest_edge.1.nest_adv
  19.6 1.7 %inner.1 = (f32[19,144,128]{2,1,0:T(8,128)S(1)}, f32[19,168,128]{2,1,0:T(8,128)S(1)}, f32[14,168,128]{2,1,0:T(8,128)S(1)}, f32[14,168,128]{2,1,0:T(8,128)S(1)}, ...) custom-call(f32[1296,128]{1,0:T(8,128)S(1)} %get-tuple-element.55.adv, ...), custom_call_target="tpu_custom_call" | custom-call | tf_op jit(solution)/shard_map/inner/pallas_call | solution.py:736
  21.3 0.5 %collective-permute-done.4.recv_b = bf16[448,128]{1,0:T(8,128)(2,1)S(1)} collective-permute-done((bf16[448,128]{1,0:T(8,128)(2,1)S(1)}, bf16[448,128]{1,0:T(8,128)(2,1)S(1)}, u32[]{:S(2)}, u32[]{:S(2)}) %collective-permute-start.4) | collective-permute-done | bytes 114720 | tf_op jit(solution)/shard_map/ppermute | solution.py:707
  21.7 0.4 collective-permute-done.6.other
  22.1 1.7 %sources.1 = (f32[1296,128]{1,0:T(8,128)}, bf16[256,384]{1,0:T(8,128)(2,1)S(1)}, f32[19,144,128]{2,1,0:T(8,128)S(1)}, f32[19,168,128]{2,1,0:T(8,128)S(1)}, f32[1...) custom-call(f32[1296,128]{1,0:T(8,128)S(1)} %get-tuple-element.55.ad, ...), custom_call_target="tpu_custom_call", output_to_operand_aliasing={{2}: (9, {}), {3}: (10, {}), {4}: (11, {}), {5}: (12, {}), ... | custom-call | tf_op jit(solution)/shard_map/sources/pallas_call | solution.py:744
  23.8 11.1 %all_to_all.11 = bf16[8,32,384]{2,1,0:T(8,128)(2,1)S(1)} all-to-all(bf16[8,32,384]{2,1,0:T(8,128)(2,1)S(1)} %bitcast.21), channel_id=1, replica_groups=mesh['grid'=8,'spec'=4] {'grid'}, dimensions={0} | all-to-all | bytes 393216 | tf_op jit(solution)/shard_map/all_to_all | solution.py:753
  34.9 1.4 %blend.1 = f32[1296,128]{1,0:T(8,128)} custom-call(bf16[256,384]{1,0:T(8,128)(2,1)S(1)} %bitcast.18, f32[1296,128]{1,0:T(8,128)S(1)} %nest_edge.1.nest_adv), custom_call_target="tpu_custom_call" | custom-call | tf_op jit(solution)/shard_map/blend/pallas_call | solution.py:754
  (3 shorter events, 0.0 us)
Async XLA Ops:
  0.6 11.6 %copy-start.1 = (f32[9,36,4,128]{3,2,1,0:T(4,128)S(1)}, f32[9,36,4,128]{3,2,1,0:T(4,128)}, u32[]{:S(2)}) copy-start(f32[9,36,4,128]{3,2,1,0:T(4,128)} %param.10) | copy-start | bytes 1990660
  0.6 7.9 %copy-start = (f32[9,36,4,128]{3,2,1,0:T(4,128)S(1)}, f32[9,36,4,128]{3,2,1,0:T(4,128)}, u32[]{:S(2)}) copy-start(f32[9,36,4,128]{3,2,1,0:T(4,128)} %param.9) | copy-start | bytes 1990660
  2.4 11.2 %collective-permute-start.1 = (bf16[336,128]{1,0:T(8,128)(2,1)S(1)}, bf16[336,128]{1,0:T(8,128)(2,1)S(1)}, u32[]{:S(2)}, u32[]{:S(2)}) collective-permute-start(bf16[336,128]{1,0:T(8,128)(2,1)S(1)} %get-tuple-element.42), channel_id=1, source_target_pairs={{0,4},{4,8},{8,12},{12,16},{16,20},{20,24},{24,28},{28,0},{1,5},{5... | collective-permute-start | bytes 258056 | tf_op jit(solution)/shard_map/ppermute | solution.py:669
  5.4 8.2 %collective-permute-start = (bf16[688,128]{1,0:T(8,128)(2,1)S(1)}, bf16[688,128]{1,0:T(8,128)(2,1)S(1)}, u32[]{:S(2)}, u32[]{:S(2)}) collective-permute-start(bf16[688,128]{1,0:T(8,128)(2,1)S(1)} %get-tuple-element.41), channel_id=1, source_target_pairs={{4,0},{8,4},{12,8},{16,12},{20,16},{24,20},{28,24},{0,28},{5,1},{9... | collective-permute-start | bytes 528392 | tf_op jit(solution)/shard_map/ppermute | solution.py:668
  8.6 5.0 %collective-permute-start.3 = (bf16[720,128]{1,0:T(8,128)(2,1)S(1)}, bf16[720,128]{1,0:T(8,128)(2,1)S(1)}, u32[]{:S(2)}, u32[]{:S(2)}) collective-permute-start(bf16[720,128]{1,0:T(8,128)(2,1)S(1)} %get-tuple-element.44), channel_id=1, source_target_pairs={{1,2},{2,1},{5,6},{6,5},{9,10},{10,9},{13,14},{14,13},{17,18},{18,... | collective-permute-start | bytes 552968 | tf_op jit(solution)/shard_map/ppermute | solution.py:676
  9.2 4.3 %collective-permute-start.2 = (bf16[720,128]{1,0:T(8,128)(2,1)S(1)}, bf16[720,128]{1,0:T(8,128)(2,1)S(1)}, u32[]{:S(2)}, u32[]{:S(2)}) collective-permute-start(bf16[720,128]{1,0:T(8,128)(2,1)S(1)} %get-tuple-element.43), channel_id=1, source_target_pairs={{0,1},{1,0},{2,3},{3,2},{4,5},{5,4},{6,7},{7,6},{8,9},{9,8},{10,11... | collective-permute-start | bytes 552968 | tf_op jit(solution)/shard_map/ppermute | solution.py:677
  12.3 0.9 %copy-start.2 = (f32[128,3]{0,1:T(4,128)S(1)}, f32[128,3]{0,1:T(4,128)}, u32[]{:S(2)}) copy-start(f32[128,3]{0,1:T(4,128)} %param.16) | copy-start | bytes 4612
  12.3 0.9 %copy-start.3 = (s32[128,2]{0,1:T(2,128)S(1)}, s32[128,2]{0,1:T(2,128)}, u32[]{:S(2)}) copy-start(s32[128,2]{0,1:T(2,128)} %param.13) | copy-start | bytes 3076
  12.3 0.9 %copy-start.4 = (s32[128,1]{0,1:T(1,128)S(1)}, s32[128,1]{0,1:T(1,128)}, u32[]{:S(2)}) copy-start(s32[128,1]{0,1:T(1,128)} %param.14) | copy-start | bytes 1540
  12.3 0.9 %copy-start.5 = (s32[128]{0:T(128)S(1)}, s32[128]{0:T(128)}, u32[]{:S(2)}) copy-start(s32[128]{0:T(128)} %param.15) | copy-start | bytes 1540
  14.7 3.6 %collective-permute-start.5 = (bf16[432,128]{1,0:T(8,128)(2,1)S(1)}, bf16[432,128]{1,0:T(8,128)(2,1)S(1)}, u32[]{:S(2)}, u32[]{:S(2)}) collective-permute-start(bf16[432,128]{1,0:T(8,128)(2,1)S(1)} %get-tuple-element.61), channel_id=1, source_target_pairs={{0,1},{1,0},{2,3},{3,2},{4,5},{5,4},{6,7},{7,6},{8,9},{9,8},{10,11... | collective-permute-start | bytes 331784 | tf_op jit(solution)/shard_map/ppermute | solution.py:706
  16.5 5.2 %collective-permute-start.4 = (bf16[448,128]{1,0:T(8,128)(2,1)S(1)}, bf16[448,128]{1,0:T(8,128)(2,1)S(1)}, u32[]{:S(2)}, u32[]{:S(2)}) collective-permute-start(bf16[448,128]{1,0:T(8,128)(2,1)S(1)} %get-tuple-element.58), channel_id=1, source_target_pairs={{0,3},{1,2},{2,1},{3,0},{4,7},{5,6},{6,5},{7,4},{8,11},{9,10},{10,... | collective-permute-start | bytes 344072 | tf_op jit(solution)/shard_map/ppermute | solution.py:707
  18.3 3.8 %collective-permute-start.6 = (f32[8,128]{1,0:T(8,128)S(1)}, f32[8,128]{1,0:T(8,128)S(1)}, u32[]{:S(2)}, u32[]{:S(2)}) collective-permute-start(f32[8,128]{1,0:T(8,128)S(1)} %add.3.pair), channel_id=1, source_target_pairs={{0,2},{1,3},{2,0},{3,1},{4,6},{5,7},{6,4},{7,5},{8,10},{9,11},{10,... | collective-permute-start | bytes 12296 | tf_op jit(solution)/shard_map/ppermute | solution.py:714

commit v3 on v2

--- a/solution.py
+++ b/solution.py
@@ -46,10 +46,12 @@
         self.thick_nest = (self.info + 7 + VREG - 1) // VREG * VREG
         self.thick_rows = (self.thick_nest + self.thin + 15) // 16 * 16
         self.edge_rows = reach * self.ring
-        self.rim_band = (2 * self.half + VREG - 1) // VREG * VREG
-        self.far_band = self.rim_band + self.side
-        self.sum_row = reach * self.far_band
+        self.rim_band = 2 * self.half
+        self.far_band = self.rim_band + self.angles
+        self.sum_row = (reach * self.far_band + VREG - 1) // VREG * VREG
         self.fix_rows = (self.sum_row + 3 * VREG + 15) // 16 * 16
+        self.pass_thick = (reach * self.half + VREG - 1) // VREG * VREG
+        self.pass_rows = max(self.fix_rows + 16, (self.pass_thick + reach * self.thick + 15) // 16 * 16)
 
 
 def band_ratio(sz, band, inverse=False):
@@ -124,11 +126,7 @@
     thin, thick, moves, nest_moves, s_moves, gain, sea,
     table_v, field, nest_field, mask_v, wind_v, tmp_thin, tmp_thick, sems,
 ):
-    pairs = [(table, table_v), (mask, mask_v), (wind, wind_v)]
-    for source, target in ((energy, field), (nest, nest_field)):
-        for k in range(sz.bands):
-            band = pl.ds(k * sz.ring, sz.ring)
-            pairs.append((source.at[band], target.at[band]))
+    pairs = [(table, table_v), (mask, mask_v), (wind, wind_v), (energy, field), (nest, nest_field)]
     copies = [pltpu.make_async_copy(a, b, sems.at[i]) for i, (a, b) in enumerate(pairs)]
     for copy in copies:
         copy.start()
@@ -166,15 +164,15 @@
         start = row + sz.quarter * sz.cols
         tmp_thick[pl.ds(at, sz.half), :] = source[pl.ds(start, sz.half, stride=sz.cols), :]
 
+    copies[3].wait()
     for k in range(sz.bands):
-        copies[k + 3].wait()
         row = k * sz.ring
         west(field, row, k * sz.half)
         at = k * sz.thick
         tmp_thick[pl.ds(at, sz.angles), :] = field[pl.ds(row, sz.angles, stride=sz.cols), :]
         east(field, row + 1, at + sz.angles)
+    copies[4].wait()
     for k in range(sz.bands):
-        copies[k + 3 + sz.bands].wait()
         row = k * sz.ring
         west(nest_field, row, sz.thin + k * sz.half)
         east(nest_field, row, sz.thick_nest + k * sz.half)
@@ -187,15 +185,16 @@
         raw[...] = energy[pl.ds(pl.multiple_of(first * sz.ring, VREG), sz.edge_rows), :].astype(BF16)
 
 
-def spread_halo(sz, wide_w, first_w, wide_e, stride_e, first_e, halo):
-    for k in range(sz.bands):
-        at = first_w + k * sz.half
-        for first, count in west_half(sz):
-            start = k * sz.ring + first * sz.cols
-            halo[pl.ds(start, count, stride=sz.cols), :] = wide_w[pl.ds(at, count), :]
-            at += count
-        start = k * sz.ring + (sz.quarter + 1) * sz.cols - 1
-        halo[pl.ds(start, sz.half, stride=sz.cols), :] = wide_e[pl.ds(k * stride_e + first_e, sz.half), :]
+def pass_kernel(sz, from_w, from_e, msg, wide_w, wide_e, tmp):
+    wide_w[...] = from_w[...].astype(F32)
+    wide_e[...] = from_e[...].astype(F32)
+    tmp[...] = jnp.zeros_like(tmp)
+    first = far_band(sz)
+    count = reach * sz.half
+    tmp[pl.ds(0, count), :] = wide_w[pl.ds(first * sz.half, count), :]
+    start = pl.multiple_of(first * sz.thick, VREG)
+    tmp[pl.ds(sz.pass_thick, reach * sz.thick), :] = wide_e[pl.ds(start, reach * sz.thick), :]
+    msg[...] = tmp[...].astype(BF16)
 
 
 def fill_moves(sz, rows, table, cols, targets):
@@ -224,7 +223,7 @@
     return jnp.where(sub < turn, pltpu.roll(x, 1, 1), pltpu.roll(x, sz.lat - 1, 1))
 
 
-def transported(sz, field, halo, base, v, moves, speed):
+def transported(sz, field, base, v, moves, speed):
     here = pl.ds(v * VREG, VREG)
     x = field[pl.ds(base + v * VREG, VREG), :]
     wests, west, col = upwind(sz, v)
@@ -235,85 +234,111 @@
     else:
         near = jnp.where(west, pltpu.roll(x, 1, 0), pltpu.roll(x, VREG - 1, 0))
         at_edge = jnp.where(west, col, sz.cols - 1 - col) == 0
-    edge = 0.0 if halo is None else halo[pl.ds(base + v * VREG, VREG), :]
-    near = jnp.where(at_edge, edge, near)
+    near = jnp.where(at_edge, 0.0, near)
     south = sz.half * sz.cols - v * VREG
     return x - speed * (moves[0, here, :] * x - moves[1, here, :] * near - moves[2, here, :] * beside(sz, x, south))
 
 
-def advect_kernel(
-    sz, energy, from_w, from_e, moves, s_moves, sea, adv, side, msg_a, msg_b, part,
-    wide_w, wide_e, halo, s_near, totals, fix,
+def edge_parts(sz, moves, wide_w, at_w, wide_e, at_e):
+    parts = []
+    for first, count in west_half(sz):
+        parts.append((first, count, 0, wide_w[pl.ds(at_w, count), :]))
+        at_w += count
+    parts.append((sz.quarter, sz.half, sz.cols - 1, wide_e[pl.ds(at_e, sz.half), :]))
+    for first, count, col, cells in parts:
+        yield first, count, col, moves[1, pl.ds(first * sz.cols, count, stride=sz.cols), :] * cells
+
+
+def side_transported(sz, x, near, v, s_moves, speed):
+    here = pl.ds(v * VREG, VREG)
+    move = s_moves[0, here, :] * x - s_moves[1, here, :] * near
+    return x - speed * (move - s_moves[2, here, :] * beside(sz, x, sz.half - v * VREG))
+
+
+def local_kernel(sz, energy, moves, sea, adv, total):
+    total[...] = jnp.zeros_like(total)
+
+    def band(k, inverse):
+        base = pl.multiple_of(k * sz.ring, VREG)
+        line = jnp.zeros((VREG, sz.lat), F32)
+        for v in range(sz.vregs):
+            out = sea[...] * transported(sz, energy, base, v, moves, speed_coef * inverse)
+            adv[pl.ds(base + v * VREG, VREG), :] = out
+            line = line + out
+        total[...] = total[...] * F32(1.0 / ratio_step) + line
+
+    over_bands(sz.bands, band_ratio(sz, 0, True), band, True)
+    total[...] = total[...] * (0.1 * band_ratio(sz, sz.bands - 1))
+
+
+def edge_kernel(
+    sz, adv_in, total, energy, from_w, from_e, moves, s_moves, sea, adv, side, msg_a, part,
+    wide_w, wide_e, s_near, fix,
 ):
     wide_w[...] = from_w[...].astype(F32)
     wide_e[...] = from_e[...].astype(F32)
-    spread_halo(sz, wide_w, 0, wide_e, sz.thick, sz.quarter, halo)
+    s_sea = wide_e[pl.ds(sz.info, 1), :]
+    sub = lax.broadcasted_iota(jnp.int32, (VREG, sz.lat), 0)
+    s_total = jnp.zeros((VREG, sz.lat), F32)
+    lines = {}
     for k in range(sz.bands):
+        inverse = band_ratio(sz, k, True)
+        weight = 0.1 * band_ratio(sz, k)
+        speed = speed_coef * inverse
+        at_e = k * sz.thick + sz.quarter
+        for first, count, col, moved in edge_parts(sz, moves, wide_w, k * sz.half, wide_e, at_e):
+            moved = moved * (speed * sea[col : col + 1, :])
+            rows = pl.ds(k * sz.ring + first * sz.cols + col, count, stride=sz.cols)
+            adv[rows, :] = adv[rows, :] + moved
+            lines[first, col] = lines.get((first, col), 0.0) + moved * weight
+        at = k * sz.side
         for first, count in west_half(sz):
             start = k * sz.ring + first * sz.cols + sz.cols - 1
-            s_near[pl.ds(k * sz.side + first, count), :] = energy[pl.ds(start, count, stride=sz.cols), :]
-        there = pl.ds(k * sz.thick + sz.angles, sz.half)
-        s_near[pl.ds(k * sz.side + sz.quarter, sz.half), :] = wide_e[there, :]
+            s_near[pl.ds(at + first, count), :] = energy[pl.ds(start, count, stride=sz.cols), :]
+        s_near[pl.ds(at + sz.quarter, sz.half), :] = wide_e[pl.ds(k * sz.thick + sz.angles, sz.half), :]
         if sz.side > sz.angles:
             rest = sz.side - sz.angles
-            s_near[pl.ds(k * sz.side + sz.angles, rest), :] = jnp.zeros((rest, sz.lat), F32)
-    s_sea = wide_e[pl.ds(sz.info, 1), :]
-    sub = lax.broadcasted_iota(jnp.int32, (VREG, sz.lat), 0)
-    totals[...] = jnp.zeros_like(totals)
-
-    def band(k, inverse):
-        speed = speed_coef * inverse
-        base = pl.multiple_of(k * sz.ring, VREG)
-        line = jnp.zeros((VREG, sz.lat), F32)
-        for v in range(sz.vregs):
-            out = sea[...] * transported(sz, energy, halo, base, v, moves, speed)
-            adv[pl.ds(base + v * VREG, VREG), :] = out
-            line = line + out
+            s_near[pl.ds(at + sz.angles, rest), :] = jnp.zeros((rest, sz.lat), F32)
         s_line = jnp.zeros((VREG, sz.lat), F32)
-        s_base = pl.multiple_of(k * sz.side, VREG)
-        from_base = pl.multiple_of(k * sz.thick, VREG)
         for v in range(sz.side // VREG):
-            here = pl.ds(v * VREG, VREG)
-            x = wide_e[pl.ds(from_base + v * VREG, VREG), :]
-            near = s_near[pl.ds(s_base + v * VREG, VREG), :]
-            move = s_moves[0, here, :] * x - s_moves[1, here, :] * near
-            move = move - s_moves[2, here, :] * beside(sz, x, sz.half - v * VREG)
-            out = s_sea * (x - speed * move)
-            side[pl.ds(s_base + v * VREG, VREG), :] = out
-            s_line = s_line + jnp.where(sub < sz.angles - v * VREG, out, 0.0)
-        totals[0] = totals[0] * F32(1.0 / ratio_step) + line
-        totals[1] = totals[1] * F32(1.0 / ratio_step) + s_line
-
-    over_bands(sz.bands, band_ratio(sz, 0, True), band, True)
-    weight = 0.1 * band_ratio(sz, sz.bands - 1)
-    total, s_total = totals[0] * weight, totals[1] * weight
-    sums = total[0 : sz.cols]
+            x = wide_e[pl.ds(k * sz.thick + v * VREG, VREG), :]
+            near = s_near[pl.ds(at + v * VREG, VREG), :]
+            out = s_sea * side_transported(sz, x, near, v, s_moves, speed)
+            side[pl.ds(at + v * VREG, VREG), :] = out
+            s_line = s_line + (out if (v + 1) * VREG <= sz.angles else jnp.where(sub < sz.angles - v * VREG, out, 0.0))
+        s_total = s_total + s_line * weight
+    mine = total[0 : sz.cols, :]
     for i in range(1, VREG // sz.cols):
-        sums = sums + total[i * sz.cols : (i + 1) * sz.cols]
+        mine = mine + total[i * sz.cols : (i + 1) * sz.cols, :]
+    west, east = (
+        sum(jnp.sum(x, axis=0, keepdims=True) for (_, c), x in lines.items() if c == col) for col in (0, sz.cols - 1)
+    )
+    between = jnp.zeros((sz.cols - 2, sz.lat), F32)
+    mine = mine + jnp.concatenate([west, between, east], axis=0)
     s_sum = jnp.sum(s_total, axis=0, keepdims=True)
-    sums = jnp.concatenate([sums, s_sum, jnp.zeros((VREG - sz.cols - 1, sz.lat), F32)], axis=0)
+    sums = jnp.concatenate([mine, s_sum, jnp.zeros((VREG - sz.cols - 1, sz.lat), F32)], axis=0)
     part[...] = sums
     fix[...] = jnp.zeros_like(fix)
     fix[pl.ds(sz.sum_row, 3 * VREG), :] = jnp.concatenate(split3(sums), axis=0)
-    for msg, start in ((msg_a, sz.bands - reach - far_band(sz)), (msg_b, far_band(sz))):
-        for k in range(reach):
-            band_row = pl.multiple_of((start + k) * sz.ring, VREG)
-            at = k * sz.far_band
-            for first, count in west_half(sz):
-                fix[pl.ds(at, count), :] = adv[pl.ds(band_row + first * sz.cols, count, stride=sz.cols), :]
-                at += count
-            last = band_row + (sz.quarter + 1) * sz.cols - 1
-            fix[pl.ds(at, sz.half), :] = adv[pl.ds(last, sz.half, stride=sz.cols), :]
-            s_row = pl.multiple_of((start + k) * sz.side, VREG)
-            fix[pl.ds(k * sz.far_band + sz.rim_band, sz.side), :] = side[pl.ds(s_row, sz.side), :]
-        msg[...] = fix[...].astype(BF16) if msg is msg_a else jnp.concatenate([fix[...], fix[0:16, :]], axis=0).astype(BF16)
+    start = sz.bands - reach - far_band(sz)
+    for k in range(reach):
+        band_row = pl.multiple_of((start + k) * sz.ring, VREG)
+        at = k * sz.far_band
+        for first, count in west_half(sz):
+            fix[pl.ds(at, count), :] = adv[pl.ds(band_row + first * sz.cols, count, stride=sz.cols), :]
+            at += count
+        last = band_row + (sz.quarter + 1) * sz.cols - 1
+        fix[pl.ds(at, sz.half), :] = adv[pl.ds(last, sz.half, stride=sz.cols), :]
+        s_row = pl.multiple_of((start + k) * sz.side, VREG)
+        fix[pl.ds(k * sz.far_band + sz.rim_band, sz.angles), :] = side[pl.ds(s_row, sz.angles), :]
+    msg_a[...] = fix[...].astype(BF16)
 
 
 def nest_kernel(sz, nest, moves, out):
     def band(k, inverse):
         base = pl.multiple_of(k * sz.ring, VREG)
         for v in range(sz.vregs):
-            moved = transported(sz, nest, None, base, v, moves, nest_speedup * speed_coef * inverse)
+            moved = transported(sz, nest, base, v, moves, nest_speedup * speed_coef * inverse)
             out[pl.ds(base + v * VREG, VREG), :] = moved
 
     over_bands(sz.bands, band_ratio(sz, 0, True), band, True)
@@ -328,17 +353,10 @@
     wide_e[...] = from_e[...].astype(F32)
     for k in range(sz.bands):
         speed = nest_speedup * speed_coef * band_ratio(sz, k, True)
-
-        def add(first, count, col, wide, at, keep):
+        at_w, at_e = sz.thin + k * sz.half, sz.thick_nest + k * sz.half
+        for first, count, col, moved in edge_parts(sz, moves, wide_w, at_w, wide_e, at_e):
             rows = pl.ds(k * sz.ring + first * sz.cols + col, count, stride=sz.cols)
-            by = moves[1, pl.ds(first * sz.cols, count, stride=sz.cols), :] * (speed * keep)
-            out[rows, :] = out[rows, :] + by * wide[pl.ds(at, count), :]
-
-        at = sz.thin + k * sz.half
-        for first, count in west_half(sz):
-            add(first, count, 0, wide_w, at, keep_w)
-            at += count
-        add(sz.quarter, sz.half, sz.cols - 1, wide_e, sz.thick_nest + k * sz.half, keep_e)
+            out[rows, :] = out[rows, :] + moved * (speed * (keep_w if col == 0 else keep_e))
 
 
 def dot_lanes(a, b):
@@ -440,7 +458,7 @@
     return lax.rem(lax.axis_index("spec"), 2) == 0
 
 
-def complete(sz, slot, fix, k, plain, turned, s_plain, real=None):
+def complete(sz, slot, fix, k, plain, s_plain):
     at = k * sz.far_band
     for start, count in west_half(sz):
         plain[slot, pl.ds(start * sz.cols, count, stride=sz.cols), :] = fix[pl.ds(at, count), :]
@@ -461,7 +479,7 @@
 
 
 def inner_kernel(
-    sz, adv, side, recv_a, raw_a, raw_b, moves, sea, plain, turned, plus, minus, s_plain, s_plus, s_minus, wide, fix
+    sz, adv, side, recv_a, raw_a, raw_b, moves, sea, plain, turned, plus, minus, s_plain, s_plus, s_minus, far_near, wide, fix
 ):
     base_a = jnp.where(is_even(), sz.bands + reach, 0)
     base_b = sz.bands + reach - base_a
@@ -485,14 +503,19 @@
         def transport(k, r, first=first):
             base = pl.multiple_of(k * sz.ring, VREG)
             for v in range(sz.vregs):
-                moved = transported(sz, wide, None, base, v, moves, speed_coef * r)
+                moved = transported(sz, wide, base, v, moves, speed_coef * r)
                 plain[first + k, pl.ds(v * VREG, VREG), :] = sea[...] * moved
 
         over_bands(reach, inverse, transport, True)
 
+    far_near[...] = jnp.zeros_like(far_near)
+    for k in range(reach):
+        for first, count in west_half(sz):
+            start = k * sz.ring + first * sz.cols + sz.cols - 1
+            far_near[pl.ds(k * sz.side + first, count), :] = wide[pl.ds(start, count, stride=sz.cols), :]
     fix[...] = recv_a[...].astype(F32)
     for k in range(reach):
-        complete(sz, base_a + k, fix, k, plain, turned, s_plain)
+        complete(sz, base_a + k, fix, k, plain, s_plain)
     turn_halo(sz, base_a, plain, turned)
 
     arrays = (plain, turned, plus, minus, s_plain, s_plus, s_minus)
@@ -502,26 +525,43 @@
 
 
 def source_kernel(
-    sz, adv, side, recv_b, pair, other, gain, s_moves, from_e, mix,
+    sz, adv, side, recv_b, pair, other, gain, moves, s_moves, sea, from_e, mix, far_near,
     plain_in, turned_in, plus_in, minus_in, s_plain_in, s_plus_in, s_minus_in,
-    out, msg, plain, turned, plus, minus, s_plain, s_plus, s_minus, s_out, fix,
+    result_hbm, msg, plain, turned, plus, minus, s_plain, s_plus, s_minus, s_out, wide, s_near, out, sems,
 ):
     spec_rank = lax.axis_index("spec")
     nv, ns = sz.vregs, sz.side // VREG
     low, turn = low_rows(sz), VREG // 2
     base_b = jnp.where(is_even(), 0, sz.bands + reach)
     real_b = jnp.where((spec_rank == 0) | (spec_rank == sz.spec - 1), 0.0, 1.0).astype(F32)
-    fix[...] = recv_b[...].astype(F32) * real_b
+    info = from_e[pl.ds(sz.info // 16 * 16, 32), :].astype(F32)
+    at = sz.info % 16
+    s_sea = info[at : at + 1] * real_b
+    wide[...] = recv_b[...].astype(F32)
+    s_near[...] = far_near[...]
+    inverse = jnp.where(is_even(), band_ratio(sz, -reach, True), band_ratio(sz, sz.bands, True))
     for k in range(reach):
-        complete(sz, base_b + k, fix, k, plain, turned, s_plain)
+        speed = inverse * (speed_coef / ratio_step**k)
+        slot, row = base_b + k, sz.pass_thick + k * sz.thick
+        for start, count, col, moved in edge_parts(sz, moves, wide, k * sz.half, wide, row + sz.quarter):
+            rows = pl.ds(start * sz.cols + col, count, stride=sz.cols)
+            plain[slot, rows, :] = plain[slot, rows, :] + moved * (speed * sea[col : col + 1, :])
+        at_near = k * sz.side
+        s_near[pl.ds(at_near + sz.quarter, sz.half), :] = wide[pl.ds(row + sz.angles, sz.half), :]
+
+        def column(v):
+            x = wide[pl.ds(row + v * VREG, VREG), :]
+            near = s_near[pl.ds(at_near + v * VREG, VREG), :]
+            return s_sea * side_transported(sz, x, near, v, s_moves, speed)
+
+        s_put(sz, s_plain, slot, column)
     turn_halo(sz, base_b, plain, turned, real_b)
     arrays = (plain, turned, plus, minus, s_plain, s_plus, s_minus)
     begin = jnp.where(is_even(), 0, sz.bands)
     ratio = jnp.where(is_even(), band_ratio(sz, 3 - reach), band_ratio(sz, sz.bands + 3 - reach))
     over_bands(reach, ratio, lambda i, r: strengths(sz, r, begin + i, *arrays))
 
-    info = from_e[pl.ds(sz.info // 16 * 16, 32), :].astype(F32)
-    at = sz.info % 16 + 1
+    at = at + 1
     s_east = info[at : at + 1] + info[at + 1 : at + 2] + info[at + 2 : at + 3]
     s_north = info[at + 3 : at + 4] + info[at + 4 : at + 5] + info[at + 5 : at + 6]
     total_weight = sz.angles * 0.1 * sum(ratio_step ** (k - sz.freqs // 2) for k in range(sz.freqs))
@@ -551,6 +591,11 @@
             a = adv[pl.ds(base + v * VREG, VREG), :]
             grown = ratio * gain[pl.ds(v * VREG, VREG), :]
             out[pl.ds(base + v * VREG, VREG), :] = (a + grown * a + transfer) * scale
+        write(k).start()
+
+    def write(k):
+        band = pl.ds(pl.multiple_of(k * sz.ring, VREG), sz.ring)
+        return pltpu.make_async_copy(out.at[band], result_hbm.at[band], sems.at[k])
 
     over_bands(sz.bands, band_ratio(sz, 0), result)
 
@@ -584,31 +629,46 @@
     about = mix[:, n : n + 128].astype(F32)
     msg[:, 0 : sz.lanes - 128] = spectra[:, : sz.lanes - 128].astype(BF16)
     msg[:, sz.lanes - 128 : sz.lanes] = (spectra[:, sz.lanes - 128 :] + about).astype(BF16)
-
-
-def blend_kernel(sz, recv, nest_adv, out):
-    spectra = recv[...]
+    for k in range(sz.bands):
+        write(k).wait()
+
+
+def blend_kernel(sz, recv, nest_adv, result_hbm, out, sems):
     at = sz.bins - (sz.lanes - 128)
-    about = spectra[:, sz.lanes - 128 :].astype(F32)
+    about = recv[:, sz.lanes - 128 :].astype(F32)
     t_col, t_row, rate = about[:, at : at + 1], about[:, at + 1 : at + 2], about[:, at + 2 : at + 3]
     lane = lax.broadcasted_iota(jnp.int32, (sz.slots, sz.lat), 1).astype(F32)
     hit = jnp.where(lane == t_row, rate, 0.0)
-    for c in range(sz.cols):
-        relax = jnp.where(t_col == float(c), hit, 0.0)
-        kept = 1.0 - jnp.sum(relax, axis=0, keepdims=True)
+    relax = [jnp.where(t_col == float(c), hit, 0.0) for c in range(sz.cols)]
+    kept = [1.0 - jnp.sum(r, axis=0, keepdims=True) for r in relax]
+    relax = jnp.concatenate(relax, axis=1).astype(BF16)
+    writes = []
+    for part, start in enumerate(range(0, sz.bins, 128)):
+        count = min(128, sz.bins - start)
         added = lax.dot_general(
-            spectra, relax.astype(BF16), (((0,), (0,)), ((), ())), preferred_element_type=F32
+            recv[:, start : start + 128], relax, (((0,), (0,)), ((), ())), preferred_element_type=F32
         )
-        here = pl.ds(c, sz.bins, stride=sz.cols)
-        out[here, :] = nest_adv[here, :] * kept + added[: sz.bins]
-
-
-def kernel_call(body, out_shape, n_in, hbm=(), scratch=(), aliases=None, flops=0, name=None):
+        for c in range(sz.cols):
+            here = pl.ds(start * sz.cols + c, count, stride=sz.cols)
+            out[here, :] = nest_adv[here, :] * kept[c] + added[:count, c * sz.lat : (c + 1) * sz.lat]
+        rows = pl.ds(start * sz.cols, count * sz.cols)
+        writes.append(pltpu.make_async_copy(out.at[rows], result_hbm.at[rows], sems.at[part]))
+        writes[-1].start()
+    for write in writes:
+        write.wait()
+
+
+def kernel_call(body, out_shape, n_in, hbm=(), out_hbm=(), scratch=(), aliases=None, flops=0, name=None):
+    def specs(count, far):
+        return [pl.BlockSpec(memory_space=pltpu.HBM if i in far else pltpu.VMEM) for i in range(count)]
+
+    many = isinstance(out_shape, tuple)
+    out_specs = specs(len(out_shape) if many else 1, out_hbm)
     return pl.pallas_call(
         body,
         out_shape=out_shape,
-        in_specs=[pl.BlockSpec(memory_space=pltpu.HBM if i in hbm else pltpu.VMEM) for i in range(n_in)],
-        out_specs=jax.tree.map(lambda _: pl.BlockSpec(memory_space=pltpu.VMEM), out_shape),
+        in_specs=specs(n_in, hbm),
+        out_specs=out_specs if many else out_specs[0],
         scratch_shapes=list(scratch),
         input_output_aliases=aliases or {},
         compiler_params=pltpu.CompilerParams(vmem_limit_bytes=20 * 2**20),
@@ -662,7 +722,7 @@
             pltpu.VMEM(wind_field.shape, F32),
         ]
         + near_rows
-        + [pltpu.SemaphoreType.DMA((2 * sz.bands + 3,))],
+        + [pltpu.SemaphoreType.DMA((5,))],
         name="pack",
     )(stay(table), stay(energy), stay(nest), stay(ocean_mask), stay(wind_field))
     from_e = lax.ppermute(thick, "grid", down)
@@ -685,24 +745,30 @@
     )(*rim)
     nest, raw_a = lax.optimization_barrier((nest, raw_a))
     nest_inner = kernel_call(functools.partial(nest_kernel, sz), field, 2, flops=3 * 10**10, name="nest")(nest, nest_moves)
-    from_e, from_w, recv_raw_a, recv_raw_b, mix, nest_inner = lax.optimization_barrier(
-        (from_e, from_w, recv_raw_a, recv_raw_b, mix, nest_inner)
-    )
-
-    adv, side, msg_a, msg_b, part = kernel_call(
-        functools.partial(advect_kernel, sz),
-        (field, array(sz.bands * sz.side), half(sz.fix_rows), half(sz.fix_rows + 16), array(VREG)),
-        6,
-        scratch=near_rows
-        + [
-            vmem(sz.rows),
-            vmem(sz.bands * sz.side),
-            vmem(2, VREG),
-            vmem(sz.fix_rows),
-        ],
-        name="advect",
-    )(energy, from_w, from_e, moves, s_moves, sea)
-
+    energy, raw_a = lax.optimization_barrier((energy, raw_a))
+    adv, total = kernel_call(
+        functools.partial(local_kernel, sz), (field, array(VREG)), 3, flops=3 * 10**10, name="local"
+    )(energy, moves, sea)
+    from_e, from_w, mix, nest_inner, adv = lax.optimization_barrier((from_e, from_w, mix, nest_inner, adv))
+
+    msg_b = kernel_call(
+        functools.partial(pass_kernel, sz),
+        half(sz.pass_rows),
+        2,
+        scratch=near_rows + [vmem(sz.pass_rows)],
+        name="pass",
+    )(from_w, from_e)
+    adv, side, msg_a, part = kernel_call(
+        functools.partial(edge_kernel, sz),
+        (field, array(sz.bands * sz.side), half(sz.fix_rows), array(VREG)),
+        8,
+        scratch=near_rows + [vmem(sz.bands * sz.side), vmem(sz.fix_rows)],
+        aliases={0: 0},
+        flops=3 * 10**10,
+        name="edges",
+    )(adv, total, energy, from_w, from_e, moves, s_moves, sea)
+
+    msg_a, msg_b, recv_raw_a, recv_raw_b = lax.optimization_barrier((msg_a, msg_b, recv_raw_a, recv_raw_b))
     recv_a = lax.ppermute(msg_a, "spec", pairs)
     recv_b = lax.ppermute(msg_b, "spec", across)
     pieces = recv_a[sz.sum_row : sz.sum_row + 3 * VREG].astype(F32)
@@ -733,9 +799,9 @@
         array(centres, sz.frame),
         array(centres, sz.frame),
     )
-    inner = kernel_call(
+    *inner, far_near = kernel_call(
         functools.partial(inner_kernel, sz),
-        arrays,
+        arrays + (array(reach * sz.side),),
         7,
         scratch=[vmem(sz.edge_rows), vmem(sz.fix_rows)],
         name="inner",
@@ -744,14 +810,22 @@
     global_next, msg, *_ = kernel_call(
         functools.partial(source_kernel, sz),
         (field, jax.ShapeDtypeStruct((sz.slots, sz.lanes), BF16)) + arrays,
-        9 + len(arrays),
-        scratch=[vmem(sz.bins + VREG), vmem(sz.fix_rows + 16)],
-        aliases={9 + i: 2 + i for i in range(len(arrays))},
+        12 + len(arrays),
+        scratch=[vmem(sz.bins + VREG), vmem(sz.pass_rows), vmem(reach * sz.side), vmem(sz.rows), pltpu.SemaphoreType.DMA((sz.bands,))],
+        out_hbm=(0,),
+        aliases={12 + i: 2 + i for i in range(len(arrays))},
         name="sources",
-    )(adv, side, recv_b, pair, other, gain, s_moves, from_e, mix, *inner)
+    )(adv, side, recv_b, pair, other, gain, moves, s_moves, sea, from_e, mix, far_near, *inner)
 
     recv = lax.all_to_all(msg, "grid", split_axis=0, concat_axis=0, tiled=True)
-    nest_next = kernel_call(functools.partial(blend_kernel, sz), field, 2, name="blend")(recv, nest_adv)
+    nest_next = kernel_call(
+        functools.partial(blend_kernel, sz),
+        field,
+        2,
+        out_hbm=(0,),
+        scratch=[vmem(sz.rows), pltpu.SemaphoreType.DMA((sz.lanes // 128,))],
+        name="blend",
+    )(recv, nest_adv)
     full = (sz.bands, sz.angles, sz.cols, sz.lat)
     return global_next.reshape(full), nest_next.reshape(full)
 

time: 36.5 us -> 35.1 us (0.962)
  starting transfers between devices: 14.6 us -> 13.3 us
    ppermute x1, starting transfers between devices: 1.86 us -> 0.56 us  [per_device(): recv_a = lax.ppermute(msg_a, 'spec', pairs)]
    pallas_call x3 -> x5, Pallas kernels: 4.2 us -> 4.21 us  [the longest x1 1.74 us: per_device(): kernel_call(functools.partial(inner_kernel, sz), arrays + (array(reach *...]
  transfers between devices with their start and end apart: 7 -> 7, of which waited for: 2 -> 2; matrix products, arithmetic and copies ran while one was open for 0% -> 0% of each run, Pallas kernels for 8% -> 12%
where the time goes in v3:
time: 35.1 us; the launch traced here: 34.9 us
  starting transfers between devices  13.3 us (38%)
  blocking collectives  11.3 us (32%)
  Pallas kernels  8.71 us (25%)
  between operations  0.81 us (2%)
  waiting for transfers between devices  0.7 us (2%)
    all_to_all x1, blocking collectives, per_device(): recv = lax.all_to_all(msg, 'grid', split_axis=0, concat_axis=0, tiled=True)  11.3 us
    ppermute x1, starting transfers between devices, per_device(): from_e = lax.ppermute(thick, 'grid', down)  3.1 us
    ppermute x1, starting transfers between devices, per_device(): from_w = lax.ppermute(thin, 'grid', up)  3.02 us
    ppermute x1, starting transfers between devices, per_device(): recv_raw_a = lax.ppermute(raw_a, 'spec', pairs)  3.01 us
    pallas_call x1, Pallas kernels, per_device(): kernel_call(functools.partial(inner_kernel, sz), arrays + (array(reach *...  1.74 us
    ppermute x1, starting transfers between devices, per_device(): recv_b = lax.ppermute(msg_b, 'spec', across)  1.73 us
    pallas_call x1, Pallas kernels, per_device(): kernel_call(functools.partial(source_kernel, sz), (field, jax.ShapeDtypeS...  1.63 us
    pallas_call x1, Pallas kernels, per_device(): kernel_call(functools.partial(pack_kernel, sz), (half(sz.thin_rows), half...  1.56 us
  transfers between devices with their start and end apart: 7, of which 2 were waited for; matrix products, arithmetic and copies ran while one was open for 0% of the time, Pallas kernels for 12%

profile of v3, /device:TPU:0, one launch (start us, length us, event | category | flops | bytes accessed | tf_op | source)
XLA Modules:
  0.0 34.9 jit_solution(11729098556160304789)
XLA Ops:
  0.6 0.0 copy-start.1
  0.6 0.0 copy-start
  0.7 1.6 %pack.1 = (bf16[336,128]{1,0:T(8,128)(2,1)S(1)}, bf16[688,128]{1,0:T(8,128)(2,1)S(1)}, f32[3,144,128]{2,1,0:T(8,128)S(1)}, f32[3,144,128]{2,1,0:T(8,128)S(1)}, f...) custom-call(f32[192,128]{1,0:T(8,128)} %constant.4.clone.table, f32[1296,128]{1,0:T(8,128)} %bitcast.15, ...), custom_call_target="tpu_custom_call" | custom-call | tf_op jit(solution)/shard_map/pack/pallas_call | solution.py:704
  2.2 3.0 %collective-permute-start.1 = (bf16[336,128]{1,0:T(8,128)(2,1)S(1)}, bf16[336,128]{1,0:T(8,128)(2,1)S(1)}, u32[]{:S(2)}, u32[]{:S(2)}) collective-permute-start(bf16[336,128]{1,0:T(8,128)(2,1)S(1)} %get-tuple-element.45), channel_id=1, source_target_pairs={{0,4},{4,8},{8,12},{12,16},{16,20},{20,24},{24,28},{28,0},{1,5},{5... | collective-permute-start | bytes 258056 | tf_op jit(solution)/shard_map/ppermute | solution.py:729
  5.2 3.1 %collective-permute-start = (bf16[688,128]{1,0:T(8,128)(2,1)S(1)}, bf16[688,128]{1,0:T(8,128)(2,1)S(1)}, u32[]{:S(2)}, u32[]{:S(2)}) collective-permute-start(bf16[688,128]{1,0:T(8,128)(2,1)S(1)} %get-tuple-element.44), channel_id=1, source_target_pairs={{4,0},{8,4},{12,8},{16,12},{20,16},{24,20},{28,24},{0,28},{5,1},{9... | collective-permute-start | bytes 528392 | tf_op jit(solution)/shard_map/ppermute | solution.py:728
  8.3 0.0 copy-done
  8.4 0.7 %collective-permute-start.3 = (bf16[720,128]{1,0:T(8,128)(2,1)S(1)}, bf16[720,128]{1,0:T(8,128)(2,1)S(1)}, u32[]{:S(2)}, u32[]{:S(2)}) collective-permute-start(bf16[720,128]{1,0:T(8,128)(2,1)S(1)} %get-tuple-element.66), channel_id=1, source_target_pairs={{1,2},{2,1},{5,6},{6,5},{9,10},{10,9},{13,14},{14,13},{17,18},{18,... | collective-permute-start | bytes 552968 | tf_op jit(solution)/shard_map/ppermute | solution.py:736
  9.1 3.0 %collective-permute-start.2 = (bf16[720,128]{1,0:T(8,128)(2,1)S(1)}, bf16[720,128]{1,0:T(8,128)(2,1)S(1)}, u32[]{:S(2)}, u32[]{:S(2)}) collective-permute-start(bf16[720,128]{1,0:T(8,128)(2,1)S(1)} %get-tuple-element.48), channel_id=1, source_target_pairs={{0,1},{1,0},{2,3},{3,2},{4,5},{5,4},{6,7},{7,6},{8,9},{9,8},{10,11... | collective-permute-start | bytes 552968 | tf_op jit(solution)/shard_map/ppermute | solution.py:737
  12.1 0.0 copy-done.1
  12.1 0.8 %nest.1.inner = f32[1296,128]{1,0:T(8,128)S(1)} custom-call(f32[1296,128]{1,0:T(8,128)S(1)} %bitcast.21, f32[3,144,128]{2,1,0:T(8,128)S(1)} %get-tuple-element.53.moves), custom_call_target="tpu_custom_call" | custom-call | flops 30000001024 | tf_op jit(solution)/shard_map/nest/pallas_call | solution.py:747
  12.9 0.0 copy-start.2
  12.9 0.0 copy-start.3
  12.9 0.0 copy-start.4
  12.9 0.0 copy-start.5
  13.0 0.9 %local.1 = (f32[1296,128]{1,0:T(8,128)S(1)}, f32[8,128]{1,0:T(8,128)S(1)}) custom-call(f32[1296,128]{1,0:T(8,128)S(1)} %bitcast.17, f32[3,144,128]{2,1,0:T(8,128)S(1)} %get-tuple-element.54.moves, f32[8,128]{1,0:T(8,128)S(1)} %get-tuple-element.55.sea), custom_call_target="tpu_custom_call" | custom-call | flops 30000001024 | tf_op jit(solution)/shard_map/local/pallas_call | solution.py:749
  13.8 0.0 copy-done.2
  13.9 0.0 copy-done.3
  13.9 0.0 copy-done.4
  13.9 0.0 copy-done.5
  13.9 0.4 %rim.1.mix = bf16[256,768]{1,0:T(8,128)(2,1)S(1)} custom-call(s32[2,128]{1,0:T(2,128)S(1)} %bitcast.24, s32[1,128]{1,0:T(1,128)S(1)} %bitcast.25, s32[1,128]{1,0:T(1,128)S(1)} %bitcast.26, f32[3,128]{1,0:T(4,128)S(1)} %bitcast.23), custom_call_target="tpu_custom_call" | custom-call | tf_op jit(solution)/shard_map/rim/pallas_call | solution.py:740
  14.3 0.0 collective-permute-done.1.from_w
  14.3 0.0 collective-permute-done.from_e
  14.3 0.3 edges.1
  14.6 0.1 pass.1
  14.6 0.0 collective-permute-done.3.raw_b
  14.7 0.0 collective-permute-done.2.raw_a
  14.7 0.6 %collective-permute-start.5 = (bf16[384,128]{1,0:T(8,128)(2,1)S(1)}, bf16[384,128]{1,0:T(8,128)(2,1)S(1)}, u32[]{:S(2)}, u32[]{:S(2)}) collective-permute-start(bf16[384,128]{1,0:T(8,128)(2,1)S(1)} %get-tuple-element.70), channel_id=1, source_target_pairs={{0,1},{1,0},{2,3},{3,2},{4,5},{5,4},{6,7},{7,6},{8,9},{9,8},{10,11... | collective-permute-start | bytes 294920 | tf_op jit(solution)/shard_map/ppermute | solution.py:772
  15.2 1.7 %collective-permute-start.4 = (bf16[400,128]{1,0:T(8,128)(2,1)S(1)}, bf16[400,128]{1,0:T(8,128)(2,1)S(1)}, u32[]{:S(2)}, u32[]{:S(2)}) collective-permute-start(bf16[400,128]{1,0:T(8,128)(2,1)S(1)} %pass.1), channel_id=1, source_target_pairs={{0,3},{1,2},{2,1},{3,0},{4,7},{5,6},{6,5},{7,4},{8,11},{9,10},{10,... | collective-permute-start | bytes 307208 | tf_op jit(solution)/shard_map/ppermute | solution.py:773
  17.0 0.0 collective-permute-done.5.recv_a
  17.0 1.2 %collective-permute-start.6 = (f32[8,128]{1,0:T(8,128)S(1)}, f32[8,128]{1,0:T(8,128)S(1)}, u32[]{:S(2)}, u32[]{:S(2)}) collective-permute-start(f32[8,128]{1,0:T(8,128)S(1)} %add.3.pair), channel_id=1, source_target_pairs={{0,2},{1,3},{2,0},{3,1},{4,6},{5,7},{6,4},{7,5},{8,10},{9,11},{10,... | collective-permute-start | bytes 12296 | tf_op jit(solution)/shard_map/ppermute | solution.py:780
  18.2 0.1 nest_edge.1.nest_adv
  18.2 1.7 %inner.1 = (f32[19,144,128]{2,1,0:T(8,128)S(1)}, f32[19,168,128]{2,1,0:T(8,128)S(1)}, f32[14,168,128]{2,1,0:T(8,128)S(1)}, f32[14,168,128]{2,1,0:T(8,128)S(1)}, ...) custom-call(f32[1296,128]{1,0:T(8,128)S(1)} %get-tuple-element.62.ad, ...), custom_call_target="tpu_custom_call" | custom-call | tf_op jit(solution)/shard_map/inner/pallas_call | solution.py:802
  20.0 0.2 collective-permute-done.4.recv_b
  20.2 0.4 %collective-permute-done.6.other = f32[8,128]{1,0:T(8,128)S(1)} collective-permute-done((f32[8,128]{1,0:T(8,128)S(1)}, f32[8,128]{1,0:T(8,128)S(1)}, u32[]{:S(2)}, u32[]{:S(2)}) %collective-permute-start.6) | collective-permute-done | bytes 4128 | tf_op jit(solution)/shard_map/ppermute | solution.py:780
  20.6 1.6 %sources.1 = (f32[1296,128]{1,0:T(8,128)}, bf16[256,384]{1,0:T(8,128)(2,1)S(1)}, f32[19,144,128]{2,1,0:T(8,128)S(1)}, f32[19,168,128]{2,1,0:T(8,128)S(1)}, f32[1...) custom-call(f32[1296,128]{1,0:T(8,128)S(1)} %get-tuple-element.62.ad, ...), custom_call_target="tpu_custom_call", output_to_operand_aliasing={{2}: (12, {}), {3}: (13, {}), {4}: (14, {}), {5}: (15, {}),... | custom-call | tf_op jit(solution)/shard_map/sources/pallas_call | solution.py:810
  22.3 11.3 %all_to_all.11 = bf16[8,32,384]{2,1,0:T(8,128)(2,1)S(1)} all-to-all(bf16[8,32,384]{2,1,0:T(8,128)(2,1)S(1)} %bitcast.22), channel_id=1, replica_groups=mesh['grid'=8,'spec'=4] {'grid'}, dimensions={0} | all-to-all | bytes 393216 | tf_op jit(solution)/shard_map/all_to_all | solution.py:820
  33.6 1.3 %blend.1 = f32[1296,128]{1,0:T(8,128)} custom-call(bf16[256,384]{1,0:T(8,128)(2,1)S(1)} %bitcast.19, f32[1296,128]{1,0:T(8,128)S(1)} %nest_edge.1.nest_adv), custom_call_target="tpu_custom_call" | custom-call | tf_op jit(solution)/shard_map/blend/pallas_call | solution.py:821
  (3 shorter events, 0.0 us)
Async XLA Ops:
  0.6 11.4 %copy-start.1 = (f32[9,36,4,128]{3,2,1,0:T(4,128)S(1)}, f32[9,36,4,128]{3,2,1,0:T(4,128)}, u32[]{:S(2)}) copy-start(f32[9,36,4,128]{3,2,1,0:T(4,128)} %param.10) | copy-start | bytes 1990660
  0.6 7.7 %copy-start = (f32[9,36,4,128]{3,2,1,0:T(4,128)S(1)}, f32[9,36,4,128]{3,2,1,0:T(4,128)}, u32[]{:S(2)}) copy-start(f32[9,36,4,128]{3,2,1,0:T(4,128)} %param.9) | copy-start | bytes 1990660
  2.2 12.1 %collective-permute-start.1 = (bf16[336,128]{1,0:T(8,128)(2,1)S(1)}, bf16[336,128]{1,0:T(8,128)(2,1)S(1)}, u32[]{:S(2)}, u32[]{:S(2)}) collective-permute-start(bf16[336,128]{1,0:T(8,128)(2,1)S(1)} %get-tuple-element.45), channel_id=1, source_target_pairs={{0,4},{4,8},{8,12},{12,16},{16,20},{20,24},{24,28},{28,0},{1,5},{5... | collective-permute-start | bytes 258056 | tf_op jit(solution)/shard_map/ppermute | solution.py:729
  5.2 9.1 %collective-permute-start = (bf16[688,128]{1,0:T(8,128)(2,1)S(1)}, bf16[688,128]{1,0:T(8,128)(2,1)S(1)}, u32[]{:S(2)}, u32[]{:S(2)}) collective-permute-start(bf16[688,128]{1,0:T(8,128)(2,1)S(1)} %get-tuple-element.44), channel_id=1, source_target_pairs={{4,0},{8,4},{12,8},{16,12},{20,16},{24,20},{28,24},{0,28},{5,1},{9... | collective-permute-start | bytes 528392 | tf_op jit(solution)/shard_map/ppermute | solution.py:728
  8.4 6.3 %collective-permute-start.3 = (bf16[720,128]{1,0:T(8,128)(2,1)S(1)}, bf16[720,128]{1,0:T(8,128)(2,1)S(1)}, u32[]{:S(2)}, u32[]{:S(2)}) collective-permute-start(bf16[720,128]{1,0:T(8,128)(2,1)S(1)} %get-tuple-element.66), channel_id=1, source_target_pairs={{1,2},{2,1},{5,6},{6,5},{9,10},{10,9},{13,14},{14,13},{17,18},{18,... | collective-permute-start | bytes 552968 | tf_op jit(solution)/shard_map/ppermute | solution.py:736
  9.1 5.6 %collective-permute-start.2 = (bf16[720,128]{1,0:T(8,128)(2,1)S(1)}, bf16[720,128]{1,0:T(8,128)(2,1)S(1)}, u32[]{:S(2)}, u32[]{:S(2)}) collective-permute-start(bf16[720,128]{1,0:T(8,128)(2,1)S(1)} %get-tuple-element.48), channel_id=1, source_target_pairs={{0,1},{1,0},{2,3},{3,2},{4,5},{5,4},{6,7},{7,6},{8,9},{9,8},{10,11... | collective-permute-start | bytes 552968 | tf_op jit(solution)/shard_map/ppermute | solution.py:737
  12.9 0.9 %copy-start.2 = (f32[128,3]{0,1:T(4,128)S(1)}, f32[128,3]{0,1:T(4,128)}, u32[]{:S(2)}) copy-start(f32[128,3]{0,1:T(4,128)} %param.16) | copy-start | bytes 4612
  12.9 0.9 %copy-start.3 = (s32[128,2]{0,1:T(2,128)S(1)}, s32[128,2]{0,1:T(2,128)}, u32[]{:S(2)}) copy-start(s32[128,2]{0,1:T(2,128)} %param.13) | copy-start | bytes 3076
  12.9 0.9 %copy-start.4 = (s32[128,1]{0,1:T(1,128)S(1)}, s32[128,1]{0,1:T(1,128)}, u32[]{:S(2)}) copy-start(s32[128,1]{0,1:T(1,128)} %param.14) | copy-start | bytes 1540
  12.9 0.9 %copy-start.5 = (s32[128]{0:T(128)S(1)}, s32[128]{0:T(128)}, u32[]{:S(2)}) copy-start(s32[128]{0:T(128)} %param.15) | copy-start | bytes 1540
  14.7 2.3 %collective-permute-start.5 = (bf16[384,128]{1,0:T(8,128)(2,1)S(1)}, bf16[384,128]{1,0:T(8,128)(2,1)S(1)}, u32[]{:S(2)}, u32[]{:S(2)}) collective-permute-start(bf16[384,128]{1,0:T(8,128)(2,1)S(1)} %get-tuple-element.70), channel_id=1, source_target_pairs={{0,1},{1,0},{2,3},{3,2},{4,5},{5,4},{6,7},{7,6},{8,9},{9,8},{10,11... | collective-permute-start | bytes 294920 | tf_op jit(solution)/shard_map/ppermute | solution.py:772
  15.2 5.0 %collective-permute-start.4 = (bf16[400,128]{1,0:T(8,128)(2,1)S(1)}, bf16[400,128]{1,0:T(8,128)(2,1)S(1)}, u32[]{:S(2)}, u32[]{:S(2)}) collective-permute-start(bf16[400,128]{1,0:T(8,128)(2,1)S(1)} %pass.1), channel_id=1, source_target_pairs={{0,3},{1,2},{2,1},{3,0},{4,7},{5,6},{6,5},{7,4},{8,11},{9,10},{10,... | collective-permute-start | bytes 307208 | tf_op jit(solution)/shard_map/ppermute | solution.py:773
  17.0 3.7 %collective-permute-start.6 = (f32[8,128]{1,0:T(8,128)S(1)}, f32[8,128]{1,0:T(8,128)S(1)}, u32[]{:S(2)}, u32[]{:S(2)}) collective-permute-start(f32[8,128]{1,0:T(8,128)S(1)} %add.3.pair), channel_id=1, source_target_pairs={{0,2},{1,3},{2,0},{3,1},{4,6},{5,7},{6,4},{7,5},{8,10},{9,11},{10,... | collective-permute-start | bytes 12296 | tf_op jit(solution)/shard_map/ppermute | solution.py:780

commit v4 on v3

--- a/solution.py
+++ b/solution.py
@@ -697,7 +697,13 @@
     nest = nest_energy.reshape(sz.rows, sz.lat)
     up = [(i, (i + 1) % sz.grid) for i in range(sz.grid)]
     down = [(j, i) for i, j in up]
-    across = [(i, (i + 1 if i % 2 else i - 1) % sz.spec) for i in range(sz.spec)]
+    across = []
+    for g in range(sz.grid):
+        for i in range(sz.spec):
+            j = i + 1 if i % 2 else i - 1
+            to = (g, j) if 0 <= j < sz.spec else ((g ^ 1) % sz.grid, i)
+            across.append((g * sz.spec + i, to[0] * sz.spec + to[1]))
+    both = ("grid", "spec")
     near_rows = [vmem(sz.thin_rows), vmem(sz.thick_rows)]
 
     stay = functools.partial(pltpu.with_memory_space_constraint, memory_space=pltpu.HBM)
@@ -733,7 +739,7 @@
         functools.partial(raw_kernel, sz), (half(sz.edge_rows), half(sz.edge_rows)), 1, name="raw"
     )(energy)
     pairs = [(i, i ^ 1) for i in range(sz.spec)]
-    recv_raw_b = lax.ppermute(raw_b, "spec", [(i, j) for i, j in across if abs(i - j) == 1])
+    recv_raw_b = lax.ppermute(raw_b, "spec", [(i, (i + 1 if i % 2 else i - 1) % sz.spec) for i in range(sz.spec)])
     recv_raw_a = lax.ppermute(raw_a, "spec", pairs)
     rim = (rim_cell.T, rim_dest.T, rim_target.reshape(1, sz.rim), rim_weight.T)
     rim, raw_a = lax.optimization_barrier((rim, raw_a))
@@ -770,14 +776,14 @@
 
     msg_a, msg_b, recv_raw_a, recv_raw_b = lax.optimization_barrier((msg_a, msg_b, recv_raw_a, recv_raw_b))
     recv_a = lax.ppermute(msg_a, "spec", pairs)
-    recv_b = lax.ppermute(msg_b, "spec", across)
+    recv_b = lax.ppermute(msg_b, both, across)
     pieces = recv_a[sz.sum_row : sz.sum_row + 3 * VREG].astype(F32)
     pair = part + pieces.reshape(3, VREG, sz.lat).sum(axis=0)
     other = jnp.zeros_like(pair)
     step = 2
     while step < sz.spec:
         pair = pair + other
-        other = lax.ppermute(pair, "spec", [(i, i ^ step) for i in range(sz.spec)])
+        other = lax.ppermute(pair, "spec", [(i, i ^ (2 * step - 1)) for i in range(sz.spec)])
         step *= 2
 
     nest_adv = kernel_call(

time: 35.1 us -> 34.8 us (level)
  starting transfers between devices: 13.3 us -> 9.14 us
  waiting for transfers between devices: 0.7 us -> 4.25 us
  blocking collectives: 11.3 us -> 11.7 us
    ppermute x1, starting transfers between devices: 3.01 us -> 1.06 us  [per_device(): recv_raw_a = lax.ppermute(raw_a, 'spec', pairs)]
    ppermute x3, waiting for transfers between devices: 0.69 us -> 2.44 us  [the longest x1 1.91 us: per_device(): lax.ppermute(raw_b, 'spec', [(i, (i + 1 if i % 2 else i - 1) % sz.spec) f...]
    ppermute x3, starting transfers between devices: 3.59 us -> 1.85 us  [the longest x1 1.13 us: per_device(): lax.ppermute(pair, 'spec', [(i, i ^ 2 * step - 1) for i in range(sz.spec)])]
    ppermute x1, waiting for transfers between devices: 0.01 us -> 1.18 us  [per_device(): recv_a = lax.ppermute(msg_a, 'spec', pairs)]
    ppermute x1, waiting for transfers between devices: 0.01 us -> 0.62 us  [per_device(): from_e = lax.ppermute(thick, 'grid', down)]
    ppermute x1, starting transfers between devices: 0.56 us -> 0.12 us  [per_device(): recv_a = lax.ppermute(msg_a, 'spec', pairs)]
  transfers between devices with their start and end apart: 7 -> 7, of which waited for: 2 -> 4; matrix products, arithmetic and copies ran while one was open for 0% -> 0% of each run, Pallas kernels for 12% -> 12%
where the time goes in v4:
time: 34.8 us; the launch traced here: 34.6 us
  blocking collectives  11.7 us (34%)
  starting transfers between devices  9.14 us (26%)
  Pallas kernels  8.71 us (25%)
  waiting for transfers between devices  4.25 us (12%)
  between operations  0.78 us (2%)
    all_to_all x1, blocking collectives, per_device(): recv = lax.all_to_all(msg, 'grid', split_axis=0, concat_axis=0, tiled=True)  11.7 us
    ppermute x1, starting transfers between devices, per_device(): from_e = lax.ppermute(thick, 'grid', down)  3.1 us
    ppermute x1, starting transfers between devices, per_device(): from_w = lax.ppermute(thin, 'grid', up)  3.02 us
    ppermute x1, waiting for transfers between devices, per_device(): lax.ppermute(raw_b, 'spec', [(i, (i + 1 if i % 2 else i - 1) % sz.spec) f...  1.91 us
    pallas_call x1, Pallas kernels, per_device(): kernel_call(functools.partial(inner_kernel, sz), arrays + (array(reach *...  1.74 us
    pallas_call x1, Pallas kernels, per_device(): kernel_call(functools.partial(source_kernel, sz), (field, jax.ShapeDtypeS...  1.63 us
    pallas_call x1, Pallas kernels, per_device(): kernel_call(functools.partial(pack_kernel, sz), (half(sz.thin_rows), half...  1.56 us
    pallas_call x1, Pallas kernels, per_device(): kernel_call(functools.partial(blend_kernel, sz), field, 2, out_hbm=(0,),...  1.26 us
  transfers between devices with their start and end apart: 7, of which 4 were waited for; matrix products, arithmetic and copies ran while one was open for 0% of the time, Pallas kernels for 12%

profile of v4, /device:TPU:0, one launch (start us, length us, event | category | flops | bytes accessed | tf_op | source)
XLA Modules:
  0.0 34.6 jit_solution(3115432684878285617)
XLA Ops:
  0.6 0.0 copy-start.1
  0.6 0.0 copy-start
  0.7 1.6 %pack.1 = (bf16[336,128]{1,0:T(8,128)(2,1)S(1)}, bf16[688,128]{1,0:T(8,128)(2,1)S(1)}, f32[3,144,128]{2,1,0:T(8,128)S(1)}, f32[3,144,128]{2,1,0:T(8,128)S(1)}, f...) custom-call(f32[192,128]{1,0:T(8,128)} %constant.4.clone.table, f32[1296,128]{1,0:T(8,128)} %bitcast.15, ...), custom_call_target="tpu_custom_call" | custom-call | tf_op jit(solution)/shard_map/pack/pallas_call | solution.py:710
  2.2 3.0 %collective-permute-start.1 = (bf16[336,128]{1,0:T(8,128)(2,1)S(1)}, bf16[336,128]{1,0:T(8,128)(2,1)S(1)}, u32[]{:S(2)}, u32[]{:S(2)}) collective-permute-start(bf16[336,128]{1,0:T(8,128)(2,1)S(1)} %get-tuple-element.45), channel_id=1, source_target_pairs={{0,4},{4,8},{8,12},{12,16},{16,20},{20,24},{24,28},{28,0},{1,5},{5... | collective-permute-start | bytes 258056 | tf_op jit(solution)/shard_map/ppermute | solution.py:735
  5.2 3.1 %collective-permute-start = (bf16[688,128]{1,0:T(8,128)(2,1)S(1)}, bf16[688,128]{1,0:T(8,128)(2,1)S(1)}, u32[]{:S(2)}, u32[]{:S(2)}) collective-permute-start(bf16[688,128]{1,0:T(8,128)(2,1)S(1)} %get-tuple-element.44), channel_id=1, source_target_pairs={{4,0},{8,4},{12,8},{16,12},{20,16},{24,20},{28,24},{0,28},{5,1},{9... | collective-permute-start | bytes 528392 | tf_op jit(solution)/shard_map/ppermute | solution.py:734
  8.3 0.0 copy-done
  8.4 0.7 %collective-permute-start.3 = (bf16[720,128]{1,0:T(8,128)(2,1)S(1)}, bf16[720,128]{1,0:T(8,128)(2,1)S(1)}, u32[]{:S(2)}, u32[]{:S(2)}) collective-permute-start(bf16[720,128]{1,0:T(8,128)(2,1)S(1)} %get-tuple-element.66), channel_id=1, source_target_pairs={{0,3},{1,2},{2,1},{3,0},{4,7},{5,6},{6,5},{7,4},{8,11},{9,10},{10,... | collective-permute-start | bytes 552968 | tf_op jit(solution)/shard_map/ppermute | solution.py:742
  9.1 1.1 %collective-permute-start.2 = (bf16[720,128]{1,0:T(8,128)(2,1)S(1)}, bf16[720,128]{1,0:T(8,128)(2,1)S(1)}, u32[]{:S(2)}, u32[]{:S(2)}) collective-permute-start(bf16[720,128]{1,0:T(8,128)(2,1)S(1)} %get-tuple-element.48), channel_id=1, source_target_pairs={{0,1},{1,0},{2,3},{3,2},{4,5},{5,4},{6,7},{7,6},{8,9},{9,8},{10,11... | collective-permute-start | bytes 552968 | tf_op jit(solution)/shard_map/ppermute | solution.py:743
  10.2 0.0 copy-done.1
  10.2 0.8 %nest.1.inner = f32[1296,128]{1,0:T(8,128)S(1)} custom-call(f32[1296,128]{1,0:T(8,128)S(1)} %bitcast.21, f32[3,144,128]{2,1,0:T(8,128)S(1)} %get-tuple-element.53.moves), custom_call_target="tpu_custom_call" | custom-call | flops 30000001024 | tf_op jit(solution)/shard_map/nest/pallas_call | solution.py:753
  11.0 0.0 copy-start.2
  11.0 0.0 copy-start.3
  11.0 0.0 copy-start.4
  11.0 0.0 copy-start.5
  11.0 0.9 %local.1 = (f32[1296,128]{1,0:T(8,128)S(1)}, f32[8,128]{1,0:T(8,128)S(1)}) custom-call(f32[1296,128]{1,0:T(8,128)S(1)} %bitcast.17, f32[3,144,128]{2,1,0:T(8,128)S(1)} %get-tuple-element.54.moves, f32[8,128]{1,0:T(8,128)S(1)} %get-tuple-element.55.sea), custom_call_target="tpu_custom_call" | custom-call | flops 30000001024 | tf_op jit(solution)/shard_map/local/pallas_call | solution.py:755
  11.9 0.0 copy-done.2
  11.9 0.0 copy-done.3
  12.0 0.0 copy-done.4
  12.0 0.0 copy-done.5
  12.0 0.4 %rim.1.mix = bf16[256,768]{1,0:T(8,128)(2,1)S(1)} custom-call(s32[2,128]{1,0:T(2,128)S(1)} %bitcast.24, s32[1,128]{1,0:T(1,128)S(1)} %bitcast.25, s32[1,128]{1,0:T(1,128)S(1)} %bitcast.26, f32[3,128]{1,0:T(4,128)S(1)} %bitcast.23), custom_call_target="tpu_custom_call" | custom-call | tf_op jit(solution)/shard_map/rim/pallas_call | solution.py:746
  12.4 0.0 collective-permute-done.1.from_w
  12.4 0.6 %collective-permute-done.from_e = bf16[688,128]{1,0:T(8,128)(2,1)S(1)} collective-permute-done((bf16[688,128]{1,0:T(8,128)(2,1)S(1)}, bf16[688,128]{1,0:T(8,128)(2,1)S(1)}, u32[]{:S(2)}, u32[]{:S(2)}) %collective-permute-start) | collective-permute-done | bytes 176160 | tf_op jit(solution)/shard_map/ppermute | solution.py:734
  13.0 0.3 edges.1
  13.3 0.1 pass.1
  13.3 1.9 %collective-permute-done.3.raw_b = bf16[720,128]{1,0:T(8,128)(2,1)S(1)} collective-permute-done((bf16[720,128]{1,0:T(8,128)(2,1)S(1)}, bf16[720,128]{1,0:T(8,128)(2,1)S(1)}, u32[]{:S(2)}, u32[]{:S(2)}) %collective-permute-start.3) | collective-permute-done | bytes 184352 | tf_op jit(solution)/shard_map/ppermute | solution.py:742
  15.2 0.0 collective-permute-done.2.raw_a
  15.2 0.1 collective-permute-start.5
  15.4 0.0 collective-permute-start.4
  15.4 1.2 %collective-permute-done.5.recv_a = bf16[384,128]{1,0:T(8,128)(2,1)S(1)} collective-permute-done((bf16[384,128]{1,0:T(8,128)(2,1)S(1)}, bf16[384,128]{1,0:T(8,128)(2,1)S(1)}, u32[]{:S(2)}, u32[]{:S(2)}) %collective-permute-start.5) | collective-permute-done | bytes 98336 | tf_op jit(solution)/shard_map/ppermute | solution.py:778
  16.6 1.1 %collective-permute-start.6 = (f32[8,128]{1,0:T(8,128)S(1)}, f32[8,128]{1,0:T(8,128)S(1)}, u32[]{:S(2)}, u32[]{:S(2)}) collective-permute-start(f32[8,128]{1,0:T(8,128)S(1)} %add.3.pair), channel_id=1, source_target_pairs={{0,3},{1,2},{2,1},{3,0},{4,7},{5,6},{6,5},{7,4},{8,11},{9,10},{10,... | collective-permute-start | bytes 12296 | tf_op jit(solution)/shard_map/ppermute | solution.py:786
  17.7 0.1 nest_edge.1.nest_adv
  17.8 1.7 %inner.1 = (f32[19,144,128]{2,1,0:T(8,128)S(1)}, f32[19,168,128]{2,1,0:T(8,128)S(1)}, f32[14,168,128]{2,1,0:T(8,128)S(1)}, f32[14,168,128]{2,1,0:T(8,128)S(1)}, ...) custom-call(f32[1296,128]{1,0:T(8,128)S(1)} %get-tuple-element.62.ad, ...), custom_call_target="tpu_custom_call" | custom-call | tf_op jit(solution)/shard_map/inner/pallas_call | solution.py:808
  19.5 0.5 %collective-permute-done.4.recv_b = bf16[400,128]{1,0:T(8,128)(2,1)S(1)} collective-permute-done((bf16[400,128]{1,0:T(8,128)(2,1)S(1)}, bf16[400,128]{1,0:T(8,128)(2,1)S(1)}, u32[]{:S(2)}, u32[]{:S(2)}) %collective-permute-start.4) | collective-permute-done | bytes 102432 | tf_op jit(solution)/shard_map/ppermute | solution.py:779
  20.0 0.0 collective-permute-done.6.other
  20.0 1.6 %sources.1 = (f32[1296,128]{1,0:T(8,128)}, bf16[256,384]{1,0:T(8,128)(2,1)S(1)}, f32[19,144,128]{2,1,0:T(8,128)S(1)}, f32[19,168,128]{2,1,0:T(8,128)S(1)}, f32[1...) custom-call(f32[1296,128]{1,0:T(8,128)S(1)} %get-tuple-element.62.ad, ...), custom_call_target="tpu_custom_call", output_to_operand_aliasing={{2}: (12, {}), {3}: (13, {}), {4}: (14, {}), {5}: (15, {}),... | custom-call | tf_op jit(solution)/shard_map/sources/pallas_call | solution.py:816
  21.7 11.7 %all_to_all.11 = bf16[8,32,384]{2,1,0:T(8,128)(2,1)S(1)} all-to-all(bf16[8,32,384]{2,1,0:T(8,128)(2,1)S(1)} %bitcast.22), channel_id=1, replica_groups=mesh['grid'=8,'spec'=4] {'grid'}, dimensions={0} | all-to-all | bytes 393216 | tf_op jit(solution)/shard_map/all_to_all | solution.py:826
  33.4 1.3 %blend.1 = f32[1296,128]{1,0:T(8,128)} custom-call(bf16[256,384]{1,0:T(8,128)(2,1)S(1)} %bitcast.19, f32[1296,128]{1,0:T(8,128)S(1)} %nest_edge.1.nest_adv), custom_call_target="tpu_custom_call" | custom-call | tf_op jit(solution)/shard_map/blend/pallas_call | solution.py:827
  (3 shorter events, 0.0 us)
Async XLA Ops:
  0.6 9.5 %copy-start.1 = (f32[9,36,4,128]{3,2,1,0:T(4,128)S(1)}, f32[9,36,4,128]{3,2,1,0:T(4,128)}, u32[]{:S(2)}) copy-start(f32[9,36,4,128]{3,2,1,0:T(4,128)} %param.10) | copy-start | bytes 1990660
  0.6 7.7 %copy-start = (f32[9,36,4,128]{3,2,1,0:T(4,128)S(1)}, f32[9,36,4,128]{3,2,1,0:T(4,128)}, u32[]{:S(2)}) copy-start(f32[9,36,4,128]{3,2,1,0:T(4,128)} %param.9) | copy-start | bytes 1990660
  2.2 10.2 %collective-permute-start.1 = (bf16[336,128]{1,0:T(8,128)(2,1)S(1)}, bf16[336,128]{1,0:T(8,128)(2,1)S(1)}, u32[]{:S(2)}, u32[]{:S(2)}) collective-permute-start(bf16[336,128]{1,0:T(8,128)(2,1)S(1)} %get-tuple-element.45), channel_id=1, source_target_pairs={{0,4},{4,8},{8,12},{12,16},{16,20},{20,24},{24,28},{28,0},{1,5},{5... | collective-permute-start | bytes 258056 | tf_op jit(solution)/shard_map/ppermute | solution.py:735
  5.2 7.8 %collective-permute-start = (bf16[688,128]{1,0:T(8,128)(2,1)S(1)}, bf16[688,128]{1,0:T(8,128)(2,1)S(1)}, u32[]{:S(2)}, u32[]{:S(2)}) collective-permute-start(bf16[688,128]{1,0:T(8,128)(2,1)S(1)} %get-tuple-element.44), channel_id=1, source_target_pairs={{4,0},{8,4},{12,8},{16,12},{20,16},{24,20},{28,24},{0,28},{5,1},{9... | collective-permute-start | bytes 528392 | tf_op jit(solution)/shard_map/ppermute | solution.py:734
  8.4 6.9 %collective-permute-start.3 = (bf16[720,128]{1,0:T(8,128)(2,1)S(1)}, bf16[720,128]{1,0:T(8,128)(2,1)S(1)}, u32[]{:S(2)}, u32[]{:S(2)}) collective-permute-start(bf16[720,128]{1,0:T(8,128)(2,1)S(1)} %get-tuple-element.66), channel_id=1, source_target_pairs={{0,3},{1,2},{2,1},{3,0},{4,7},{5,6},{6,5},{7,4},{8,11},{9,10},{10,... | collective-permute-start | bytes 552968 | tf_op jit(solution)/shard_map/ppermute | solution.py:742
  9.1 6.1 %collective-permute-start.2 = (bf16[720,128]{1,0:T(8,128)(2,1)S(1)}, bf16[720,128]{1,0:T(8,128)(2,1)S(1)}, u32[]{:S(2)}, u32[]{:S(2)}) collective-permute-start(bf16[720,128]{1,0:T(8,128)(2,1)S(1)} %get-tuple-element.48), channel_id=1, source_target_pairs={{0,1},{1,0},{2,3},{3,2},{4,5},{5,4},{6,7},{7,6},{8,9},{9,8},{10,11... | collective-permute-start | bytes 552968 | tf_op jit(solution)/shard_map/ppermute | solution.py:743
  11.0 0.9 %copy-start.2 = (f32[128,3]{0,1:T(4,128)S(1)}, f32[128,3]{0,1:T(4,128)}, u32[]{:S(2)}) copy-start(f32[128,3]{0,1:T(4,128)} %param.16) | copy-start | bytes 4612
  11.0 0.9 %copy-start.3 = (s32[128,2]{0,1:T(2,128)S(1)}, s32[128,2]{0,1:T(2,128)}, u32[]{:S(2)}) copy-start(s32[128,2]{0,1:T(2,128)} %param.13) | copy-start | bytes 3076
  11.0 0.9 %copy-start.4 = (s32[128,1]{0,1:T(1,128)S(1)}, s32[128,1]{0,1:T(1,128)}, u32[]{:S(2)}) copy-start(s32[128,1]{0,1:T(1,128)} %param.14) | copy-start | bytes 1540
  11.0 0.9 %copy-start.5 = (s32[128]{0:T(128)S(1)}, s32[128]{0:T(128)}, u32[]{:S(2)}) copy-start(s32[128]{0:T(128)} %param.15) | copy-start | bytes 1540
  15.2 1.3 %collective-permute-start.5 = (bf16[384,128]{1,0:T(8,128)(2,1)S(1)}, bf16[384,128]{1,0:T(8,128)(2,1)S(1)}, u32[]{:S(2)}, u32[]{:S(2)}) collective-permute-start(bf16[384,128]{1,0:T(8,128)(2,1)S(1)} %get-tuple-element.70), channel_id=1, source_target_pairs={{0,1},{1,0},{2,3},{3,2},{4,5},{5,4},{6,7},{7,6},{8,9},{9,8},{10,11... | collective-permute-start | bytes 294920 | tf_op jit(solution)/shard_map/ppermute | solution.py:778
  15.4 4.7 %collective-permute-start.4 = (bf16[400,128]{1,0:T(8,128)(2,1)S(1)}, bf16[400,128]{1,0:T(8,128)(2,1)S(1)}, u32[]{:S(2)}, u32[]{:S(2)}) collective-permute-start(bf16[400,128]{1,0:T(8,128)(2,1)S(1)} %pass.1), channel_id=1, source_target_pairs={{0,4},{1,2},{2,1},{3,7},{4,0},{5,6},{6,5},{7,3},{8,12},{9,10},{10,... | collective-permute-start | bytes 307208 | tf_op jit(solution)/shard_map/ppermute | solution.py:779
  16.6 3.5 %collective-permute-start.6 = (f32[8,128]{1,0:T(8,128)S(1)}, f32[8,128]{1,0:T(8,128)S(1)}, u32[]{:S(2)}, u32[]{:S(2)}) collective-permute-start(f32[8,128]{1,0:T(8,128)S(1)} %add.3.pair), channel_id=1, source_target_pairs={{0,3},{1,2},{2,1},{3,0},{4,7},{5,6},{6,5},{7,4},{8,11},{9,10},{10,... | collective-permute-start | bytes 12296 | tf_op jit(solution)/shard_map/ppermute | solution.py:786

commit v5 on v4

--- a/solution.py
+++ b/solution.py
@@ -41,7 +41,7 @@
         self.frame = self.side + 2 * VREG
         self.thin = self.bands * self.half
         self.thin_rows = (2 * self.thin + 15) // 16 * 16
-        self.thick = (self.angles + self.half + VREG - 1) // VREG * VREG
+        self.thick = self.angles + self.half
         self.info = self.bands * self.thick
         self.thick_nest = (self.info + 7 + VREG - 1) // VREG * VREG
         self.thick_rows = (self.thick_nest + self.thin + 15) // 16 * 16
@@ -122,62 +122,66 @@
 
 
 def pack_kernel(
-    sz, table, energy, nest, mask, wind,
-    thin, thick, moves, nest_moves, s_moves, gain, sea,
-    table_v, field, nest_field, mask_v, wind_v, tmp_thin, tmp_thick, sems,
+    sz, energy, nest, mask, wind, thin, thick, first, second, first_n, late, early, late_n, early_n,
+    mask_v, wind_v, tmp_thin, tmp_thick, sems,
 ):
-    pairs = [(table, table_v), (mask, mask_v), (wind, wind_v), (energy, field), (nest, nest_field)]
+    from_east = pl.ds(sz.quarter, sz.half)
+    (start, count), (_, rest) = west_half(sz)
+    last = sz.cols - 1
+    pairs = [
+        (mask, mask_v),
+        (wind, wind_v),
+        (energy.at[:, :, 0], first),
+        (energy.at[:, from_east, 1], second),
+        (energy.at[:, pl.ds(start, count), last], late),
+        (energy.at[:, pl.ds(0, rest), last], early),
+        (nest.at[:, from_east, 0], first_n),
+        (nest.at[:, pl.ds(start, count), last], late_n),
+        (nest.at[:, pl.ds(0, rest), last], early_n),
+    ]
     copies = [pltpu.make_async_copy(a, b, sems.at[i]) for i, (a, b) in enumerate(pairs)]
     for copy in copies:
         copy.start()
-    rest = sz.thin_rows - 2 * sz.thin
-    if rest:
-        tmp_thin[pl.ds(2 * sz.thin, rest), :] = jnp.zeros((rest, sz.lat), F32)
+    spare = sz.thin_rows - 2 * sz.thin
+    if spare:
+        tmp_thin[pl.ds(2 * sz.thin, spare), :] = jnp.zeros((spare, sz.lat), F32)
     tmp_thick[...] = jnp.zeros_like(tmp_thick)
-    for copy in copies[:3]:
+    for copy in copies[:6]:
         copy.wait()
     info = [mask_v[0:1, :].astype(F32)] + split3(wind_v[0, 0:1, :]) + split3(wind_v[1, 0:1, :])
     for i, line in enumerate(info):
         tmp_thick[pl.ds(sz.info + i, 1), :] = line
+    for k in range(sz.bands):
+        tmp_thin[pl.ds(k * sz.half, count), :] = late[k]
+        tmp_thin[pl.ds(k * sz.half + count, rest), :] = early[k]
+        tmp_thick[pl.ds(k * sz.thick, sz.angles), :] = first[k]
+        tmp_thick[pl.ds(k * sz.thick + sz.angles, sz.half), :] = second[k]
+    for copy in copies[6:]:
+        copy.wait()
+    for k in range(sz.bands):
+        at = sz.thin + k * sz.half
+        tmp_thin[pl.ds(at, count), :] = late_n[k]
+        tmp_thin[pl.ds(at + count, rest), :] = early_n[k]
+        tmp_thick[pl.ds(sz.thick_nest + k * sz.half, sz.half), :] = first_n[k]
+    thin[...] = tmp_thin[...].astype(BF16)
+    thick[...] = tmp_thick[...].astype(BF16)
+
+
+def setup_kernel(sz, table, mask, wind, moves, nest_moves, s_moves, gain, sea):
     per = VREG // sz.cols
-    sea[...] = jnp.concatenate([mask_v[...].astype(F32)] * per, axis=0)
-    east_wind = jnp.concatenate([wind_v[0]] * per, axis=0)
-    north_wind = jnp.concatenate([wind_v[1]] * per, axis=0)
-    fill_moves(sz, 0, table_v, sz.cols, (moves, nest_moves))
-    fill_moves(sz, sz.ring + VREG, table_v, 1, (s_moves, None))
+    sea[...] = jnp.concatenate([mask[...].astype(F32)] * per, axis=0)
+    east_wind = jnp.concatenate([wind[0]] * per, axis=0)
+    north_wind = jnp.concatenate([wind[1]] * per, axis=0)
+    fill_moves(sz, 0, table, sz.cols, (moves, nest_moves))
+    fill_moves(sz, sz.ring + VREG, table, 1, (s_moves, None))
     for v in range(sz.vregs):
-        rows = table_v[pl.ds(v * VREG, VREG), :]
+        rows = table[pl.ds(v * VREG, VREG), :]
         along = rows[:, 0:1] * east_wind + rows[:, 1:2] * north_wind
         gain[pl.ds(v * VREG, VREG), :] = wind_coef * jnp.maximum(along, 0.0)
     for v in range(sz.side // VREG):
-        rows = table_v[pl.ds(sz.ring + VREG + v * VREG, VREG), :]
+        rows = table[pl.ds(sz.ring + VREG + v * VREG, VREG), :]
         for i in range(2):
             s_moves[3 + i, pl.ds(v * VREG, VREG), :] = jnp.broadcast_to(rows[:, i : i + 1], (VREG, sz.lat))
-
-    def west(source, row, at):
-        for first, count in west_half(sz):
-            start = row + first * sz.cols + sz.cols - 1
-            tmp_thin[pl.ds(at, count), :] = source[pl.ds(start, count, stride=sz.cols), :]
-            at += count
-
-    def east(source, row, at):
-        start = row + sz.quarter * sz.cols
-        tmp_thick[pl.ds(at, sz.half), :] = source[pl.ds(start, sz.half, stride=sz.cols), :]
-
-    copies[3].wait()
-    for k in range(sz.bands):
-        row = k * sz.ring
-        west(field, row, k * sz.half)
-        at = k * sz.thick
-        tmp_thick[pl.ds(at, sz.angles), :] = field[pl.ds(row, sz.angles, stride=sz.cols), :]
-        east(field, row + 1, at + sz.angles)
-    copies[4].wait()
-    for k in range(sz.bands):
-        row = k * sz.ring
-        west(nest_field, row, sz.thin + k * sz.half)
-        east(nest_field, row, sz.thick_nest + k * sz.half)
-    thin[...] = tmp_thin[...].astype(BF16)
-    thick[...] = tmp_thick[...].astype(BF16)
 
 
 def raw_kernel(sz, energy, raw_a, raw_b):
@@ -344,7 +348,7 @@
     over_bands(sz.bands, band_ratio(sz, 0, True), band, True)
 
 
-def nest_edge_kernel(sz, inner, from_w, from_e, moves, out, wide_w, wide_e):
+def nest_edge_kernel(sz, inner, from_w, from_e, moves, out, columns, wide_w, wide_e):
     grid_rank = lax.axis_index("grid")
     quarter = sz.grid // 4
     keep_w = jnp.where((grid_rank != quarter) & (grid_rank != 3 * quarter), 1.0, 0.0).astype(F32)
@@ -357,6 +361,8 @@
         for first, count, col, moved in edge_parts(sz, moves, wide_w, at_w, wide_e, at_e):
             rows = pl.ds(k * sz.ring + first * sz.cols + col, count, stride=sz.cols)
             out[rows, :] = out[rows, :] + moved * (speed * (keep_w if col == 0 else keep_e))
+    for c in range(sz.cols):
+        columns[c, pl.ds(0, sz.bins), :] = out[pl.ds(c, sz.bins, stride=sz.cols), :]
 
 
 def dot_lanes(a, b):
@@ -478,12 +484,59 @@
     lax.fori_loop(0, reach, halo, 0)
 
 
-def inner_kernel(
-    sz, adv, side, recv_a, raw_a, raw_b, moves, sea, plain, turned, plus, minus, s_plain, s_plus, s_minus, far_near, wide, fix
-):
+def numerators(sz, k, ratio, adv, gain, plus, minus, store):
+    nv, low = sz.vregs, low_rows(sz)
+    base = pl.multiple_of(k * sz.ring, VREG)
+
+    def moved_in(v):
+        return (
+            plus[k, pl.ds(v * VREG, VREG), :]
+            + minus[k, pl.ds((v + 3) * VREG, VREG), :]
+            + plus[k + 5, pl.ds((v + 2) * VREG, VREG), :]
+            + minus[k + 5, pl.ds((v + 1) * VREG, VREG), :]
+        )
+
+    before = moved_in(nv - 1)
+    for v in range(nv):
+        now = moved_in(v)
+        moved = pltpu.roll(jnp.where(low, now, before), VREG // 2, 0)
+        before = now
+        here = pl.ds((v + 1) * VREG, VREG)
+        transfer = moved - 2.0 * (plus[k + 2, here, :] + minus[k + 2, here, :])
+        a = adv[pl.ds(base + v * VREG, VREG), :]
+        grown = ratio * gain[pl.ds(v * VREG, VREG), :]
+        store(pl.ds(base + v * VREG, VREG), a + grown * a + transfer)
+
+
+def beyond_kernel(sz, raw_a, raw_b, moves, sea, plain, far_near, wide):
     base_a = jnp.where(is_even(), sz.bands + reach, 0)
     base_b = sz.bands + reach - base_a
     below, above = band_ratio(sz, -reach, True), band_ratio(sz, sz.bands, True)
+
+    for raw, first, inverse in (
+        (raw_a, base_a, jnp.where(is_even(), above, below)),
+        (raw_b, base_b, jnp.where(is_even(), below, above)),
+    ):
+        wide[...] = raw[...].astype(F32)
+
+        def transport(k, r, first=first):
+            base = pl.multiple_of(k * sz.ring, VREG)
+            for v in range(sz.vregs):
+                moved = transported(sz, wide, base, v, moves, speed_coef * r)
+                plain[first + k, pl.ds(v * VREG, VREG), :] = sea[...] * moved
+
+        over_bands(reach, inverse, transport, True)
+
+    far_near[...] = jnp.zeros_like(far_near)
+    for k in range(reach):
+        for first, count in west_half(sz):
+            start = k * sz.ring + first * sz.cols + sz.cols - 1
+            far_near[pl.ds(k * sz.side + first, count), :] = wide[pl.ds(start, count, stride=sz.cols), :]
+
+def inner_kernel(
+    sz, adv, side, recv_a, gain, plain_in, plain, turned, plus, minus, s_plain, s_plus, s_minus, num, fix
+):
+    base_a = jnp.where(is_even(), sz.bands + reach, 0)
 
     def own(k, carry):
         base = pl.multiple_of(k * sz.ring, VREG)
@@ -494,25 +547,6 @@
 
     lax.fori_loop(0, sz.bands, own, 0)
 
-    for raw, first, inverse in (
-        (raw_a, base_a, jnp.where(is_even(), above, below)),
-        (raw_b, base_b, jnp.where(is_even(), below, above)),
-    ):
-        wide[...] = raw[...].astype(F32)
-
-        def transport(k, r, first=first):
-            base = pl.multiple_of(k * sz.ring, VREG)
-            for v in range(sz.vregs):
-                moved = transported(sz, wide, base, v, moves, speed_coef * r)
-                plain[first + k, pl.ds(v * VREG, VREG), :] = sea[...] * moved
-
-        over_bands(reach, inverse, transport, True)
-
-    far_near[...] = jnp.zeros_like(far_near)
-    for k in range(reach):
-        for first, count in west_half(sz):
-            start = k * sz.ring + first * sz.cols + sz.cols - 1
-            far_near[pl.ds(k * sz.side + first, count), :] = wide[pl.ds(start, count, stride=sz.cols), :]
     fix[...] = recv_a[...].astype(F32)
     for k in range(reach):
         complete(sz, base_a + k, fix, k, plain, s_plain)
@@ -523,15 +557,46 @@
     ratio = jnp.where(is_even(), band_ratio(sz, 3), band_ratio(sz, 3 - reach))
     over_bands(sz.bands, ratio, lambda i, r: strengths(sz, r, start + i, *arrays))
 
+    def store(rows, value):
+        num[rows, :] = value
+
+    ratio = jnp.where(is_even(), band_ratio(sz, reach), band_ratio(sz, 0))
+    over_bands(
+        sz.bands - reach, ratio, lambda i, r: numerators(sz, start + i, r, adv, gain, plus, minus, store)
+    )
+
 
 def source_kernel(
-    sz, adv, side, recv_b, pair, other, gain, moves, s_moves, sea, from_e, mix, far_near,
+    sz, adv, side, recv_b, pair, other, gain, moves, s_moves, sea, from_e, mix, far_near, num,
     plain_in, turned_in, plus_in, minus_in, s_plain_in, s_plus_in, s_minus_in,
     result_hbm, msg, plain, turned, plus, minus, s_plain, s_plus, s_minus, s_out, wide, s_near, out, sems,
 ):
     spec_rank = lax.axis_index("spec")
-    nv, ns = sz.vregs, sz.side // VREG
-    low, turn = low_rows(sz), VREG // 2
+    ns = sz.side // VREG
+    total_weight = sz.angles * 0.1 * sum(ratio_step ** (k - sz.freqs // 2) for k in range(sz.freqs))
+    means = (pair[...] + other[...]) * (1.0 / total_weight)
+    mean = jnp.concatenate([means[0 : sz.cols]] * (VREG // sz.cols), axis=0)
+    s_mean = means[sz.cols : sz.cols + 1]
+
+    def write(k):
+        band = pl.ds(pl.multiple_of(k * sz.ring, VREG), sz.ring)
+        return pltpu.make_async_copy(out.at[band], result_hbm.at[band], sems.at[k])
+
+    def scale(ratio):
+        return 1.0 / (1.0 + (dissip_coef * ratio * ratio) * mean)
+
+    ready = jnp.where(is_even(), reach, 0)
+
+    def finish(i, ratio):
+        factor = scale(ratio)
+        base = pl.multiple_of((ready + i) * sz.ring, VREG)
+        for v in range(sz.vregs):
+            here = pl.ds(base + v * VREG, VREG)
+            out[here, :] = num[here, :] * factor
+        write(ready + i).start()
+
+    over_bands(sz.bands - reach, jnp.where(is_even(), band_ratio(sz, reach), band_ratio(sz, 0)), finish)
+
     base_b = jnp.where(is_even(), 0, sz.bands + reach)
     real_b = jnp.where((spec_rank == 0) | (spec_rank == sz.spec - 1), 0.0, 1.0).astype(F32)
     info = from_e[pl.ds(sz.info // 16 * 16, 32), :].astype(F32)
@@ -564,40 +629,18 @@
     at = at + 1
     s_east = info[at : at + 1] + info[at + 1 : at + 2] + info[at + 2 : at + 3]
     s_north = info[at + 3 : at + 4] + info[at + 4 : at + 5] + info[at + 5 : at + 6]
-    total_weight = sz.angles * 0.1 * sum(ratio_step ** (k - sz.freqs // 2) for k in range(sz.freqs))
-    means = (pair[...] + other[...]) * (1.0 / total_weight)
-    mean = jnp.concatenate([means[0 : sz.cols]] * (VREG // sz.cols), axis=0)
-    s_mean = means[sz.cols : sz.cols + 1]
-
-    def result(k, ratio):
-        scale = 1.0 / (1.0 + (dissip_coef * ratio * ratio) * mean)
-        base = pl.multiple_of(k * sz.ring, VREG)
-
-        def moved_in(v):
-            return (
-                plus[k, pl.ds(v * VREG, VREG), :]
-                + minus[k, pl.ds((v + 3) * VREG, VREG), :]
-                + plus[k + 5, pl.ds((v + 2) * VREG, VREG), :]
-                + minus[k + 5, pl.ds((v + 1) * VREG, VREG), :]
-            )
-
-        before = moved_in(nv - 1)
-        for v in range(nv):
-            now = moved_in(v)
-            moved = pltpu.roll(jnp.where(low, now, before), turn, 0)
-            before = now
-            here = pl.ds((v + 1) * VREG, VREG)
-            transfer = moved - 2.0 * (plus[k + 2, here, :] + minus[k + 2, here, :])
-            a = adv[pl.ds(base + v * VREG, VREG), :]
-            grown = ratio * gain[pl.ds(v * VREG, VREG), :]
-            out[pl.ds(base + v * VREG, VREG), :] = (a + grown * a + transfer) * scale
-        write(k).start()
-
-    def write(k):
-        band = pl.ds(pl.multiple_of(k * sz.ring, VREG), sz.ring)
-        return pltpu.make_async_copy(out.at[band], result_hbm.at[band], sems.at[k])
-
-    over_bands(sz.bands, band_ratio(sz, 0), result)
+    missing = jnp.where(is_even(), 0, sz.bands - reach)
+
+    def result(i, ratio):
+        factor = scale(ratio)
+
+        def store(rows, value):
+            out[rows, :] = value * factor
+
+        numerators(sz, missing + i, ratio, adv, gain, plus, minus, store)
+        write(missing + i).start()
+
+    over_bands(reach, jnp.where(is_even(), band_ratio(sz, 0), band_ratio(sz, sz.bands - reach)), result)
 
     s_gain = []
     for v in range(ns):
@@ -606,7 +649,7 @@
         s_gain.append(wind_coef * jnp.maximum(along, 0.0))
     for k in range(sz.bands):
         ratio = band_ratio(sz, k)
-        scale = 1.0 / (1.0 + (dissip_coef * ratio * ratio) * s_mean)
+        factor = 1.0 / (1.0 + (dissip_coef * ratio * ratio) * s_mean)
         for v in range(ns):
             row = (v + 1) * VREG
             here = pl.ds(row, VREG)
@@ -618,7 +661,7 @@
                 - 2.0 * (s_plus[k + 2, here, :] + s_minus[k + 2, here, :])
             )
             a = side[pl.ds(k * sz.side + v * VREG, VREG), :]
-            s_out[pl.ds(k * sz.angles + v * VREG, VREG), :] = (a + (ratio * s_gain[v]) * a + transfer) * scale
+            s_out[pl.ds(k * sz.angles + v * VREG, VREG), :] = (a + (ratio * s_gain[v]) * a + transfer) * factor
 
     pad = jnp.zeros((sz.lanes - sz.bins, sz.lat), BF16)
     columns = [out[pl.ds(c, sz.bins, stride=sz.cols), :] for c in range(sz.cols)]
@@ -650,7 +693,8 @@
         )
         for c in range(sz.cols):
             here = pl.ds(start * sz.cols + c, count, stride=sz.cols)
-            out[here, :] = nest_adv[here, :] * kept[c] + added[:count, c * sz.lat : (c + 1) * sz.lat]
+            own = nest_adv[c, pl.ds(start, count), :]
+            out[here, :] = own * kept[c] + added[:count, c * sz.lat : (c + 1) * sz.lat]
         rows = pl.ds(start * sz.cols, count * sz.cols)
         writes.append(pltpu.make_async_copy(out.at[rows], result_hbm.at[rows], sems.at[part]))
         writes[-1].start()
@@ -693,7 +737,7 @@
 
     field = array(sz.rows)
     table = jnp.asarray(angle_table(sz))
-    energy = energy.reshape(sz.rows, sz.lat)
+    energy4, energy = energy, energy.reshape(sz.rows, sz.lat)
     nest = nest_energy.reshape(sz.rows, sz.lat)
     up = [(i, (i + 1) % sz.grid) for i in range(sz.grid)]
     down = [(j, i) for i, j in up]
@@ -701,40 +745,46 @@
     for g in range(sz.grid):
         for i in range(sz.spec):
             j = i + 1 if i % 2 else i - 1
-            to = (g, j) if 0 <= j < sz.spec else ((g ^ 1) % sz.grid, i)
+            to = (g, j) if 0 <= j < sz.spec else ((g ^ 2) % sz.grid, i)
             across.append((g * sz.spec + i, to[0] * sz.spec + to[1]))
     both = ("grid", "spec")
     near_rows = [vmem(sz.thin_rows), vmem(sz.thick_rows)]
 
     stay = functools.partial(pltpu.with_memory_space_constraint, memory_space=pltpu.HBM)
-    thin, thick, moves, nest_moves, s_moves, gain, sea = kernel_call(
+    def column(n):
+        return vmem(sz.bands, n)
+
+    thin, thick = kernel_call(
         functools.partial(pack_kernel, sz),
-        (
-            half(sz.thin_rows),
-            half(sz.thick_rows),
-            array(3, sz.ring),
-            array(3, sz.ring),
-            array(5, sz.side),
-            array(sz.ring),
-            array(VREG),
-        ),
-        5,
-        hbm=range(5),
+        (half(sz.thin_rows), half(sz.thick_rows)),
+        4,
+        hbm=range(4),
         scratch=[
-            vmem(*table.shape[:1]),
-            vmem(sz.rows),
-            vmem(sz.rows),
+            column(sz.angles),
+            column(sz.half),
+            column(sz.half),
+            column(sz.angles - 3 * sz.quarter),
+            column(sz.quarter),
+            column(sz.angles - 3 * sz.quarter),
+            column(sz.quarter),
             pltpu.VMEM(ocean_mask.shape, ocean_mask.dtype),
             pltpu.VMEM(wind_field.shape, F32),
         ]
         + near_rows
-        + [pltpu.SemaphoreType.DMA((5,))],
+        + [pltpu.SemaphoreType.DMA((9,))],
         name="pack",
-    )(stay(table), stay(energy), stay(nest), stay(ocean_mask), stay(wind_field))
+    )(stay(energy4), stay(nest_energy), stay(ocean_mask), stay(wind_field))
     from_e = lax.ppermute(thick, "grid", down)
     from_w = lax.ppermute(thin, "grid", up)
 
-    energy, sea = lax.optimization_barrier((energy, sea))
+    table, thin = lax.optimization_barrier((table, thin))
+    moves, nest_moves, s_moves, gain, sea = kernel_call(
+        functools.partial(setup_kernel, sz),
+        (array(3, sz.ring), array(3, sz.ring), array(5, sz.side), array(sz.ring), array(VREG)),
+        3,
+        name="setup",
+    )(table, ocean_mask, wind_field)
+    energy, table = lax.optimization_barrier((energy, table))
     raw_a, raw_b = kernel_call(
         functools.partial(raw_kernel, sz), (half(sz.edge_rows), half(sz.edge_rows)), 1, name="raw"
     )(energy)
@@ -774,9 +824,18 @@
         name="edges",
     )(adv, total, energy, from_w, from_e, moves, s_moves, sea)
 
-    msg_a, msg_b, recv_raw_a, recv_raw_b = lax.optimization_barrier((msg_a, msg_b, recv_raw_a, recv_raw_b))
+    msg_a, msg_b = lax.optimization_barrier((msg_a, msg_b))
     recv_a = lax.ppermute(msg_a, "spec", pairs)
     recv_b = lax.ppermute(msg_b, both, across)
+    recv_a, recv_raw_a, recv_raw_b = lax.optimization_barrier((recv_a, recv_raw_a, recv_raw_b))
+    plain, far_near = kernel_call(
+        functools.partial(beyond_kernel, sz),
+        (array(sz.bands + 2 * reach, sz.ring), array(reach * sz.side)),
+        4,
+        scratch=[vmem(sz.edge_rows)],
+        flops=3 * 10**10,
+        name="beyond",
+    )(recv_raw_a, recv_raw_b, moves, sea)
     pieces = recv_a[sz.sum_row : sz.sum_row + 3 * VREG].astype(F32)
     pair = part + pieces.reshape(3, VREG, sz.lat).sum(axis=0)
     other = jnp.zeros_like(pair)
@@ -786,9 +845,9 @@
         other = lax.ppermute(pair, "spec", [(i, i ^ (2 * step - 1)) for i in range(sz.spec)])
         step *= 2
 
-    nest_adv = kernel_call(
+    _, nest_adv = kernel_call(
         functools.partial(nest_edge_kernel, sz),
-        field,
+        (field, array(sz.cols, sz.bins + VREG)),
         4,
         scratch=near_rows,
         aliases={0: 0},
@@ -805,23 +864,24 @@
         array(centres, sz.frame),
         array(centres, sz.frame),
     )
-    *inner, far_near = kernel_call(
+    *inner, num = kernel_call(
         functools.partial(inner_kernel, sz),
-        arrays + (array(reach * sz.side),),
-        7,
-        scratch=[vmem(sz.edge_rows), vmem(sz.fix_rows)],
+        arrays + (field,),
+        5,
+        scratch=[vmem(sz.fix_rows)],
+        aliases={4: 0},
         name="inner",
-    )(adv, side, recv_a, recv_raw_a, recv_raw_b, moves, sea)
+    )(adv, side, recv_a, gain, plain)
     nest_adv, recv_b = lax.optimization_barrier((nest_adv, recv_b))
     global_next, msg, *_ = kernel_call(
         functools.partial(source_kernel, sz),
         (field, jax.ShapeDtypeStruct((sz.slots, sz.lanes), BF16)) + arrays,
-        12 + len(arrays),
+        13 + len(arrays),
         scratch=[vmem(sz.bins + VREG), vmem(sz.pass_rows), vmem(reach * sz.side), vmem(sz.rows), pltpu.SemaphoreType.DMA((sz.bands,))],
         out_hbm=(0,),
-        aliases={12 + i: 2 + i for i in range(len(arrays))},
+        aliases={13 + i: 2 + i for i in range(len(arrays))},
         name="sources",
-    )(adv, side, recv_b, pair, other, gain, moves, s_moves, sea, from_e, mix, far_near, *inner)
+    )(adv, side, recv_b, pair, other, gain, moves, s_moves, sea, from_e, mix, far_near, num, *inner)
 
     recv = lax.all_to_all(msg, "grid", split_axis=0, concat_axis=0, tiled=True)
     nest_next = kernel_call(

time: 34.8 us -> 34.4 us (0.989)
  waiting for transfers between devices: 4.25 us -> 1.11 us
  blocking collectives: 11.7 us -> 13.3 us
  starting transfers between devices: 9.14 us -> 10.2 us
    all_to_all x1, blocking collectives: 11.7 us -> 13.3 us  [per_device(): recv = lax.all_to_all(msg, 'grid', split_axis=0, concat_axis=0, tiled=True)]
    ppermute x1, waiting for transfers between devices: 1.91 us -> 0.49 us  [per_device(): lax.ppermute(raw_b, 'spec', [(i, (i + 1 if i % 2 else i - 1) % sz.spec) f...]
    ppermute x1, starting transfers between devices: 0.01 us -> 1.3 us  [per_device(): recv_b = lax.ppermute(msg_b, both, across)]
    ppermute x1, waiting for transfers between devices: 1.18 us -> 0.01 us  [per_device(): recv_a = lax.ppermute(msg_a, 'spec', pairs)]
    ppermute x1, waiting for transfers between devices: 0.53 us -> 0.01 us  [per_device(): recv_b = lax.ppermute(msg_b, both, across)]
    pallas_call x2 -> x4, Pallas kernels: 1.8 us -> 2.19 us  [the longest x1 0.99 us: per_device(): kernel_call(functools.partial(beyond_kernel, sz), (array(sz.bands + 2 * r...]
  transfers between devices with their start and end apart: 7 -> 7, of which waited for: 4 -> 3; matrix products, arithmetic and copies ran while one was open for 0% -> 0% of each run, Pallas kernels for 12% -> 14%
where the time goes in v5:
time: 34.4 us; the launch traced here: 34.3 us
  blocking collectives  13.3 us (39%)
  starting transfers between devices  10.2 us (30%)
  Pallas kernels  8.75 us (25%)
  waiting for transfers between devices  1.11 us (3%)
  between operations  0.85 us (2%)
    all_to_all x1, blocking collectives, per_device(): recv = lax.all_to_all(msg, 'grid', split_axis=0, concat_axis=0, tiled=True)  13.3 us
    ppermute x1, starting transfers between devices, per_device(): from_e = lax.ppermute(thick, 'grid', down)  3.1 us
    ppermute x1, starting transfers between devices, per_device(): from_w = lax.ppermute(thin, 'grid', up)  3.02 us
    pallas_call x1, Pallas kernels, per_device(): kernel_call(functools.partial(source_kernel, sz), (field, jax.ShapeDtypeS...  1.5 us
    pallas_call x1, Pallas kernels, per_device(): kernel_call(functools.partial(pack_kernel, sz), (half(sz.thin_rows), half...  1.31 us
    ppermute x1, starting transfers between devices, per_device(): recv_b = lax.ppermute(msg_b, both, across)  1.3 us
    pallas_call x1, Pallas kernels, per_device(): kernel_call(functools.partial(blend_kernel, sz), field, 2, out_hbm=(0,),...  1.26 us
    ppermute x1, starting transfers between devices, per_device(): recv_raw_a = lax.ppermute(raw_a, 'spec', pairs)  1.06 us
  transfers between devices with their start and end apart: 7, of which 3 were waited for; matrix products, arithmetic and copies ran while one was open for 0% of the time, Pallas kernels for 14%

profile of v5, /device:TPU:0, one launch (start us, length us, event | category | flops | bytes accessed | tf_op | source)
XLA Modules:
  0.0 34.3 jit_solution(14054556164397287432)
XLA Ops:
  0.6 0.0 copy-start.3
  0.6 0.0 copy-start.4
  0.7 0.0 copy-start.1
  0.7 0.0 copy-start
  0.7 0.0 copy-start.2
  0.7 1.3 %pack.1 = (bf16[336,128]{1,0:T(8,128)(2,1)S(1)}, bf16[672,128]{1,0:T(8,128)(2,1)S(1)}) custom-call(f32[9,36,4,128]{3,2,1,0:T(4,128)} %energy.1, f32[9,36,4,128]{3,2,1,0:T(4,128)} %nest.2, s32[4,128]{1,0:T(4,128)} %mask.3, f32[2,4,128]{2,1,0:T(4,128)} %wind.3), custom_call_target="tpu_custom_call" | custom-call | tf_op jit(solution)/shard_map/pack/pallas_call | solution.py:757
  2.0 3.0 %collective-permute-start.1 = (bf16[336,128]{1,0:T(8,128)(2,1)S(1)}, bf16[336,128]{1,0:T(8,128)(2,1)S(1)}, u32[]{:S(2)}, u32[]{:S(2)}) collective-permute-start(bf16[336,128]{1,0:T(8,128)(2,1)S(1)} %get-tuple-element.49), channel_id=1, source_target_pairs={{0,4},{4,8},{8,12},{12,16},{16,20},{20,24},{24,28},{28,0},{1,5},{5... | collective-permute-start | bytes 258056 | tf_op jit(solution)/shard_map/ppermute | solution.py:778
  5.0 3.1 %collective-permute-start = (bf16[672,128]{1,0:T(8,128)(2,1)S(1)}, bf16[672,128]{1,0:T(8,128)(2,1)S(1)}, u32[]{:S(2)}, u32[]{:S(2)}) collective-permute-start(bf16[672,128]{1,0:T(8,128)(2,1)S(1)} %get-tuple-element.48), channel_id=1, source_target_pairs={{4,0},{8,4},{12,8},{16,12},{20,16},{24,20},{28,24},{0,28},{5,1},{9... | collective-permute-start | bytes 516104 | tf_op jit(solution)/shard_map/ppermute | solution.py:777
  8.1 0.0 copy-done
  8.2 0.7 %collective-permute-start.5 = (bf16[720,128]{1,0:T(8,128)(2,1)S(1)}, bf16[720,128]{1,0:T(8,128)(2,1)S(1)}, u32[]{:S(2)}, u32[]{:S(2)}) collective-permute-start(bf16[720,128]{1,0:T(8,128)(2,1)S(1)} %get-tuple-element.75), channel_id=1, source_target_pairs={{0,3},{1,2},{2,1},{3,0},{4,7},{5,6},{6,5},{7,4},{8,11},{9,10},{10,... | collective-permute-start | bytes 552968 | tf_op jit(solution)/shard_map/ppermute | solution.py:792
  8.9 1.1 %collective-permute-start.4 = (bf16[720,128]{1,0:T(8,128)(2,1)S(1)}, bf16[720,128]{1,0:T(8,128)(2,1)S(1)}, u32[]{:S(2)}, u32[]{:S(2)}) collective-permute-start(bf16[720,128]{1,0:T(8,128)(2,1)S(1)} %get-tuple-element.52), channel_id=1, source_target_pairs={{0,1},{1,0},{2,3},{3,2},{4,5},{5,4},{6,7},{7,6},{8,9},{9,8},{10,11... | collective-permute-start | bytes 552968 | tf_op jit(solution)/shard_map/ppermute | solution.py:793
  9.9 0.0 copy-done.3
  9.9 0.0 copy-done.4
  9.9 0.0 copy-done.2
  9.9 0.2 setup.1
  10.1 0.0 copy-done.1
  10.1 0.8 %nest.3.inner = f32[1296,128]{1,0:T(8,128)S(1)} custom-call(f32[1296,128]{1,0:T(8,128)S(1)} %bitcast.17, f32[3,144,128]{2,1,0:T(8,128)S(1)} %get-tuple-element.57.moves), custom_call_target="tpu_custom_call" | custom-call | flops 30000001024 | tf_op jit(solution)/shard_map/nest/pallas_call | solution.py:803
  11.0 0.0 copy-start.5
  11.0 0.0 copy-start.6
  11.0 0.0 copy-start.7
  11.0 0.0 copy-start.8
  11.0 0.9 %local.1 = (f32[1296,128]{1,0:T(8,128)S(1)}, f32[8,128]{1,0:T(8,128)S(1)}) custom-call(f32[1296,128]{1,0:T(8,128)S(1)} %bitcast.14, f32[3,144,128]{2,1,0:T(8,128)S(1)} %get-tuple-element.58.moves, f32[8,128]{1,0:T(8,128)S(1)} %get-tuple-element.59.sea), custom_call_target="tpu_custom_call" | custom-call | flops 30000001024 | tf_op jit(solution)/shard_map/local/pallas_call | solution.py:805
  11.9 0.0 copy-done.5
  11.9 0.0 copy-done.6
  11.9 0.0 copy-done.7
  11.9 0.0 copy-done.8
  11.9 0.4 %rim.1.mix = bf16[256,768]{1,0:T(8,128)(2,1)S(1)} custom-call(s32[2,128]{1,0:T(2,128)S(1)} %bitcast.20, s32[1,128]{1,0:T(1,128)S(1)} %bitcast.21, s32[1,128]{1,0:T(1,128)S(1)} %bitcast.22, f32[3,128]{1,0:T(4,128)S(1)} %bitcast.19), custom_call_target="tpu_custom_call" | custom-call | tf_op jit(solution)/shard_map/rim/pallas_call | solution.py:796
  12.3 0.0 collective-permute-done.1.from_w
  12.4 0.3 collective-permute-done.from_e
  12.7 0.3 edges.1
  13.0 0.1 pass.1
  13.0 0.1 collective-permute-start.3
  13.1 1.3 %collective-permute-start.2 = (bf16[400,128]{1,0:T(8,128)(2,1)S(1)}, bf16[400,128]{1,0:T(8,128)(2,1)S(1)}, u32[]{:S(2)}, u32[]{:S(2)}) collective-permute-start(bf16[400,128]{1,0:T(8,128)(2,1)S(1)} %pass.1), channel_id=1, source_target_pairs={{0,8},{1,2},{2,1},{3,11},{4,12},{5,6},{6,5},{7,15},{8,0},{9,10},{1... | collective-permute-start | bytes 307208 | tf_op jit(solution)/shard_map/ppermute | solution.py:829
  14.4 0.1 nest_edge.1
  14.5 0.5 %collective-permute-done.5.raw_b = bf16[720,128]{1,0:T(8,128)(2,1)S(1)} collective-permute-done((bf16[720,128]{1,0:T(8,128)(2,1)S(1)}, bf16[720,128]{1,0:T(8,128)(2,1)S(1)}, u32[]{:S(2)}, u32[]{:S(2)}) %collective-permute-start.5) | collective-permute-done | bytes 184352 | tf_op jit(solution)/shard_map/ppermute | solution.py:792
  15.0 0.0 collective-permute-done.4.raw_a
  15.0 0.0 collective-permute-done.3.recv_a
  15.1 0.9 %collective-permute-start.6 = (f32[8,128]{1,0:T(8,128)S(1)}, f32[8,128]{1,0:T(8,128)S(1)}, u32[]{:S(2)}, u32[]{:S(2)}) collective-permute-start(f32[8,128]{1,0:T(8,128)S(1)} %add.3.pair), channel_id=1, source_target_pairs={{0,3},{1,2},{2,1},{3,0},{4,7},{5,6},{6,5},{7,4},{8,11},{9,10},{10,... | collective-permute-start | bytes 12296 | tf_op jit(solution)/shard_map/ppermute | solution.py:845
  15.9 1.0 %beyond.1 = (f32[19,144,128]{2,1,0:T(8,128)S(1)}, f32[200,128]{1,0:T(8,128)S(1)}) custom-call(bf16[720,128]{1,0:T(8,128)(2,1)S(1)} %collective-permute-done.4.raw_a, bf16[720,128]{1,0:T(8,128)(2,1)S(1)} %collective-permute-done.5.raw_b, f32[3,144,128]{2,1,0:T(8,128)S(1)} %get-tuple-element.58.moves, f32[8,128]{1,0:T(8,128)S(1)} %get-tuple-element.59.sea), custom_call_target="tpu_custom_call" | custom-call | flops 30000001024 | tf_op jit(solution)/shard_map/beyond/pallas_call | solution.py:831
  16.9 0.9 %inner.1 = (f32[19,144,128]{2,1,0:T(8,128)S(1)}, f32[19,168,128]{2,1,0:T(8,128)S(1)}, f32[14,168,128]{2,1,0:T(8,128)S(1)}, f32[14,168,128]{2,1,0:T(8,128)S(1)}, ...) custom-call(f32[1296,128]{1,0:T(8,128)S(1)} %get-tuple-element.66.ad, ...), custom_call_target="tpu_custom_call", output_to_operand_aliasing={{0}: (4, {})} | custom-call | tf_op jit(solution)/shard_map/inner/pallas_call | solution.py:867
  17.9 0.0 collective-permute-done.2.recv_b
  17.9 0.3 collective-permute-done.6.other
  18.1 1.5 %sources.1 = (f32[1296,128]{1,0:T(8,128)}, bf16[256,384]{1,0:T(8,128)(2,1)S(1)}, f32[19,144,128]{2,1,0:T(8,128)S(1)}, f32[19,168,128]{2,1,0:T(8,128)S(1)}, f32[1...) custom-call(f32[1296,128]{1,0:T(8,128)S(1)} %get-tuple-element.66.ad, ...), custom_call_target="tpu_custom_call", output_to_operand_aliasing={{2}: (13, {}), {3}: (14, {}), {4}: (15, {}), {5}: (16, {}),... | custom-call | tf_op jit(solution)/shard_map/sources/pallas_call | solution.py:876
  19.7 13.3 %all_to_all.11 = bf16[8,32,384]{2,1,0:T(8,128)(2,1)S(1)} all-to-all(bf16[8,32,384]{2,1,0:T(8,128)(2,1)S(1)} %bitcast.18), channel_id=1, replica_groups=mesh['grid'=8,'spec'=4] {'grid'}, dimensions={0} | all-to-all | bytes 393216 | tf_op jit(solution)/shard_map/all_to_all | solution.py:886
  33.0 1.3 %blend.1 = f32[1296,128]{1,0:T(8,128)} custom-call(bf16[256,384]{1,0:T(8,128)(2,1)S(1)} %bitcast.16, f32[4,332,128]{2,1,0:T(8,128)S(1)} %get-tuple-element.93.nest_adv), custom_call_target="tpu_custom_call" | custom-call | tf_op jit(solution)/shard_map/blend/pallas_call | solution.py:887
  (3 shorter events, 0.0 us)
Async XLA Ops:
  0.6 9.3 %copy-start.3 = (f32[2,4,128]{2,1,0:T(4,128)S(1)}, f32[2,4,128]{2,1,0:T(4,128)}, u32[]{:S(2)}) copy-start(f32[2,4,128]{2,1,0:T(4,128)} %wind.3) | copy-start | bytes 12292
  0.6 9.3 %copy-start.4 = (s32[4,128]{1,0:T(4,128)S(1)}, s32[4,128]{1,0:T(4,128)}, u32[]{:S(2)}) copy-start(s32[4,128]{1,0:T(4,128)} %mask.3) | copy-start | bytes 6148
  0.7 9.5 %copy-start.1 = (f32[9,36,4,128]{3,2,1,0:T(4,128)S(1)}, f32[9,36,4,128]{3,2,1,0:T(4,128)}, u32[]{:S(2)}) copy-start(f32[9,36,4,128]{3,2,1,0:T(4,128)} %nest.2) | copy-start | bytes 1990660
  0.7 7.5 %copy-start = (f32[9,36,4,128]{3,2,1,0:T(4,128)S(1)}, f32[9,36,4,128]{3,2,1,0:T(4,128)}, u32[]{:S(2)}) copy-start(f32[9,36,4,128]{3,2,1,0:T(4,128)} %energy.1) | copy-start | bytes 1990660
  0.7 9.3 %copy-start.2 = (f32[192,128]{1,0:T(8,128)S(1)}, f32[192,128]{1,0:T(8,128)}, u32[]{:S(2)}) copy-start(f32[192,128]{1,0:T(8,128)} %constant.4.clone.table) | copy-start | bytes 294916
  2.0 10.4 %collective-permute-start.1 = (bf16[336,128]{1,0:T(8,128)(2,1)S(1)}, bf16[336,128]{1,0:T(8,128)(2,1)S(1)}, u32[]{:S(2)}, u32[]{:S(2)}) collective-permute-start(bf16[336,128]{1,0:T(8,128)(2,1)S(1)} %get-tuple-element.49), channel_id=1, source_target_pairs={{0,4},{4,8},{8,12},{12,16},{16,20},{20,24},{24,28},{28,0},{1,5},{5... | collective-permute-start | bytes 258056 | tf_op jit(solution)/shard_map/ppermute | solution.py:778
  5.0 7.7 %collective-permute-start = (bf16[672,128]{1,0:T(8,128)(2,1)S(1)}, bf16[672,128]{1,0:T(8,128)(2,1)S(1)}, u32[]{:S(2)}, u32[]{:S(2)}) collective-permute-start(bf16[672,128]{1,0:T(8,128)(2,1)S(1)} %get-tuple-element.48), channel_id=1, source_target_pairs={{4,0},{8,4},{12,8},{16,12},{20,16},{24,20},{28,24},{0,28},{5,1},{9... | collective-permute-start | bytes 516104 | tf_op jit(solution)/shard_map/ppermute | solution.py:777
  8.2 6.9 %collective-permute-start.5 = (bf16[720,128]{1,0:T(8,128)(2,1)S(1)}, bf16[720,128]{1,0:T(8,128)(2,1)S(1)}, u32[]{:S(2)}, u32[]{:S(2)}) collective-permute-start(bf16[720,128]{1,0:T(8,128)(2,1)S(1)} %get-tuple-element.75), channel_id=1, source_target_pairs={{0,3},{1,2},{2,1},{3,0},{4,7},{5,6},{6,5},{7,4},{8,11},{9,10},{10,... | collective-permute-start | bytes 552968 | tf_op jit(solution)/shard_map/ppermute | solution.py:792
  8.9 6.1 %collective-permute-start.4 = (bf16[720,128]{1,0:T(8,128)(2,1)S(1)}, bf16[720,128]{1,0:T(8,128)(2,1)S(1)}, u32[]{:S(2)}, u32[]{:S(2)}) collective-permute-start(bf16[720,128]{1,0:T(8,128)(2,1)S(1)} %get-tuple-element.52), channel_id=1, source_target_pairs={{0,1},{1,0},{2,3},{3,2},{4,5},{5,4},{6,7},{7,6},{8,9},{9,8},{10,11... | collective-permute-start | bytes 552968 | tf_op jit(solution)/shard_map/ppermute | solution.py:793
  11.0 0.9 %copy-start.5 = (f32[128,3]{0,1:T(4,128)S(1)}, f32[128,3]{0,1:T(4,128)}, u32[]{:S(2)}) copy-start(f32[128,3]{0,1:T(4,128)} %param.16) | copy-start | bytes 4612
  11.0 0.9 %copy-start.6 = (s32[128,2]{0,1:T(2,128)S(1)}, s32[128,2]{0,1:T(2,128)}, u32[]{:S(2)}) copy-start(s32[128,2]{0,1:T(2,128)} %param.13) | copy-start | bytes 3076
  11.0 0.9 %copy-start.7 = (s32[128,1]{0,1:T(1,128)S(1)}, s32[128,1]{0,1:T(1,128)}, u32[]{:S(2)}) copy-start(s32[128,1]{0,1:T(1,128)} %param.14) | copy-start | bytes 1540
  11.0 0.9 %copy-start.8 = (s32[128]{0:T(128)S(1)}, s32[128]{0:T(128)}, u32[]{:S(2)}) copy-start(s32[128]{0:T(128)} %param.15) | copy-start | bytes 1540
  13.0 2.0 %collective-permute-start.3 = (bf16[384,128]{1,0:T(8,128)(2,1)S(1)}, bf16[384,128]{1,0:T(8,128)(2,1)S(1)}, u32[]{:S(2)}, u32[]{:S(2)}) collective-permute-start(bf16[384,128]{1,0:T(8,128)(2,1)S(1)} %get-tuple-element.74), channel_id=1, source_target_pairs={{0,1},{1,0},{2,3},{3,2},{4,5},{5,4},{6,7},{7,6},{8,9},{9,8},{10,11... | collective-permute-start | bytes 294920 | tf_op jit(solution)/shard_map/ppermute | solution.py:828
  13.1 4.7 %collective-permute-start.2 = (bf16[400,128]{1,0:T(8,128)(2,1)S(1)}, bf16[400,128]{1,0:T(8,128)(2,1)S(1)}, u32[]{:S(2)}, u32[]{:S(2)}) collective-permute-start(bf16[400,128]{1,0:T(8,128)(2,1)S(1)} %pass.1), channel_id=1, source_target_pairs={{0,8},{1,2},{2,1},{3,11},{4,12},{5,6},{6,5},{7,15},{8,0},{9,10},{1... | collective-permute-start | bytes 307208 | tf_op jit(solution)/shard_map/ppermute | solution.py:829
  15.1 3.1 %collective-permute-start.6 = (f32[8,128]{1,0:T(8,128)S(1)}, f32[8,128]{1,0:T(8,128)S(1)}, u32[]{:S(2)}, u32[]{:S(2)}) collective-permute-start(f32[8,128]{1,0:T(8,128)S(1)} %add.3.pair), channel_id=1, source_target_pairs={{0,3},{1,2},{2,1},{3,0},{4,7},{5,6},{6,5},{7,4},{8,11},{9,10},{10,... | collective-permute-start | bytes 12296 | tf_op jit(solution)/shard_map/ppermute | solution.py:845

commit v6 on v5

--- a/solution.py
+++ b/solution.py
@@ -708,7 +708,7 @@
 
     many = isinstance(out_shape, tuple)
     out_specs = specs(len(out_shape) if many else 1, out_hbm)
-    return pl.pallas_call(
+    call = pl.pallas_call(
         body,
         out_shape=out_shape,
         in_specs=specs(n_in, hbm),
@@ -719,6 +719,14 @@
         cost_estimate=pl.CostEstimate(flops=flops, bytes_accessed=0, transcendentals=0) if flops else None,
         name=name,
     )
+    if not aliases:
+        return call
+
+    def in_place(*args):
+        pin = functools.partial(pltpu.with_memory_space_constraint, memory_space=pltpu.VMEM)
+        return call(*[pin(a) if i in aliases else a for i, a in enumerate(args)])
+
+    return in_place
 
 
 def per_device(

time: 34.4 us -> 34.4 us (level)
  no operation moved by 1% of the time
where the time goes in v6:
time: 34.4 us; the launch traced here: 34.3 us
  blocking collectives  13.3 us (39%)
  starting transfers between devices  10.2 us (30%)
  Pallas kernels  8.75 us (25%)
  waiting for transfers between devices  1.11 us (3%)
  between operations  0.85 us (2%)
    all_to_all x1, blocking collectives, per_device(): recv = lax.all_to_all(msg, 'grid', split_axis=0, concat_axis=0, tiled=True)  13.3 us
    ppermute x1, starting transfers between devices, per_device(): from_e = lax.ppermute(thick, 'grid', down)  3.1 us
    ppermute x1, starting transfers between devices, per_device(): from_w = lax.ppermute(thin, 'grid', up)  3.02 us
    pallas_call x4, Pallas kernels, in_place(): return call(*[pin(a) if i in aliases else a for i, a in enumerate(args)])  2.83 us
    pallas_call x1, Pallas kernels, per_device(): kernel_call(functools.partial(pack_kernel, sz), (half(sz.thin_rows), half...  1.31 us
    ppermute x1, starting transfers between devices, per_device(): recv_b = lax.ppermute(msg_b, both, across)  1.3 us
    pallas_call x1, Pallas kernels, per_device(): kernel_call(functools.partial(blend_kernel, sz), field, 2, out_hbm=(0,),...  1.26 us
    ppermute x1, starting transfers between devices, per_device(): recv_raw_a = lax.ppermute(raw_a, 'spec', pairs)  1.06 us
  transfers between devices with their start and end apart: 7, of which 3 were waited for; matrix products, arithmetic and copies ran while one was open for 0% of the time, Pallas kernels for 14%

profile of v6, /device:TPU:0, one launch (start us, length us, event | category | flops | bytes accessed | tf_op | source)
XLA Modules:
  0.0 34.3 jit_solution(14054556164397287432)
XLA Ops:
  0.6 0.0 copy-start.3
  0.6 0.0 copy-start.4
  0.7 0.0 copy-start.1
  0.7 0.0 copy-start
  0.7 0.0 copy-start.2
  0.7 1.3 %pack.1 = (bf16[336,128]{1,0:T(8,128)(2,1)S(1)}, bf16[672,128]{1,0:T(8,128)(2,1)S(1)}) custom-call(f32[9,36,4,128]{3,2,1,0:T(4,128)} %energy.1, f32[9,36,4,128]{3,2,1,0:T(4,128)} %nest.2, s32[4,128]{1,0:T(4,128)} %mask.3, f32[2,4,128]{2,1,0:T(4,128)} %wind.3), custom_call_target="tpu_custom_call" | custom-call | tf_op jit(solution)/shard_map/pack/pallas_call | solution.py:765
  2.0 3.0 %collective-permute-start.1 = (bf16[336,128]{1,0:T(8,128)(2,1)S(1)}, bf16[336,128]{1,0:T(8,128)(2,1)S(1)}, u32[]{:S(2)}, u32[]{:S(2)}) collective-permute-start(bf16[336,128]{1,0:T(8,128)(2,1)S(1)} %get-tuple-element.49), channel_id=1, source_target_pairs={{0,4},{4,8},{8,12},{12,16},{16,20},{20,24},{24,28},{28,0},{1,5},{5... | collective-permute-start | bytes 258056 | tf_op jit(solution)/shard_map/ppermute | solution.py:786
  5.0 3.1 %collective-permute-start = (bf16[672,128]{1,0:T(8,128)(2,1)S(1)}, bf16[672,128]{1,0:T(8,128)(2,1)S(1)}, u32[]{:S(2)}, u32[]{:S(2)}) collective-permute-start(bf16[672,128]{1,0:T(8,128)(2,1)S(1)} %get-tuple-element.48), channel_id=1, source_target_pairs={{4,0},{8,4},{12,8},{16,12},{20,16},{24,20},{28,24},{0,28},{5,1},{9... | collective-permute-start | bytes 516104 | tf_op jit(solution)/shard_map/ppermute | solution.py:785
  8.1 0.0 copy-done
  8.2 0.7 %collective-permute-start.5 = (bf16[720,128]{1,0:T(8,128)(2,1)S(1)}, bf16[720,128]{1,0:T(8,128)(2,1)S(1)}, u32[]{:S(2)}, u32[]{:S(2)}) collective-permute-start(bf16[720,128]{1,0:T(8,128)(2,1)S(1)} %get-tuple-element.75), channel_id=1, source_target_pairs={{0,3},{1,2},{2,1},{3,0},{4,7},{5,6},{6,5},{7,4},{8,11},{9,10},{10,... | collective-permute-start | bytes 552968 | tf_op jit(solution)/shard_map/ppermute | solution.py:800
  8.9 1.1 %collective-permute-start.4 = (bf16[720,128]{1,0:T(8,128)(2,1)S(1)}, bf16[720,128]{1,0:T(8,128)(2,1)S(1)}, u32[]{:S(2)}, u32[]{:S(2)}) collective-permute-start(bf16[720,128]{1,0:T(8,128)(2,1)S(1)} %get-tuple-element.52), channel_id=1, source_target_pairs={{0,1},{1,0},{2,3},{3,2},{4,5},{5,4},{6,7},{7,6},{8,9},{9,8},{10,11... | collective-permute-start | bytes 552968 | tf_op jit(solution)/shard_map/ppermute | solution.py:801
  9.9 0.0 copy-done.3
  9.9 0.0 copy-done.4
  9.9 0.0 copy-done.2
  9.9 0.2 setup.1
  10.1 0.0 copy-done.1
  10.1 0.8 %nest.3.inner = f32[1296,128]{1,0:T(8,128)S(1)} custom-call(f32[1296,128]{1,0:T(8,128)S(1)} %bitcast.17, f32[3,144,128]{2,1,0:T(8,128)S(1)} %get-tuple-element.57.moves), custom_call_target="tpu_custom_call" | custom-call | flops 30000001024 | tf_op jit(solution)/shard_map/nest/pallas_call | solution.py:811
  11.0 0.0 copy-start.5
  11.0 0.0 copy-start.6
  11.0 0.0 copy-start.7
  11.0 0.0 copy-start.8
  11.0 0.9 %local.1 = (f32[1296,128]{1,0:T(8,128)S(1)}, f32[8,128]{1,0:T(8,128)S(1)}) custom-call(f32[1296,128]{1,0:T(8,128)S(1)} %bitcast.14, f32[3,144,128]{2,1,0:T(8,128)S(1)} %get-tuple-element.58.moves, f32[8,128]{1,0:T(8,128)S(1)} %get-tuple-element.59.sea), custom_call_target="tpu_custom_call" | custom-call | flops 30000001024 | tf_op jit(solution)/shard_map/local/pallas_call | solution.py:813
  11.9 0.0 copy-done.5
  11.9 0.0 copy-done.6
  11.9 0.0 copy-done.7
  11.9 0.0 copy-done.8
  11.9 0.4 %rim.1.mix = bf16[256,768]{1,0:T(8,128)(2,1)S(1)} custom-call(s32[2,128]{1,0:T(2,128)S(1)} %bitcast.20, s32[1,128]{1,0:T(1,128)S(1)} %bitcast.21, s32[1,128]{1,0:T(1,128)S(1)} %bitcast.22, f32[3,128]{1,0:T(4,128)S(1)} %bitcast.19), custom_call_target="tpu_custom_call" | custom-call | tf_op jit(solution)/shard_map/rim/pallas_call | solution.py:804
  12.3 0.0 collective-permute-done.1.from_w
  12.4 0.3 collective-permute-done.from_e
  12.7 0.3 edges.1
  13.0 0.1 pass.1
  13.0 0.1 collective-permute-start.3
  13.1 1.3 %collective-permute-start.2 = (bf16[400,128]{1,0:T(8,128)(2,1)S(1)}, bf16[400,128]{1,0:T(8,128)(2,1)S(1)}, u32[]{:S(2)}, u32[]{:S(2)}) collective-permute-start(bf16[400,128]{1,0:T(8,128)(2,1)S(1)} %pass.1), channel_id=1, source_target_pairs={{0,8},{1,2},{2,1},{3,11},{4,12},{5,6},{6,5},{7,15},{8,0},{9,10},{1... | collective-permute-start | bytes 307208 | tf_op jit(solution)/shard_map/ppermute | solution.py:837
  14.4 0.1 nest_edge.1
  14.5 0.5 %collective-permute-done.5.raw_b = bf16[720,128]{1,0:T(8,128)(2,1)S(1)} collective-permute-done((bf16[720,128]{1,0:T(8,128)(2,1)S(1)}, bf16[720,128]{1,0:T(8,128)(2,1)S(1)}, u32[]{:S(2)}, u32[]{:S(2)}) %collective-permute-start.5) | collective-permute-done | bytes 184352 | tf_op jit(solution)/shard_map/ppermute | solution.py:800
  15.0 0.0 collective-permute-done.4.raw_a
  15.0 0.0 collective-permute-done.3.recv_a
  15.1 0.9 %collective-permute-start.6 = (f32[8,128]{1,0:T(8,128)S(1)}, f32[8,128]{1,0:T(8,128)S(1)}, u32[]{:S(2)}, u32[]{:S(2)}) collective-permute-start(f32[8,128]{1,0:T(8,128)S(1)} %add.3.pair), channel_id=1, source_target_pairs={{0,3},{1,2},{2,1},{3,0},{4,7},{5,6},{6,5},{7,4},{8,11},{9,10},{10,... | collective-permute-start | bytes 12296 | tf_op jit(solution)/shard_map/ppermute | solution.py:853
  15.9 1.0 %beyond.1 = (f32[19,144,128]{2,1,0:T(8,128)S(1)}, f32[200,128]{1,0:T(8,128)S(1)}) custom-call(bf16[720,128]{1,0:T(8,128)(2,1)S(1)} %collective-permute-done.4.raw_a, bf16[720,128]{1,0:T(8,128)(2,1)S(1)} %collective-permute-done.5.raw_b, f32[3,144,128]{2,1,0:T(8,128)S(1)} %get-tuple-element.58.moves, f32[8,128]{1,0:T(8,128)S(1)} %get-tuple-element.59.sea), custom_call_target="tpu_custom_call" | custom-call | flops 30000001024 | tf_op jit(solution)/shard_map/beyond/pallas_call | solution.py:839
  16.9 0.9 %inner.1 = (f32[19,144,128]{2,1,0:T(8,128)S(1)}, f32[19,168,128]{2,1,0:T(8,128)S(1)}, f32[14,168,128]{2,1,0:T(8,128)S(1)}, f32[14,168,128]{2,1,0:T(8,128)S(1)}, ...) custom-call(f32[1296,128]{1,0:T(8,128)S(1)} %get-tuple-element.66.ad, ...), custom_call_target="tpu_custom_call", output_to_operand_aliasing={{0}: (4, {})} | custom-call | tf_op jit(solution)/shard_map/inner/pallas_call | solution.py:727
  17.9 0.0 collective-permute-done.2.recv_b
  17.9 0.3 collective-permute-done.6.other
  18.1 1.5 %sources.1 = (f32[1296,128]{1,0:T(8,128)}, bf16[256,384]{1,0:T(8,128)(2,1)S(1)}, f32[19,144,128]{2,1,0:T(8,128)S(1)}, f32[19,168,128]{2,1,0:T(8,128)S(1)}, f32[1...) custom-call(f32[1296,128]{1,0:T(8,128)S(1)} %get-tuple-element.66.ad, ...), custom_call_target="tpu_custom_call", output_to_operand_aliasing={{2}: (13, {}), {3}: (14, {}), {4}: (15, {}), {5}: (16, {}),... | custom-call | tf_op jit(solution)/shard_map/sources/pallas_call | solution.py:727
  19.7 13.3 %all_to_all.11 = bf16[8,32,384]{2,1,0:T(8,128)(2,1)S(1)} all-to-all(bf16[8,32,384]{2,1,0:T(8,128)(2,1)S(1)} %bitcast.18), channel_id=1, replica_groups=mesh['grid'=8,'spec'=4] {'grid'}, dimensions={0} | all-to-all | bytes 393216 | tf_op jit(solution)/shard_map/all_to_all | solution.py:894
  33.0 1.3 %blend.1 = f32[1296,128]{1,0:T(8,128)} custom-call(bf16[256,384]{1,0:T(8,128)(2,1)S(1)} %bitcast.16, f32[4,332,128]{2,1,0:T(8,128)S(1)} %get-tuple-element.93.nest_adv), custom_call_target="tpu_custom_call" | custom-call | tf_op jit(solution)/shard_map/blend/pallas_call | solution.py:895
  (3 shorter events, 0.0 us)
Async XLA Ops:
  0.6 9.3 %copy-start.3 = (f32[2,4,128]{2,1,0:T(4,128)S(1)}, f32[2,4,128]{2,1,0:T(4,128)}, u32[]{:S(2)}) copy-start(f32[2,4,128]{2,1,0:T(4,128)} %wind.3) | copy-start | bytes 12292
  0.6 9.3 %copy-start.4 = (s32[4,128]{1,0:T(4,128)S(1)}, s32[4,128]{1,0:T(4,128)}, u32[]{:S(2)}) copy-start(s32[4,128]{1,0:T(4,128)} %mask.3) | copy-start | bytes 6148
  0.7 9.5 %copy-start.1 = (f32[9,36,4,128]{3,2,1,0:T(4,128)S(1)}, f32[9,36,4,128]{3,2,1,0:T(4,128)}, u32[]{:S(2)}) copy-start(f32[9,36,4,128]{3,2,1,0:T(4,128)} %nest.2) | copy-start | bytes 1990660
  0.7 7.5 %copy-start = (f32[9,36,4,128]{3,2,1,0:T(4,128)S(1)}, f32[9,36,4,128]{3,2,1,0:T(4,128)}, u32[]{:S(2)}) copy-start(f32[9,36,4,128]{3,2,1,0:T(4,128)} %energy.1) | copy-start | bytes 1990660
  0.7 9.3 %copy-start.2 = (f32[192,128]{1,0:T(8,128)S(1)}, f32[192,128]{1,0:T(8,128)}, u32[]{:S(2)}) copy-start(f32[192,128]{1,0:T(8,128)} %constant.4.clone.table) | copy-start | bytes 294916
  2.0 10.4 %collective-permute-start.1 = (bf16[336,128]{1,0:T(8,128)(2,1)S(1)}, bf16[336,128]{1,0:T(8,128)(2,1)S(1)}, u32[]{:S(2)}, u32[]{:S(2)}) collective-permute-start(bf16[336,128]{1,0:T(8,128)(2,1)S(1)} %get-tuple-element.49), channel_id=1, source_target_pairs={{0,4},{4,8},{8,12},{12,16},{16,20},{20,24},{24,28},{28,0},{1,5},{5... | collective-permute-start | bytes 258056 | tf_op jit(solution)/shard_map/ppermute | solution.py:786
  5.0 7.7 %collective-permute-start = (bf16[672,128]{1,0:T(8,128)(2,1)S(1)}, bf16[672,128]{1,0:T(8,128)(2,1)S(1)}, u32[]{:S(2)}, u32[]{:S(2)}) collective-permute-start(bf16[672,128]{1,0:T(8,128)(2,1)S(1)} %get-tuple-element.48), channel_id=1, source_target_pairs={{4,0},{8,4},{12,8},{16,12},{20,16},{24,20},{28,24},{0,28},{5,1},{9... | collective-permute-start | bytes 516104 | tf_op jit(solution)/shard_map/ppermute | solution.py:785
  8.2 6.9 %collective-permute-start.5 = (bf16[720,128]{1,0:T(8,128)(2,1)S(1)}, bf16[720,128]{1,0:T(8,128)(2,1)S(1)}, u32[]{:S(2)}, u32[]{:S(2)}) collective-permute-start(bf16[720,128]{1,0:T(8,128)(2,1)S(1)} %get-tuple-element.75), channel_id=1, source_target_pairs={{0,3},{1,2},{2,1},{3,0},{4,7},{5,6},{6,5},{7,4},{8,11},{9,10},{10,... | collective-permute-start | bytes 552968 | tf_op jit(solution)/shard_map/ppermute | solution.py:800
  8.9 6.1 %collective-permute-start.4 = (bf16[720,128]{1,0:T(8,128)(2,1)S(1)}, bf16[720,128]{1,0:T(8,128)(2,1)S(1)}, u32[]{:S(2)}, u32[]{:S(2)}) collective-permute-start(bf16[720,128]{1,0:T(8,128)(2,1)S(1)} %get-tuple-element.52), channel_id=1, source_target_pairs={{0,1},{1,0},{2,3},{3,2},{4,5},{5,4},{6,7},{7,6},{8,9},{9,8},{10,11... | collective-permute-start | bytes 552968 | tf_op jit(solution)/shard_map/ppermute | solution.py:801
  11.0 0.9 %copy-start.5 = (f32[128,3]{0,1:T(4,128)S(1)}, f32[128,3]{0,1:T(4,128)}, u32[]{:S(2)}) copy-start(f32[128,3]{0,1:T(4,128)} %param.16) | copy-start | bytes 4612
  11.0 0.9 %copy-start.6 = (s32[128,2]{0,1:T(2,128)S(1)}, s32[128,2]{0,1:T(2,128)}, u32[]{:S(2)}) copy-start(s32[128,2]{0,1:T(2,128)} %param.13) | copy-start | bytes 3076
  11.0 0.9 %copy-start.7 = (s32[128,1]{0,1:T(1,128)S(1)}, s32[128,1]{0,1:T(1,128)}, u32[]{:S(2)}) copy-start(s32[128,1]{0,1:T(1,128)} %param.14) | copy-start | bytes 1540
  11.0 0.9 %copy-start.8 = (s32[128]{0:T(128)S(1)}, s32[128]{0:T(128)}, u32[]{:S(2)}) copy-start(s32[128]{0:T(128)} %param.15) | copy-start | bytes 1540
  13.0 2.0 %collective-permute-start.3 = (bf16[384,128]{1,0:T(8,128)(2,1)S(1)}, bf16[384,128]{1,0:T(8,128)(2,1)S(1)}, u32[]{:S(2)}, u32[]{:S(2)}) collective-permute-start(bf16[384,128]{1,0:T(8,128)(2,1)S(1)} %get-tuple-element.74), channel_id=1, source_target_pairs={{0,1},{1,0},{2,3},{3,2},{4,5},{5,4},{6,7},{7,6},{8,9},{9,8},{10,11... | collective-permute-start | bytes 294920 | tf_op jit(solution)/shard_map/ppermute | solution.py:836
  13.1 4.7 %collective-permute-start.2 = (bf16[400,128]{1,0:T(8,128)(2,1)S(1)}, bf16[400,128]{1,0:T(8,128)(2,1)S(1)}, u32[]{:S(2)}, u32[]{:S(2)}) collective-permute-start(bf16[400,128]{1,0:T(8,128)(2,1)S(1)} %pass.1), channel_id=1, source_target_pairs={{0,8},{1,2},{2,1},{3,11},{4,12},{5,6},{6,5},{7,15},{8,0},{9,10},{1... | collective-permute-start | bytes 307208 | tf_op jit(solution)/shard_map/ppermute | solution.py:837
  15.1 3.1 %collective-permute-start.6 = (f32[8,128]{1,0:T(8,128)S(1)}, f32[8,128]{1,0:T(8,128)S(1)}, u32[]{:S(2)}, u32[]{:S(2)}) collective-permute-start(f32[8,128]{1,0:T(8,128)S(1)} %add.3.pair), channel_id=1, source_target_pairs={{0,3},{1,2},{2,1},{3,0},{4,7},{5,6},{6,5},{7,4},{8,11},{9,10},{10,... | collective-permute-start | bytes 12296 | tf_op jit(solution)/shard_map/ppermute | solution.py:853

commit v7 on v6

--- a/solution.py
+++ b/solution.py
@@ -508,30 +508,32 @@
         store(pl.ds(base + v * VREG, VREG), a + grown * a + transfer)
 
 
-def beyond_kernel(sz, raw_a, raw_b, moves, sea, plain, far_near, wide):
-    base_a = jnp.where(is_even(), sz.bands + reach, 0)
-    base_b = sz.bands + reach - base_a
-    below, above = band_ratio(sz, -reach, True), band_ratio(sz, sz.bands, True)
-
-    for raw, first, inverse in (
-        (raw_a, base_a, jnp.where(is_even(), above, below)),
-        (raw_b, base_b, jnp.where(is_even(), below, above)),
-    ):
-        wide[...] = raw[...].astype(F32)
-
-        def transport(k, r, first=first):
-            base = pl.multiple_of(k * sz.ring, VREG)
-            for v in range(sz.vregs):
-                moved = transported(sz, wide, base, v, moves, speed_coef * r)
-                plain[first + k, pl.ds(v * VREG, VREG), :] = sea[...] * moved
-
-        over_bands(reach, inverse, transport, True)
-
+def transport_raw(sz, raw, moves, sea, plain, wide, upper):
+    base = jnp.where(upper, sz.bands + reach, 0)
+    inverse = jnp.where(upper, band_ratio(sz, sz.bands, True), band_ratio(sz, -reach, True))
+    wide[...] = raw[...].astype(F32)
+
+    def transport(k, r):
+        start = pl.multiple_of(k * sz.ring, VREG)
+        for v in range(sz.vregs):
+            moved = transported(sz, wide, start, v, moves, speed_coef * r)
+            plain[base + k, pl.ds(v * VREG, VREG), :] = sea[...] * moved
+
+    over_bands(reach, inverse, transport, True)
+
+
+def beside_kernel(sz, raw_a, moves, sea, plain, wide):
+    transport_raw(sz, raw_a, moves, sea, plain, wide, is_even())
+
+
+def beyond_kernel(sz, raw_b, moves, sea, plain_in, plain, far_near, wide):
+    transport_raw(sz, raw_b, moves, sea, plain, wide, jnp.logical_not(is_even()))
     far_near[...] = jnp.zeros_like(far_near)
     for k in range(reach):
         for first, count in west_half(sz):
             start = k * sz.ring + first * sz.cols + sz.cols - 1
             far_near[pl.ds(k * sz.side + first, count), :] = wide[pl.ds(start, count, stride=sz.cols), :]
+
 
 def inner_kernel(
     sz, adv, side, recv_a, gain, plain_in, plain, turned, plus, minus, s_plain, s_plus, s_minus, num, fix
@@ -566,37 +568,13 @@
     )
 
 
-def source_kernel(
-    sz, adv, side, recv_b, pair, other, gain, moves, s_moves, sea, from_e, mix, far_near, num,
+def outer_kernel(
+    sz, adv, side, recv_b, gain, moves, s_moves, sea, from_e, far_near, num_in,
     plain_in, turned_in, plus_in, minus_in, s_plain_in, s_plus_in, s_minus_in,
-    result_hbm, msg, plain, turned, plus, minus, s_plain, s_plus, s_minus, s_out, wide, s_near, out, sems,
+    num, plain, turned, plus, minus, s_plain, s_plus, s_minus, s_num, wide, s_near,
 ):
     spec_rank = lax.axis_index("spec")
     ns = sz.side // VREG
-    total_weight = sz.angles * 0.1 * sum(ratio_step ** (k - sz.freqs // 2) for k in range(sz.freqs))
-    means = (pair[...] + other[...]) * (1.0 / total_weight)
-    mean = jnp.concatenate([means[0 : sz.cols]] * (VREG // sz.cols), axis=0)
-    s_mean = means[sz.cols : sz.cols + 1]
-
-    def write(k):
-        band = pl.ds(pl.multiple_of(k * sz.ring, VREG), sz.ring)
-        return pltpu.make_async_copy(out.at[band], result_hbm.at[band], sems.at[k])
-
-    def scale(ratio):
-        return 1.0 / (1.0 + (dissip_coef * ratio * ratio) * mean)
-
-    ready = jnp.where(is_even(), reach, 0)
-
-    def finish(i, ratio):
-        factor = scale(ratio)
-        base = pl.multiple_of((ready + i) * sz.ring, VREG)
-        for v in range(sz.vregs):
-            here = pl.ds(base + v * VREG, VREG)
-            out[here, :] = num[here, :] * factor
-        write(ready + i).start()
-
-    over_bands(sz.bands - reach, jnp.where(is_even(), band_ratio(sz, reach), band_ratio(sz, 0)), finish)
-
     base_b = jnp.where(is_even(), 0, sz.bands + reach)
     real_b = jnp.where((spec_rank == 0) | (spec_rank == sz.spec - 1), 0.0, 1.0).astype(F32)
     info = from_e[pl.ds(sz.info // 16 * 16, 32), :].astype(F32)
@@ -631,16 +609,14 @@
     s_north = info[at + 3 : at + 4] + info[at + 4 : at + 5] + info[at + 5 : at + 6]
     missing = jnp.where(is_even(), 0, sz.bands - reach)
 
-    def result(i, ratio):
-        factor = scale(ratio)
-
-        def store(rows, value):
-            out[rows, :] = value * factor
-
-        numerators(sz, missing + i, ratio, adv, gain, plus, minus, store)
-        write(missing + i).start()
-
-    over_bands(reach, jnp.where(is_even(), band_ratio(sz, 0), band_ratio(sz, sz.bands - reach)), result)
+    def store(rows, value):
+        num[rows, :] = value
+
+    over_bands(
+        reach,
+        jnp.where(is_even(), band_ratio(sz, 0), band_ratio(sz, sz.bands - reach)),
+        lambda i, r: numerators(sz, missing + i, r, adv, gain, plus, minus, store),
+    )
 
     s_gain = []
     for v in range(ns):
@@ -649,7 +625,6 @@
         s_gain.append(wind_coef * jnp.maximum(along, 0.0))
     for k in range(sz.bands):
         ratio = band_ratio(sz, k)
-        factor = 1.0 / (1.0 + (dissip_coef * ratio * ratio) * s_mean)
         for v in range(ns):
             row = (v + 1) * VREG
             here = pl.ds(row, VREG)
@@ -661,7 +636,29 @@
                 - 2.0 * (s_plus[k + 2, here, :] + s_minus[k + 2, here, :])
             )
             a = side[pl.ds(k * sz.side + v * VREG, VREG), :]
-            s_out[pl.ds(k * sz.angles + v * VREG, VREG), :] = (a + (ratio * s_gain[v]) * a + transfer) * factor
+            s_num[pl.ds(k * sz.side + v * VREG, VREG), :] = a + (ratio * s_gain[v]) * a + transfer
+
+
+def source_kernel(sz, num, s_num, pair, other, mix, out, msg, s_out):
+    total_weight = sz.angles * 0.1 * sum(ratio_step ** (k - sz.freqs // 2) for k in range(sz.freqs))
+    means = (pair[...] + other[...]) * (1.0 / total_weight)
+    mean = jnp.concatenate([means[0 : sz.cols]] * (VREG // sz.cols), axis=0)
+    s_mean = means[sz.cols : sz.cols + 1]
+
+    def finish(k, ratio):
+        factor = 1.0 / (1.0 + (dissip_coef * ratio * ratio) * mean)
+        base = pl.multiple_of(k * sz.ring, VREG)
+        for v in range(sz.vregs):
+            here = pl.ds(base + v * VREG, VREG)
+            out[here, :] = num[here, :] * factor
+
+    over_bands(sz.bands, band_ratio(sz, 0), finish)
+    for k in range(sz.bands):
+        ratio = band_ratio(sz, k)
+        factor = 1.0 / (1.0 + (dissip_coef * ratio * ratio) * s_mean)
+        for v in range(sz.side // VREG):
+            here = pl.ds(k * sz.angles + v * VREG, VREG)
+            s_out[here, :] = s_num[pl.ds(k * sz.side + v * VREG, VREG), :] * factor
 
     pad = jnp.zeros((sz.lanes - sz.bins, sz.lat), BF16)
     columns = [out[pl.ds(c, sz.bins, stride=sz.cols), :] for c in range(sz.cols)]
@@ -672,11 +669,11 @@
     about = mix[:, n : n + 128].astype(F32)
     msg[:, 0 : sz.lanes - 128] = spectra[:, : sz.lanes - 128].astype(BF16)
     msg[:, sz.lanes - 128 : sz.lanes] = (spectra[:, sz.lanes - 128 :] + about).astype(BF16)
-    for k in range(sz.bands):
-        write(k).wait()
-
-
-def blend_kernel(sz, recv, nest_adv, result_hbm, out, sems):
+
+
+def blend_kernel(sz, recv, nest_adv, spectra, global_hbm, result_hbm, out, sems):
+    writes = [pltpu.make_async_copy(spectra, global_hbm, sems.at[sz.lanes // 128])]
+    writes[0].start()
     at = sz.bins - (sz.lanes - 128)
     about = recv[:, sz.lanes - 128 :].astype(F32)
     t_col, t_row, rate = about[:, at : at + 1], about[:, at + 1 : at + 2], about[:, at + 2 : at + 3]
@@ -685,7 +682,6 @@
     relax = [jnp.where(t_col == float(c), hit, 0.0) for c in range(sz.cols)]
     kept = [1.0 - jnp.sum(r, axis=0, keepdims=True) for r in relax]
     relax = jnp.concatenate(relax, axis=1).astype(BF16)
-    writes = []
     for part, start in enumerate(range(0, sz.bins, 128)):
         count = min(128, sz.bins - start)
         added = lax.dot_general(
@@ -753,7 +749,7 @@
     for g in range(sz.grid):
         for i in range(sz.spec):
             j = i + 1 if i % 2 else i - 1
-            to = (g, j) if 0 <= j < sz.spec else ((g ^ 2) % sz.grid, i)
+            to = (g, j) if 0 <= j < sz.spec else ((g ^ 1) % sz.grid, i)
             across.append((g * sz.spec + i, to[0] * sz.spec + to[1]))
     both = ("grid", "spec")
     near_rows = [vmem(sz.thin_rows), vmem(sz.thick_rows)]
@@ -813,7 +809,13 @@
     adv, total = kernel_call(
         functools.partial(local_kernel, sz), (field, array(VREG)), 3, flops=3 * 10**10, name="local"
     )(energy, moves, sea)
-    from_e, from_w, mix, nest_inner, adv = lax.optimization_barrier((from_e, from_w, mix, nest_inner, adv))
+    band_fields = array(sz.bands + 2 * reach, sz.ring)
+    plain = kernel_call(
+        functools.partial(beside_kernel, sz), band_fields, 3, scratch=[vmem(sz.edge_rows)], flops=10**10, name="beside"
+    )(recv_raw_a, moves, sea)
+    from_e, from_w, mix, nest_inner, adv, plain = lax.optimization_barrier(
+        (from_e, from_w, mix, nest_inner, adv, plain)
+    )
 
     msg_b = kernel_call(
         functools.partial(pass_kernel, sz),
@@ -832,18 +834,18 @@
         name="edges",
     )(adv, total, energy, from_w, from_e, moves, s_moves, sea)
 
-    msg_a, msg_b = lax.optimization_barrier((msg_a, msg_b))
     recv_a = lax.ppermute(msg_a, "spec", pairs)
     recv_b = lax.ppermute(msg_b, both, across)
-    recv_a, recv_raw_a, recv_raw_b = lax.optimization_barrier((recv_a, recv_raw_a, recv_raw_b))
+    recv_a, recv_raw_b = lax.optimization_barrier((recv_a, recv_raw_b))
     plain, far_near = kernel_call(
         functools.partial(beyond_kernel, sz),
-        (array(sz.bands + 2 * reach, sz.ring), array(reach * sz.side)),
+        (band_fields, array(reach * sz.side)),
         4,
         scratch=[vmem(sz.edge_rows)],
+        aliases={3: 0},
         flops=3 * 10**10,
         name="beyond",
-    )(recv_raw_a, recv_raw_b, moves, sea)
+    )(recv_raw_b, moves, sea, plain)
     pieces = recv_a[sz.sum_row : sz.sum_row + 3 * VREG].astype(F32)
     pair = part + pieces.reshape(3, VREG, sz.lat).sum(axis=0)
     other = jnp.zeros_like(pair)
@@ -881,25 +883,31 @@
         name="inner",
     )(adv, side, recv_a, gain, plain)
     nest_adv, recv_b = lax.optimization_barrier((nest_adv, recv_b))
-    global_next, msg, *_ = kernel_call(
+    num, *_, s_num = kernel_call(
+        functools.partial(outer_kernel, sz),
+        (field,) + arrays + (array(sz.bands * sz.side),),
+        10 + len(arrays),
+        scratch=[vmem(sz.pass_rows), vmem(reach * sz.side)],
+        aliases={9 + i: i for i in range(1 + len(arrays))},
+        name="outer",
+    )(adv, side, recv_b, gain, moves, s_moves, sea, from_e, far_near, num, *inner)
+    spectra, msg = kernel_call(
         functools.partial(source_kernel, sz),
-        (field, jax.ShapeDtypeStruct((sz.slots, sz.lanes), BF16)) + arrays,
-        13 + len(arrays),
-        scratch=[vmem(sz.bins + VREG), vmem(sz.pass_rows), vmem(reach * sz.side), vmem(sz.rows), pltpu.SemaphoreType.DMA((sz.bands,))],
-        out_hbm=(0,),
-        aliases={13 + i: 2 + i for i in range(len(arrays))},
+        (field, jax.ShapeDtypeStruct((sz.slots, sz.lanes), BF16)),
+        5,
+        scratch=[vmem(sz.bins + VREG)],
         name="sources",
-    )(adv, side, recv_b, pair, other, gain, moves, s_moves, sea, from_e, mix, far_near, num, *inner)
+    )(num, s_num, pair, other, mix)
 
     recv = lax.all_to_all(msg, "grid", split_axis=0, concat_axis=0, tiled=True)
-    nest_next = kernel_call(
+    global_next, nest_next = kernel_call(
         functools.partial(blend_kernel, sz),
-        field,
-        2,
-        out_hbm=(0,),
-        scratch=[vmem(sz.rows), pltpu.SemaphoreType.DMA((sz.lanes // 128,))],
+        (field, field),
+        3,
+        out_hbm=(0, 1),
+        scratch=[vmem(sz.rows), pltpu.SemaphoreType.DMA((sz.lanes // 128 + 1,))],
         name="blend",
-    )(recv, nest_adv)
+    )(recv, nest_adv, pltpu.with_memory_space_constraint(spectra, pltpu.VMEM))
     full = (sz.bands, sz.angles, sz.cols, sz.lat)
     return global_next.reshape(full), nest_next.reshape(full)
 

time: 34.4 us -> 34.2 us (level)
  starting transfers between devices: 10.2 us -> 9.31 us
  waiting for transfers between devices: 1.11 us -> 1.83 us
    ppermute x1, starting transfers between devices: 1.3 us -> 0.46 us  [per_device(): recv_b = lax.ppermute(msg_b, both, across)]
    ppermute x1, waiting for transfers between devices: 0.49 us -> 1.15 us  [per_device(): lax.ppermute(raw_b, 'spec', [(i, (i + 1 if i % 2 else i - 1) % sz.spec) f...]
    ppermute x1, waiting for transfers between devices: 0.01 us -> 0.66 us  [per_device(): recv_b = lax.ppermute(msg_b, both, across)]
    pallas_call x4 -> x5, Pallas kernels: 2.83 us -> 2.62 us  [in_place(): return call(*[pin(a) if i in aliases else a for i, a in enumerate(args)])]
    pallas_call x2 -> x3, Pallas kernels: 2.24 us -> 2.3 us  [the longest x1 1.27 us: per_device(): kernel_call(functools.partial(blend_kernel, sz), (field, field), 3, out_h...]
  transfers between devices with their start and end apart: 7 -> 7, of which waited for: 3 -> 2; matrix products, arithmetic and copies ran while one was open for 0% -> 0% of each run, Pallas kernels for 14% -> 16%
where the time goes in v7:
time: 34.2 us; the launch traced here: 34 us
  blocking collectives  13.4 us (39%)
  starting transfers between devices  9.31 us (27%)
  Pallas kernels  8.6 us (25%)
  waiting for transfers between devices  1.83 us (5%)
  between operations  0.86 us (3%)
    all_to_all x1, blocking collectives, per_device(): recv = lax.all_to_all(msg, 'grid', split_axis=0, concat_axis=0, tiled=True)  13.4 us
    ppermute x1, starting transfers between devices, per_device(): from_e = lax.ppermute(thick, 'grid', down)  3.1 us
    ppermute x1, starting transfers between devices, per_device(): from_w = lax.ppermute(thin, 'grid', up)  3.02 us
    pallas_call x5, Pallas kernels, in_place(): return call(*[pin(a) if i in aliases else a for i, a in enumerate(args)])  2.62 us
    pallas_call x1, Pallas kernels, per_device(): kernel_call(functools.partial(pack_kernel, sz), (half(sz.thin_rows), half...  1.31 us
    pallas_call x1, Pallas kernels, per_device(): kernel_call(functools.partial(blend_kernel, sz), (field, field), 3, out_h...  1.27 us
    ppermute x1, waiting for transfers between devices, per_device(): lax.ppermute(raw_b, 'spec', [(i, (i + 1 if i % 2 else i - 1) % sz.spec) f...  1.15 us
    ppermute x1, starting transfers between devices, per_device(): recv_raw_a = lax.ppermute(raw_a, 'spec', pairs)  1.06 us
  transfers between devices with their start and end apart: 7, of which 2 were waited for; matrix products, arithmetic and copies ran while one was open for 0% of the time, Pallas kernels for 16%

profile of v7, /device:TPU:0, one launch (start us, length us, event | category | flops | bytes accessed | tf_op | source)
XLA Modules:
  0.0 34.0 jit_solution(16716924814924386322)
XLA Ops:
  0.6 0.0 copy-start.3
  0.6 0.0 copy-start.4
  0.7 0.0 copy-start.1
  0.7 0.0 copy-start
  0.7 0.0 copy-start.2
  0.7 1.3 %pack.1 = (bf16[336,128]{1,0:T(8,128)(2,1)S(1)}, bf16[672,128]{1,0:T(8,128)(2,1)S(1)}) custom-call(f32[9,36,4,128]{3,2,1,0:T(4,128)} %energy.1, f32[9,36,4,128]{3,2,1,0:T(4,128)} %nest.2, s32[4,128]{1,0:T(4,128)} %mask.3, f32[2,4,128]{2,1,0:T(4,128)} %wind.3), custom_call_target="tpu_custom_call" | custom-call | tf_op jit(solution)/shard_map/pack/pallas_call | solution.py:761
  2.0 3.0 %collective-permute-start.1 = (bf16[336,128]{1,0:T(8,128)(2,1)S(1)}, bf16[336,128]{1,0:T(8,128)(2,1)S(1)}, u32[]{:S(2)}, u32[]{:S(2)}) collective-permute-start(bf16[336,128]{1,0:T(8,128)(2,1)S(1)} %get-tuple-element.51), channel_id=1, source_target_pairs={{0,4},{4,8},{8,12},{12,16},{16,20},{20,24},{24,28},{28,0},{1,5},{5... | collective-permute-start | bytes 258056 | tf_op jit(solution)/shard_map/ppermute | solution.py:782
  5.0 3.1 %collective-permute-start = (bf16[672,128]{1,0:T(8,128)(2,1)S(1)}, bf16[672,128]{1,0:T(8,128)(2,1)S(1)}, u32[]{:S(2)}, u32[]{:S(2)}) collective-permute-start(bf16[672,128]{1,0:T(8,128)(2,1)S(1)} %get-tuple-element.50), channel_id=1, source_target_pairs={{4,0},{8,4},{12,8},{16,12},{20,16},{24,20},{28,24},{0,28},{5,1},{9... | collective-permute-start | bytes 516104 | tf_op jit(solution)/shard_map/ppermute | solution.py:781
  8.1 0.0 copy-done
  8.2 0.7 %collective-permute-start.5 = (bf16[720,128]{1,0:T(8,128)(2,1)S(1)}, bf16[720,128]{1,0:T(8,128)(2,1)S(1)}, u32[]{:S(2)}, u32[]{:S(2)}) collective-permute-start(bf16[720,128]{1,0:T(8,128)(2,1)S(1)} %get-tuple-element.75), channel_id=1, source_target_pairs={{0,3},{1,2},{2,1},{3,0},{4,7},{5,6},{6,5},{7,4},{8,11},{9,10},{10,... | collective-permute-start | bytes 552968 | tf_op jit(solution)/shard_map/ppermute | solution.py:796
  8.9 1.1 %collective-permute-start.2 = (bf16[720,128]{1,0:T(8,128)(2,1)S(1)}, bf16[720,128]{1,0:T(8,128)(2,1)S(1)}, u32[]{:S(2)}, u32[]{:S(2)}) collective-permute-start(bf16[720,128]{1,0:T(8,128)(2,1)S(1)} %get-tuple-element.54), channel_id=1, source_target_pairs={{0,1},{1,0},{2,3},{3,2},{4,5},{5,4},{6,7},{7,6},{8,9},{9,8},{10,11... | collective-permute-start | bytes 552968 | tf_op jit(solution)/shard_map/ppermute | solution.py:797
  9.9 0.0 copy-done.3
  9.9 0.0 copy-done.4
  9.9 0.0 copy-done.2
  9.9 0.2 setup.1
  10.1 0.0 copy-done.1
  10.1 0.8 %nest.3.inner = f32[1296,128]{1,0:T(8,128)S(1)} custom-call(f32[1296,128]{1,0:T(8,128)S(1)} %bitcast.17, f32[3,144,128]{2,1,0:T(8,128)S(1)} %get-tuple-element.59.moves), custom_call_target="tpu_custom_call" | custom-call | flops 30000001024 | tf_op jit(solution)/shard_map/nest/pallas_call | solution.py:807
  11.0 0.0 copy-start.5
  11.0 0.0 copy-start.6
  11.0 0.0 copy-start.7
  11.0 0.0 copy-start.8
  11.0 0.9 %local.1 = (f32[1296,128]{1,0:T(8,128)S(1)}, f32[8,128]{1,0:T(8,128)S(1)}) custom-call(f32[1296,128]{1,0:T(8,128)S(1)} %bitcast.14, f32[3,144,128]{2,1,0:T(8,128)S(1)} %get-tuple-element.60.moves, f32[8,128]{1,0:T(8,128)S(1)} %get-tuple-element.61.sea), custom_call_target="tpu_custom_call" | custom-call | flops 30000001024 | tf_op jit(solution)/shard_map/local/pallas_call | solution.py:809
  11.9 0.0 copy-done.5
  11.9 0.0 copy-done.6
  11.9 0.0 copy-done.7
  11.9 0.0 copy-done.8
  11.9 0.4 %rim.1.mix = bf16[256,768]{1,0:T(8,128)(2,1)S(1)} custom-call(s32[2,128]{1,0:T(2,128)S(1)} %bitcast.20, s32[1,128]{1,0:T(1,128)S(1)} %bitcast.21, s32[1,128]{1,0:T(1,128)S(1)} %bitcast.22, f32[3,128]{1,0:T(4,128)S(1)} %bitcast.19), custom_call_target="tpu_custom_call" | custom-call | tf_op jit(solution)/shard_map/rim/pallas_call | solution.py:800
  12.3 0.0 collective-permute-done.2.raw_a
  12.4 0.5 %beside.1.plain_in = f32[19,144,128]{2,1,0:T(8,128)S(1)} custom-call(bf16[720,128]{1,0:T(8,128)(2,1)S(1)} %collective-permute-done.2.raw_a, f32[3,144,128]{2,1,0:T(8,128)S(1)} %get-tuple-element.60.moves, f32[8,128]{1,0:T(8,128)S(1)} %get-tuple-element.61.sea), custom_call_target="tpu_custom_call" | custom-call | flops 10000000000 | tf_op jit(solution)/shard_map/beside/pallas_call | solution.py:813
  12.9 0.0 collective-permute-done.1.from_w
  12.9 0.0 collective-permute-done.from_e
  12.9 0.3 edges.1
  13.2 0.1 collective-permute-start.4
  13.2 0.1 pass.1
  13.3 0.5 %collective-permute-start.3 = (bf16[400,128]{1,0:T(8,128)(2,1)S(1)}, bf16[400,128]{1,0:T(8,128)(2,1)S(1)}, u32[]{:S(2)}, u32[]{:S(2)}) collective-permute-start(bf16[400,128]{1,0:T(8,128)(2,1)S(1)} %pass.1), channel_id=1, source_target_pairs={{0,4},{1,2},{2,1},{3,7},{4,0},{5,6},{6,5},{7,3},{8,12},{9,10},{10,... | collective-permute-start | bytes 307208 | tf_op jit(solution)/shard_map/ppermute | solution.py:838
  13.8 0.1 nest_edge.1
  13.9 1.2 %collective-permute-done.5.raw_b = bf16[720,128]{1,0:T(8,128)(2,1)S(1)} collective-permute-done((bf16[720,128]{1,0:T(8,128)(2,1)S(1)}, bf16[720,128]{1,0:T(8,128)(2,1)S(1)}, u32[]{:S(2)}, u32[]{:S(2)}) %collective-permute-start.5) | collective-permute-done | bytes 184352 | tf_op jit(solution)/shard_map/ppermute | solution.py:796
  15.0 0.0 collective-permute-done.4.recv_a
  15.0 0.9 %collective-permute-start.6 = (f32[8,128]{1,0:T(8,128)S(1)}, f32[8,128]{1,0:T(8,128)S(1)}, u32[]{:S(2)}, u32[]{:S(2)}) collective-permute-start(f32[8,128]{1,0:T(8,128)S(1)} %add.3.pair), channel_id=1, source_target_pairs={{0,3},{1,2},{2,1},{3,0},{4,7},{5,6},{6,5},{7,4},{8,11},{9,10},{10,... | collective-permute-start | bytes 12296 | tf_op jit(solution)/shard_map/ppermute | solution.py:855
  15.9 0.5 %beyond.1 = (f32[19,144,128]{2,1,0:T(8,128)S(1)}, f32[200,128]{1,0:T(8,128)S(1)}) custom-call(bf16[720,128]{1,0:T(8,128)(2,1)S(1)} %collective-permute-done.5.raw_b, f32[3,144,128]{2,1,0:T(8,128)S(1)} %get-tuple-element.60.moves, f32[8,128]{1,0:T(8,128)S(1)} %get-tuple-element.61.sea, ...), custom_call_target="tpu_custom_call", output_to_operand_aliasing={{0}: (3, {})} | custom-call | flops 30000001024 | tf_op jit(solution)/shard_map/beyond/pallas_call | solution.py:723
  16.4 0.9 %inner.1 = (f32[19,144,128]{2,1,0:T(8,128)S(1)}, f32[19,168,128]{2,1,0:T(8,128)S(1)}, f32[14,168,128]{2,1,0:T(8,128)S(1)}, f32[14,168,128]{2,1,0:T(8,128)S(1)}, ...) custom-call(f32[1296,128]{1,0:T(8,128)S(1)} %get-tuple-element.68.ad, ...), custom_call_target="tpu_custom_call", output_to_operand_aliasing={{0}: (4, {})} | custom-call | tf_op jit(solution)/shard_map/inner/pallas_call | solution.py:723
  17.4 0.7 %collective-permute-done.3.recv_b = bf16[400,128]{1,0:T(8,128)(2,1)S(1)} collective-permute-done((bf16[400,128]{1,0:T(8,128)(2,1)S(1)}, bf16[400,128]{1,0:T(8,128)(2,1)S(1)}, u32[]{:S(2)}, u32[]{:S(2)}) %collective-permute-start.3) | collective-permute-done | bytes 102432 | tf_op jit(solution)/shard_map/ppermute | solution.py:838
  18.0 0.8 %outer.1 = (f32[1296,128]{1,0:T(8,128)S(1)}, f32[19,144,128]{2,1,0:T(8,128)S(1)}, f32[19,168,128]{2,1,0:T(8,128)S(1)}, f32[14,168,128]{2,1,0:T(8,128)S(1)}, f32[...) custom-call(f32[1296,128]{1,0:T(8,128)S(1)} %get-tuple-element.68.ad, ...), custom_call_target="tpu_custom_call", output_to_operand_aliasing={{0}: (9, {}), {1}: (10, {}), {2}: (11, {}), {3}: (12, {}), ... | custom-call | tf_op jit(solution)/shard_map/outer/pallas_call | solution.py:723
  18.8 0.0 collective-permute-done.6.other
  18.8 0.5 %sources.1 = (f32[1296,128]{1,0:T(8,128)S(1)}, bf16[256,384]{1,0:T(8,128)(2,1)S(1)}) custom-call(f32[1296,128]{1,0:T(8,128)S(1)} %get-tuple-element.89.num, f32[360,128]{1,0:T(8,128)S(1)} %get-tuple-element.90.s_num, f32[8,128]{1,0:T(8,128)S(1)} %add.3.pair, f32[8,128]{1,0:T(8,128)S(1)} %collective-permute-done.6.other, bf16[256,768]{1,0:T(8,128)(2,1)S(1)} %rim.1.mix), custom_call_target="tpu_custom_call" | custom-call | tf_op jit(solution)/shard_map/sources/pallas_call | solution.py:894
  19.4 13.4 %all_to_all.11 = bf16[8,32,384]{2,1,0:T(8,128)(2,1)S(1)} all-to-all(bf16[8,32,384]{2,1,0:T(8,128)(2,1)S(1)} %bitcast.18), channel_id=1, replica_groups=mesh['grid'=8,'spec'=4] {'grid'}, dimensions={0} | all-to-all | bytes 393216 | tf_op jit(solution)/shard_map/all_to_all | solution.py:902
  32.7 1.3 %blend.1 = (f32[1296,128]{1,0:T(8,128)}, f32[1296,128]{1,0:T(8,128)}) custom-call(bf16[256,384]{1,0:T(8,128)(2,1)S(1)} %bitcast.16, f32[4,332,128]{2,1,0:T(8,128)S(1)} %get-tuple-element.94.nest_adv, f32[1296,128]{1,0:T(8,128)S(1)} %get-tuple-element.95.spectra), custom_call_target="tpu_custom_call" | custom-call | tf_op jit(solution)/shard_map/blend/pallas_call | solution.py:903
  (3 shorter events, 0.0 us)
Async XLA Ops:
  0.6 9.3 %copy-start.3 = (f32[2,4,128]{2,1,0:T(4,128)S(1)}, f32[2,4,128]{2,1,0:T(4,128)}, u32[]{:S(2)}) copy-start(f32[2,4,128]{2,1,0:T(4,128)} %wind.3) | copy-start | bytes 12292
  0.6 9.3 %copy-start.4 = (s32[4,128]{1,0:T(4,128)S(1)}, s32[4,128]{1,0:T(4,128)}, u32[]{:S(2)}) copy-start(s32[4,128]{1,0:T(4,128)} %mask.3) | copy-start | bytes 6148
  0.7 9.5 %copy-start.1 = (f32[9,36,4,128]{3,2,1,0:T(4,128)S(1)}, f32[9,36,4,128]{3,2,1,0:T(4,128)}, u32[]{:S(2)}) copy-start(f32[9,36,4,128]{3,2,1,0:T(4,128)} %nest.2) | copy-start | bytes 1990660
  0.7 7.5 %copy-start = (f32[9,36,4,128]{3,2,1,0:T(4,128)S(1)}, f32[9,36,4,128]{3,2,1,0:T(4,128)}, u32[]{:S(2)}) copy-start(f32[9,36,4,128]{3,2,1,0:T(4,128)} %energy.1) | copy-start | bytes 1990660
  0.7 9.3 %copy-start.2 = (f32[192,128]{1,0:T(8,128)S(1)}, f32[192,128]{1,0:T(8,128)}, u32[]{:S(2)}) copy-start(f32[192,128]{1,0:T(8,128)} %constant.4.clone.table) | copy-start | bytes 294916
  2.0 10.9 %collective-permute-start.1 = (bf16[336,128]{1,0:T(8,128)(2,1)S(1)}, bf16[336,128]{1,0:T(8,128)(2,1)S(1)}, u32[]{:S(2)}, u32[]{:S(2)}) collective-permute-start(bf16[336,128]{1,0:T(8,128)(2,1)S(1)} %get-tuple-element.51), channel_id=1, source_target_pairs={{0,4},{4,8},{8,12},{12,16},{16,20},{20,24},{24,28},{28,0},{1,5},{5... | collective-permute-start | bytes 258056 | tf_op jit(solution)/shard_map/ppermute | solution.py:782
  5.0 7.9 %collective-permute-start = (bf16[672,128]{1,0:T(8,128)(2,1)S(1)}, bf16[672,128]{1,0:T(8,128)(2,1)S(1)}, u32[]{:S(2)}, u32[]{:S(2)}) collective-permute-start(bf16[672,128]{1,0:T(8,128)(2,1)S(1)} %get-tuple-element.50), channel_id=1, source_target_pairs={{4,0},{8,4},{12,8},{16,12},{20,16},{24,20},{28,24},{0,28},{5,1},{9... | collective-permute-start | bytes 516104 | tf_op jit(solution)/shard_map/ppermute | solution.py:781
  8.2 6.9 %collective-permute-start.5 = (bf16[720,128]{1,0:T(8,128)(2,1)S(1)}, bf16[720,128]{1,0:T(8,128)(2,1)S(1)}, u32[]{:S(2)}, u32[]{:S(2)}) collective-permute-start(bf16[720,128]{1,0:T(8,128)(2,1)S(1)} %get-tuple-element.75), channel_id=1, source_target_pairs={{0,3},{1,2},{2,1},{3,0},{4,7},{5,6},{6,5},{7,4},{8,11},{9,10},{10,... | collective-permute-start | bytes 552968 | tf_op jit(solution)/shard_map/ppermute | solution.py:796
  8.9 3.5 %collective-permute-start.2 = (bf16[720,128]{1,0:T(8,128)(2,1)S(1)}, bf16[720,128]{1,0:T(8,128)(2,1)S(1)}, u32[]{:S(2)}, u32[]{:S(2)}) collective-permute-start(bf16[720,128]{1,0:T(8,128)(2,1)S(1)} %get-tuple-element.54), channel_id=1, source_target_pairs={{0,1},{1,0},{2,3},{3,2},{4,5},{5,4},{6,7},{7,6},{8,9},{9,8},{10,11... | collective-permute-start | bytes 552968 | tf_op jit(solution)/shard_map/ppermute | solution.py:797
  11.0 0.9 %copy-start.5 = (f32[128,3]{0,1:T(4,128)S(1)}, f32[128,3]{0,1:T(4,128)}, u32[]{:S(2)}) copy-start(f32[128,3]{0,1:T(4,128)} %param.16) | copy-start | bytes 4612
  11.0 0.9 %copy-start.6 = (s32[128,2]{0,1:T(2,128)S(1)}, s32[128,2]{0,1:T(2,128)}, u32[]{:S(2)}) copy-start(s32[128,2]{0,1:T(2,128)} %param.13) | copy-start | bytes 3076
  11.0 0.9 %copy-start.7 = (s32[128,1]{0,1:T(1,128)S(1)}, s32[128,1]{0,1:T(1,128)}, u32[]{:S(2)}) copy-start(s32[128,1]{0,1:T(1,128)} %param.14) | copy-start | bytes 1540
  11.0 0.9 %copy-start.8 = (s32[128]{0:T(128)S(1)}, s32[128]{0:T(128)}, u32[]{:S(2)}) copy-start(s32[128]{0:T(128)} %param.15) | copy-start | bytes 1540
  13.2 1.9 %collective-permute-start.4 = (bf16[384,128]{1,0:T(8,128)(2,1)S(1)}, bf16[384,128]{1,0:T(8,128)(2,1)S(1)}, u32[]{:S(2)}, u32[]{:S(2)}) collective-permute-start(bf16[384,128]{1,0:T(8,128)(2,1)S(1)} %get-tuple-element.74), channel_id=1, source_target_pairs={{0,1},{1,0},{2,3},{3,2},{4,5},{5,4},{6,7},{7,6},{8,9},{9,8},{10,11... | collective-permute-start | bytes 294920 | tf_op jit(solution)/shard_map/ppermute | solution.py:837
  13.3 4.7 %collective-permute-start.3 = (bf16[400,128]{1,0:T(8,128)(2,1)S(1)}, bf16[400,128]{1,0:T(8,128)(2,1)S(1)}, u32[]{:S(2)}, u32[]{:S(2)}) collective-permute-start(bf16[400,128]{1,0:T(8,128)(2,1)S(1)} %pass.1), channel_id=1, source_target_pairs={{0,4},{1,2},{2,1},{3,7},{4,0},{5,6},{6,5},{7,3},{8,12},{9,10},{10,... | collective-permute-start | bytes 307208 | tf_op jit(solution)/shard_map/ppermute | solution.py:838
  15.0 3.8 %collective-permute-start.6 = (f32[8,128]{1,0:T(8,128)S(1)}, f32[8,128]{1,0:T(8,128)S(1)}, u32[]{:S(2)}, u32[]{:S(2)}) collective-permute-start(f32[8,128]{1,0:T(8,128)S(1)} %add.3.pair), channel_id=1, source_target_pairs={{0,3},{1,2},{2,1},{3,0},{4,7},{5,6},{6,5},{7,4},{8,11},{9,10},{10,... | collective-permute-start | bytes 12296 | tf_op jit(solution)/shard_map/ppermute | solution.py:855

commit v8 on v7

--- a/solution.py
+++ b/solution.py
@@ -855,15 +855,6 @@
         other = lax.ppermute(pair, "spec", [(i, i ^ (2 * step - 1)) for i in range(sz.spec)])
         step *= 2
 
-    _, nest_adv = kernel_call(
-        functools.partial(nest_edge_kernel, sz),
-        (field, array(sz.cols, sz.bins + VREG)),
-        4,
-        scratch=near_rows,
-        aliases={0: 0},
-        name="nest_edge",
-    )(nest_inner, from_w, from_e, nest_moves)
-
     padded, centres, turns = sz.bands + 2 * reach, sz.bands + reach, sz.ring + 3 * VREG
     arrays = (
         array(padded, sz.ring),
@@ -882,6 +873,15 @@
         aliases={4: 0},
         name="inner",
     )(adv, side, recv_a, gain, plain)
+    nest_inner, num = lax.optimization_barrier((nest_inner, num))
+    _, nest_adv = kernel_call(
+        functools.partial(nest_edge_kernel, sz),
+        (field, array(sz.cols, sz.bins + VREG)),
+        4,
+        scratch=near_rows,
+        aliases={0: 0},
+        name="nest_edge",
+    )(nest_inner, from_w, from_e, nest_moves)
     nest_adv, recv_b = lax.optimization_barrier((nest_adv, recv_b))
     num, *_, s_num = kernel_call(
         functools.partial(outer_kernel, sz),

time: 34.2 us -> 34.2 us (level)
  no operation moved by 1% of the time
where the time goes in v8:
time: 34.2 us; the launch traced here: 34 us
  blocking collectives  13.4 us (39%)
  starting transfers between devices  9.31 us (27%)
  Pallas kernels  8.6 us (25%)
  waiting for transfers between devices  1.82 us (5%)
  between operations  0.86 us (3%)
    all_to_all x1, blocking collectives, per_device(): recv = lax.all_to_all(msg, 'grid', split_axis=0, concat_axis=0, tiled=True)  13.4 us
    ppermute x1, starting transfers between devices, per_device(): from_e = lax.ppermute(thick, 'grid', down)  3.1 us
    ppermute x1, starting transfers between devices, per_device(): from_w = lax.ppermute(thin, 'grid', up)  3.02 us
    pallas_call x5, Pallas kernels, in_place(): return call(*[pin(a) if i in aliases else a for i, a in enumerate(args)])  2.63 us
    pallas_call x1, Pallas kernels, per_device(): kernel_call(functools.partial(pack_kernel, sz), (half(sz.thin_rows), half...  1.31 us
    pallas_call x1, Pallas kernels, per_device(): kernel_call(functools.partial(blend_kernel, sz), (field, field), 3, out_h...  1.27 us
    ppermute x1, waiting for transfers between devices, per_device(): lax.ppermute(raw_b, 'spec', [(i, (i + 1 if i % 2 else i - 1) % sz.spec) f...  1.26 us
    ppermute x1, starting transfers between devices, per_device(): recv_raw_a = lax.ppermute(raw_a, 'spec', pairs)  1.06 us
  transfers between devices with their start and end apart: 7, of which 2 were waited for; matrix products, arithmetic and copies ran while one was open for 0% of the time, Pallas kernels for 16%

profile of v8, /device:TPU:0, one launch (start us, length us, event | category | flops | bytes accessed | tf_op | source)
XLA Modules:
  0.0 34.0 jit_solution(5997154247553076307)
XLA Ops:
  0.6 0.0 copy-start.3
  0.6 0.0 copy-start.4
  0.7 0.0 copy-start.1
  0.7 0.0 copy-start
  0.7 0.0 copy-start.2
  0.7 1.3 %pack.1 = (bf16[336,128]{1,0:T(8,128)(2,1)S(1)}, bf16[672,128]{1,0:T(8,128)(2,1)S(1)}) custom-call(f32[9,36,4,128]{3,2,1,0:T(4,128)} %energy.1, f32[9,36,4,128]{3,2,1,0:T(4,128)} %nest.2, s32[4,128]{1,0:T(4,128)} %mask.3, f32[2,4,128]{2,1,0:T(4,128)} %wind.3), custom_call_target="tpu_custom_call" | custom-call | tf_op jit(solution)/shard_map/pack/pallas_call | solution.py:761
  2.0 3.0 %collective-permute-start.1 = (bf16[336,128]{1,0:T(8,128)(2,1)S(1)}, bf16[336,128]{1,0:T(8,128)(2,1)S(1)}, u32[]{:S(2)}, u32[]{:S(2)}) collective-permute-start(bf16[336,128]{1,0:T(8,128)(2,1)S(1)} %get-tuple-element.53), channel_id=1, source_target_pairs={{0,4},{4,8},{8,12},{12,16},{16,20},{20,24},{24,28},{28,0},{1,5},{5... | collective-permute-start | bytes 258056 | tf_op jit(solution)/shard_map/ppermute | solution.py:782
  5.0 3.1 %collective-permute-start = (bf16[672,128]{1,0:T(8,128)(2,1)S(1)}, bf16[672,128]{1,0:T(8,128)(2,1)S(1)}, u32[]{:S(2)}, u32[]{:S(2)}) collective-permute-start(bf16[672,128]{1,0:T(8,128)(2,1)S(1)} %get-tuple-element.52), channel_id=1, source_target_pairs={{4,0},{8,4},{12,8},{16,12},{20,16},{24,20},{28,24},{0,28},{5,1},{9... | collective-permute-start | bytes 516104 | tf_op jit(solution)/shard_map/ppermute | solution.py:781
  8.1 0.0 copy-done
  8.2 0.7 %collective-permute-start.4 = (bf16[720,128]{1,0:T(8,128)(2,1)S(1)}, bf16[720,128]{1,0:T(8,128)(2,1)S(1)}, u32[]{:S(2)}, u32[]{:S(2)}) collective-permute-start(bf16[720,128]{1,0:T(8,128)(2,1)S(1)} %get-tuple-element.74), channel_id=1, source_target_pairs={{0,3},{1,2},{2,1},{3,0},{4,7},{5,6},{6,5},{7,4},{8,11},{9,10},{10,... | collective-permute-start | bytes 552968 | tf_op jit(solution)/shard_map/ppermute | solution.py:796
  8.9 1.1 %collective-permute-start.2 = (bf16[720,128]{1,0:T(8,128)(2,1)S(1)}, bf16[720,128]{1,0:T(8,128)(2,1)S(1)}, u32[]{:S(2)}, u32[]{:S(2)}) collective-permute-start(bf16[720,128]{1,0:T(8,128)(2,1)S(1)} %get-tuple-element.56), channel_id=1, source_target_pairs={{0,1},{1,0},{2,3},{3,2},{4,5},{5,4},{6,7},{7,6},{8,9},{9,8},{10,11... | collective-permute-start | bytes 552968 | tf_op jit(solution)/shard_map/ppermute | solution.py:797
  9.9 0.0 copy-done.3
  9.9 0.0 copy-done.4
  9.9 0.0 copy-done.2
  9.9 0.2 setup.1
  10.1 0.0 copy-done.1
  10.1 0.8 %nest.3.inner = f32[1296,128]{1,0:T(8,128)S(1)} custom-call(f32[1296,128]{1,0:T(8,128)S(1)} %bitcast.17, f32[3,144,128]{2,1,0:T(8,128)S(1)} %get-tuple-element.61.moves), custom_call_target="tpu_custom_call" | custom-call | flops 30000001024 | tf_op jit(solution)/shard_map/nest/pallas_call | solution.py:807
  11.0 0.0 copy-start.5
  11.0 0.0 copy-start.6
  11.0 0.0 copy-start.7
  11.0 0.0 copy-start.8
  11.0 0.9 %local.1 = (f32[1296,128]{1,0:T(8,128)S(1)}, f32[8,128]{1,0:T(8,128)S(1)}) custom-call(f32[1296,128]{1,0:T(8,128)S(1)} %bitcast.14, f32[3,144,128]{2,1,0:T(8,128)S(1)} %get-tuple-element.62.moves, f32[8,128]{1,0:T(8,128)S(1)} %get-tuple-element.63.sea), custom_call_target="tpu_custom_call" | custom-call | flops 30000001024 | tf_op jit(solution)/shard_map/local/pallas_call | solution.py:809
  11.9 0.0 copy-done.5
  11.9 0.0 copy-done.6
  11.9 0.0 copy-done.7
  11.9 0.0 copy-done.8
  11.9 0.4 %rim.1.mix = bf16[256,768]{1,0:T(8,128)(2,1)S(1)} custom-call(s32[2,128]{1,0:T(2,128)S(1)} %bitcast.20, s32[1,128]{1,0:T(1,128)S(1)} %bitcast.21, s32[1,128]{1,0:T(1,128)S(1)} %bitcast.22, f32[3,128]{1,0:T(4,128)S(1)} %bitcast.19), custom_call_target="tpu_custom_call" | custom-call | tf_op jit(solution)/shard_map/rim/pallas_call | solution.py:800
  12.3 0.0 collective-permute-done.2.raw_a
  12.4 0.5 %beside.1.plain_in = f32[19,144,128]{2,1,0:T(8,128)S(1)} custom-call(bf16[720,128]{1,0:T(8,128)(2,1)S(1)} %collective-permute-done.2.raw_a, f32[3,144,128]{2,1,0:T(8,128)S(1)} %get-tuple-element.62.moves, f32[8,128]{1,0:T(8,128)S(1)} %get-tuple-element.63.sea), custom_call_target="tpu_custom_call" | custom-call | flops 10000000000 | tf_op jit(solution)/shard_map/beside/pallas_call | solution.py:813
  12.9 0.0 collective-permute-done.1.from_w
  12.9 0.0 collective-permute-done.from_e
  12.9 0.3 edges.1
  13.2 0.1 collective-permute-start.3
  13.2 0.1 pass.1
  13.3 0.5 %collective-permute-start.5 = (bf16[400,128]{1,0:T(8,128)(2,1)S(1)}, bf16[400,128]{1,0:T(8,128)(2,1)S(1)}, u32[]{:S(2)}, u32[]{:S(2)}) collective-permute-start(bf16[400,128]{1,0:T(8,128)(2,1)S(1)} %pass.1), channel_id=1, source_target_pairs={{0,4},{1,2},{2,1},{3,7},{4,0},{5,6},{6,5},{7,3},{8,12},{9,10},{10,... | collective-permute-start | bytes 307208 | tf_op jit(solution)/shard_map/ppermute | solution.py:838
  13.8 1.3 %collective-permute-done.4.raw_b = bf16[720,128]{1,0:T(8,128)(2,1)S(1)} collective-permute-done((bf16[720,128]{1,0:T(8,128)(2,1)S(1)}, bf16[720,128]{1,0:T(8,128)(2,1)S(1)}, u32[]{:S(2)}, u32[]{:S(2)}) %collective-permute-start.4) | collective-permute-done | bytes 184352 | tf_op jit(solution)/shard_map/ppermute | solution.py:796
  15.0 0.0 collective-permute-done.3.recv_a
  15.0 0.9 %collective-permute-start.6 = (f32[8,128]{1,0:T(8,128)S(1)}, f32[8,128]{1,0:T(8,128)S(1)}, u32[]{:S(2)}, u32[]{:S(2)}) collective-permute-start(f32[8,128]{1,0:T(8,128)S(1)} %add.3.pair), channel_id=1, source_target_pairs={{0,3},{1,2},{2,1},{3,0},{4,7},{5,6},{6,5},{7,4},{8,11},{9,10},{10,... | collective-permute-start | bytes 12296 | tf_op jit(solution)/shard_map/ppermute | solution.py:855
  15.9 0.5 %beyond.1 = (f32[19,144,128]{2,1,0:T(8,128)S(1)}, f32[200,128]{1,0:T(8,128)S(1)}) custom-call(bf16[720,128]{1,0:T(8,128)(2,1)S(1)} %collective-permute-done.4.raw_b, f32[3,144,128]{2,1,0:T(8,128)S(1)} %get-tuple-element.62.moves, f32[8,128]{1,0:T(8,128)S(1)} %get-tuple-element.63.sea, ...), custom_call_target="tpu_custom_call", output_to_operand_aliasing={{0}: (3, {})} | custom-call | flops 30000001024 | tf_op jit(solution)/shard_map/beyond/pallas_call | solution.py:723
  16.4 0.9 %inner.1 = (f32[19,144,128]{2,1,0:T(8,128)S(1)}, f32[19,168,128]{2,1,0:T(8,128)S(1)}, f32[14,168,128]{2,1,0:T(8,128)S(1)}, f32[14,168,128]{2,1,0:T(8,128)S(1)}, ...) custom-call(f32[1296,128]{1,0:T(8,128)S(1)} %get-tuple-element.70.ad, ...), custom_call_target="tpu_custom_call", output_to_operand_aliasing={{0}: (4, {})} | custom-call | tf_op jit(solution)/shard_map/inner/pallas_call | solution.py:723
  17.4 0.1 nest_edge.1
  17.5 0.5 %collective-permute-done.5.recv_b = bf16[400,128]{1,0:T(8,128)(2,1)S(1)} collective-permute-done((bf16[400,128]{1,0:T(8,128)(2,1)S(1)}, bf16[400,128]{1,0:T(8,128)(2,1)S(1)}, u32[]{:S(2)}, u32[]{:S(2)}) %collective-permute-start.5) | collective-permute-done | bytes 102432 | tf_op jit(solution)/shard_map/ppermute | solution.py:838
  18.0 0.8 %outer.1 = (f32[1296,128]{1,0:T(8,128)S(1)}, f32[19,144,128]{2,1,0:T(8,128)S(1)}, f32[19,168,128]{2,1,0:T(8,128)S(1)}, f32[14,168,128]{2,1,0:T(8,128)S(1)}, f32[...) custom-call(f32[1296,128]{1,0:T(8,128)S(1)} %get-tuple-element.70.ad, ...), custom_call_target="tpu_custom_call", output_to_operand_aliasing={{0}: (9, {}), {1}: (10, {}), {2}: (11, {}), {3}: (12, {}), ... | custom-call | tf_op jit(solution)/shard_map/outer/pallas_call | solution.py:723
  18.8 0.0 collective-permute-done.6.other
  18.8 0.5 %sources.1 = (f32[1296,128]{1,0:T(8,128)S(1)}, bf16[256,384]{1,0:T(8,128)(2,1)S(1)}) custom-call(f32[1296,128]{1,0:T(8,128)S(1)} %get-tuple-element.93.num, f32[360,128]{1,0:T(8,128)S(1)} %get-tuple-element.94.s_num, f32[8,128]{1,0:T(8,128)S(1)} %add.3.pair, f32[8,128]{1,0:T(8,128)S(1)} %collective-permute-done.6.other, bf16[256,768]{1,0:T(8,128)(2,1)S(1)} %rim.1.mix), custom_call_target="tpu_custom_call" | custom-call | tf_op jit(solution)/shard_map/sources/pallas_call | solution.py:894
  19.4 13.4 %all_to_all.11 = bf16[8,32,384]{2,1,0:T(8,128)(2,1)S(1)} all-to-all(bf16[8,32,384]{2,1,0:T(8,128)(2,1)S(1)} %bitcast.18), channel_id=1, replica_groups=mesh['grid'=8,'spec'=4] {'grid'}, dimensions={0} | all-to-all | bytes 393216 | tf_op jit(solution)/shard_map/all_to_all | solution.py:902
  32.7 1.3 %blend.1 = (f32[1296,128]{1,0:T(8,128)}, f32[1296,128]{1,0:T(8,128)}) custom-call(bf16[256,384]{1,0:T(8,128)(2,1)S(1)} %bitcast.16, f32[4,332,128]{2,1,0:T(8,128)S(1)} %get-tuple-element.98.nest_adv, f32[1296,128]{1,0:T(8,128)S(1)} %get-tuple-element.99.spectra), custom_call_target="tpu_custom_call" | custom-call | tf_op jit(solution)/shard_map/blend/pallas_call | solution.py:903
  (3 shorter events, 0.0 us)
Async XLA Ops:
  0.6 9.3 %copy-start.3 = (f32[2,4,128]{2,1,0:T(4,128)S(1)}, f32[2,4,128]{2,1,0:T(4,128)}, u32[]{:S(2)}) copy-start(f32[2,4,128]{2,1,0:T(4,128)} %wind.3) | copy-start | bytes 12292
  0.6 9.3 %copy-start.4 = (s32[4,128]{1,0:T(4,128)S(1)}, s32[4,128]{1,0:T(4,128)}, u32[]{:S(2)}) copy-start(s32[4,128]{1,0:T(4,128)} %mask.3) | copy-start | bytes 6148
  0.7 9.5 %copy-start.1 = (f32[9,36,4,128]{3,2,1,0:T(4,128)S(1)}, f32[9,36,4,128]{3,2,1,0:T(4,128)}, u32[]{:S(2)}) copy-start(f32[9,36,4,128]{3,2,1,0:T(4,128)} %nest.2) | copy-start | bytes 1990660
  0.7 7.5 %copy-start = (f32[9,36,4,128]{3,2,1,0:T(4,128)S(1)}, f32[9,36,4,128]{3,2,1,0:T(4,128)}, u32[]{:S(2)}) copy-start(f32[9,36,4,128]{3,2,1,0:T(4,128)} %energy.1) | copy-start | bytes 1990660
  0.7 9.3 %copy-start.2 = (f32[192,128]{1,0:T(8,128)S(1)}, f32[192,128]{1,0:T(8,128)}, u32[]{:S(2)}) copy-start(f32[192,128]{1,0:T(8,128)} %constant.4.clone.table) | copy-start | bytes 294916
  2.0 10.9 %collective-permute-start.1 = (bf16[336,128]{1,0:T(8,128)(2,1)S(1)}, bf16[336,128]{1,0:T(8,128)(2,1)S(1)}, u32[]{:S(2)}, u32[]{:S(2)}) collective-permute-start(bf16[336,128]{1,0:T(8,128)(2,1)S(1)} %get-tuple-element.53), channel_id=1, source_target_pairs={{0,4},{4,8},{8,12},{12,16},{16,20},{20,24},{24,28},{28,0},{1,5},{5... | collective-permute-start | bytes 258056 | tf_op jit(solution)/shard_map/ppermute | solution.py:782
  5.0 7.8 %collective-permute-start = (bf16[672,128]{1,0:T(8,128)(2,1)S(1)}, bf16[672,128]{1,0:T(8,128)(2,1)S(1)}, u32[]{:S(2)}, u32[]{:S(2)}) collective-permute-start(bf16[672,128]{1,0:T(8,128)(2,1)S(1)} %get-tuple-element.52), channel_id=1, source_target_pairs={{4,0},{8,4},{12,8},{16,12},{20,16},{24,20},{28,24},{0,28},{5,1},{9... | collective-permute-start | bytes 516104 | tf_op jit(solution)/shard_map/ppermute | solution.py:781
  8.2 6.9 %collective-permute-start.4 = (bf16[720,128]{1,0:T(8,128)(2,1)S(1)}, bf16[720,128]{1,0:T(8,128)(2,1)S(1)}, u32[]{:S(2)}, u32[]{:S(2)}) collective-permute-start(bf16[720,128]{1,0:T(8,128)(2,1)S(1)} %get-tuple-element.74), channel_id=1, source_target_pairs={{0,3},{1,2},{2,1},{3,0},{4,7},{5,6},{6,5},{7,4},{8,11},{9,10},{10,... | collective-permute-start | bytes 552968 | tf_op jit(solution)/shard_map/ppermute | solution.py:796
  8.9 3.5 %collective-permute-start.2 = (bf16[720,128]{1,0:T(8,128)(2,1)S(1)}, bf16[720,128]{1,0:T(8,128)(2,1)S(1)}, u32[]{:S(2)}, u32[]{:S(2)}) collective-permute-start(bf16[720,128]{1,0:T(8,128)(2,1)S(1)} %get-tuple-element.56), channel_id=1, source_target_pairs={{0,1},{1,0},{2,3},{3,2},{4,5},{5,4},{6,7},{7,6},{8,9},{9,8},{10,11... | collective-permute-start | bytes 552968 | tf_op jit(solution)/shard_map/ppermute | solution.py:797
  11.0 0.9 %copy-start.5 = (f32[128,3]{0,1:T(4,128)S(1)}, f32[128,3]{0,1:T(4,128)}, u32[]{:S(2)}) copy-start(f32[128,3]{0,1:T(4,128)} %param.16) | copy-start | bytes 4612
  11.0 0.9 %copy-start.6 = (s32[128,2]{0,1:T(2,128)S(1)}, s32[128,2]{0,1:T(2,128)}, u32[]{:S(2)}) copy-start(s32[128,2]{0,1:T(2,128)} %param.13) | copy-start | bytes 3076
  11.0 0.9 %copy-start.7 = (s32[128,1]{0,1:T(1,128)S(1)}, s32[128,1]{0,1:T(1,128)}, u32[]{:S(2)}) copy-start(s32[128,1]{0,1:T(1,128)} %param.14) | copy-start | bytes 1540
  11.0 0.9 %copy-start.8 = (s32[128]{0:T(128)S(1)}, s32[128]{0:T(128)}, u32[]{:S(2)}) copy-start(s32[128]{0:T(128)} %param.15) | copy-start | bytes 1540
  13.2 1.9 %collective-permute-start.3 = (bf16[384,128]{1,0:T(8,128)(2,1)S(1)}, bf16[384,128]{1,0:T(8,128)(2,1)S(1)}, u32[]{:S(2)}, u32[]{:S(2)}) collective-permute-start(bf16[384,128]{1,0:T(8,128)(2,1)S(1)} %get-tuple-element.73), channel_id=1, source_target_pairs={{0,1},{1,0},{2,3},{3,2},{4,5},{5,4},{6,7},{7,6},{8,9},{9,8},{10,11... | collective-permute-start | bytes 294920 | tf_op jit(solution)/shard_map/ppermute | solution.py:837
  13.3 4.7 %collective-permute-start.5 = (bf16[400,128]{1,0:T(8,128)(2,1)S(1)}, bf16[400,128]{1,0:T(8,128)(2,1)S(1)}, u32[]{:S(2)}, u32[]{:S(2)}) collective-permute-start(bf16[400,128]{1,0:T(8,128)(2,1)S(1)} %pass.1), channel_id=1, source_target_pairs={{0,4},{1,2},{2,1},{3,7},{4,0},{5,6},{6,5},{7,3},{8,12},{9,10},{10,... | collective-permute-start | bytes 307208 | tf_op jit(solution)/shard_map/ppermute | solution.py:838
  15.0 3.8 %collective-permute-start.6 = (f32[8,128]{1,0:T(8,128)S(1)}, f32[8,128]{1,0:T(8,128)S(1)}, u32[]{:S(2)}, u32[]{:S(2)}) collective-permute-start(f32[8,128]{1,0:T(8,128)S(1)} %add.3.pair), channel_id=1, source_target_pairs={{0,3},{1,2},{2,1},{3,0},{4,7},{5,6},{6,5},{7,4},{8,11},{9,10},{10,... | collective-permute-start | bytes 12296 | tf_op jit(solution)/shard_map/ppermute | solution.py:855

commit v9 on v8

--- a/solution.py
+++ b/solution.py
@@ -508,6 +508,11 @@
         store(pl.ds(base + v * VREG, VREG), a + grown * a + transfer)
 
 
+def has_across(sz):
+    rank = lax.axis_index("spec")
+    return jnp.where((rank == 0) | (rank == sz.spec - 1), 0.0, 1.0).astype(F32)
+
+
 def transport_raw(sz, raw, moves, sea, plain, wide, upper):
     base = jnp.where(upper, sz.bands + reach, 0)
     inverse = jnp.where(upper, band_ratio(sz, sz.bands, True), band_ratio(sz, -reach, True))
@@ -517,17 +522,17 @@
         start = pl.multiple_of(k * sz.ring, VREG)
         for v in range(sz.vregs):
             moved = transported(sz, wide, start, v, moves, speed_coef * r)
-            plain[base + k, pl.ds(v * VREG, VREG), :] = sea[...] * moved
+            plain[base + k, pl.ds(v * VREG, VREG), :] = sea * moved
 
     over_bands(reach, inverse, transport, True)
 
 
 def beside_kernel(sz, raw_a, moves, sea, plain, wide):
-    transport_raw(sz, raw_a, moves, sea, plain, wide, is_even())
+    transport_raw(sz, raw_a, moves, sea[...], plain, wide, is_even())
 
 
 def beyond_kernel(sz, raw_b, moves, sea, plain_in, plain, far_near, wide):
-    transport_raw(sz, raw_b, moves, sea, plain, wide, jnp.logical_not(is_even()))
+    transport_raw(sz, raw_b, moves, sea[...] * has_across(sz), plain, wide, jnp.logical_not(is_even()))
     far_near[...] = jnp.zeros_like(far_near)
     for k in range(reach):
         for first, count in west_half(sz):
@@ -576,7 +581,7 @@
     spec_rank = lax.axis_index("spec")
     ns = sz.side // VREG
     base_b = jnp.where(is_even(), 0, sz.bands + reach)
-    real_b = jnp.where((spec_rank == 0) | (spec_rank == sz.spec - 1), 0.0, 1.0).astype(F32)
+    real_b = has_across(sz)
     info = from_e[pl.ds(sz.info // 16 * 16, 32), :].astype(F32)
     at = sz.info % 16
     s_sea = info[at : at + 1] * real_b
@@ -588,7 +593,7 @@
         slot, row = base_b + k, sz.pass_thick + k * sz.thick
         for start, count, col, moved in edge_parts(sz, moves, wide, k * sz.half, wide, row + sz.quarter):
             rows = pl.ds(start * sz.cols + col, count, stride=sz.cols)
-            plain[slot, rows, :] = plain[slot, rows, :] + moved * (speed * sea[col : col + 1, :])
+            plain[slot, rows, :] = plain[slot, rows, :] + moved * (speed * real_b * sea[col : col + 1, :])
         at_near = k * sz.side
         s_near[pl.ds(at_near + sz.quarter, sz.half), :] = wide[pl.ds(row + sz.angles, sz.half), :]
 
@@ -598,7 +603,7 @@
             return s_sea * side_transported(sz, x, near, v, s_moves, speed)
 
         s_put(sz, s_plain, slot, column)
-    turn_halo(sz, base_b, plain, turned, real_b)
+    turn_halo(sz, base_b, plain, turned)
     arrays = (plain, turned, plus, minus, s_plain, s_plus, s_minus)
     begin = jnp.where(is_even(), 0, sz.bands)
     ratio = jnp.where(is_even(), band_ratio(sz, 3 - reach), band_ratio(sz, sz.bands + 3 - reach))

time: 34.2 us -> 34.2 us (level)
  no operation moved by 1% of the time
where the time goes in v9:
time: 34.2 us; the launch traced here: 34 us
  blocking collectives  13.4 us (39%)
  starting transfers between devices  9.31 us (27%)
  Pallas kernels  8.58 us (25%)
  waiting for transfers between devices  1.82 us (5%)
  between operations  0.86 us (3%)
    all_to_all x1, blocking collectives, per_device(): recv = lax.all_to_all(msg, 'grid', split_axis=0, concat_axis=0, tiled=True)  13.4 us
    ppermute x1, starting transfers between devices, per_device(): from_e = lax.ppermute(thick, 'grid', down)  3.1 us
    ppermute x1, starting transfers between devices, per_device(): from_w = lax.ppermute(thin, 'grid', up)  3.02 us
    pallas_call x5, Pallas kernels, in_place(): return call(*[pin(a) if i in aliases else a for i, a in enumerate(args)])  2.61 us
    pallas_call x1, Pallas kernels, per_device(): kernel_call(functools.partial(pack_kernel, sz), (half(sz.thin_rows), half...  1.31 us
    pallas_call x1, Pallas kernels, per_device(): kernel_call(functools.partial(blend_kernel, sz), (field, field), 3, out_h...  1.27 us
    ppermute x1, waiting for transfers between devices, per_device(): lax.ppermute(raw_b, 'spec', [(i, (i + 1 if i % 2 else i - 1) % sz.spec) f...  1.26 us
    ppermute x1, starting transfers between devices, per_device(): recv_raw_a = lax.ppermute(raw_a, 'spec', pairs)  1.06 us
  transfers between devices with their start and end apart: 7, of which 2 were waited for; matrix products, arithmetic and copies ran while one was open for 0% of the time, Pallas kernels for 16%

profile of v9, /device:TPU:0, one launch (start us, length us, event | category | flops | bytes accessed | tf_op | source)
XLA Modules:
  0.0 34.0 jit_solution(8775572305976625385)
XLA Ops:
  0.6 0.0 copy-start.3
  0.6 0.0 copy-start.4
  0.7 0.0 copy-start.1
  0.7 0.0 copy-start
  0.7 0.0 copy-start.2
  0.7 1.3 %pack.1 = (bf16[336,128]{1,0:T(8,128)(2,1)S(1)}, bf16[672,128]{1,0:T(8,128)(2,1)S(1)}) custom-call(f32[9,36,4,128]{3,2,1,0:T(4,128)} %energy.1, f32[9,36,4,128]{3,2,1,0:T(4,128)} %nest.2, s32[4,128]{1,0:T(4,128)} %mask.3, f32[2,4,128]{2,1,0:T(4,128)} %wind.3), custom_call_target="tpu_custom_call" | custom-call | tf_op jit(solution)/shard_map/pack/pallas_call | solution.py:766
  2.0 3.0 %collective-permute-start.1 = (bf16[336,128]{1,0:T(8,128)(2,1)S(1)}, bf16[336,128]{1,0:T(8,128)(2,1)S(1)}, u32[]{:S(2)}, u32[]{:S(2)}) collective-permute-start(bf16[336,128]{1,0:T(8,128)(2,1)S(1)} %get-tuple-element.53), channel_id=1, source_target_pairs={{0,4},{4,8},{8,12},{12,16},{16,20},{20,24},{24,28},{28,0},{1,5},{5... | collective-permute-start | bytes 258056 | tf_op jit(solution)/shard_map/ppermute | solution.py:787
  5.0 3.1 %collective-permute-start = (bf16[672,128]{1,0:T(8,128)(2,1)S(1)}, bf16[672,128]{1,0:T(8,128)(2,1)S(1)}, u32[]{:S(2)}, u32[]{:S(2)}) collective-permute-start(bf16[672,128]{1,0:T(8,128)(2,1)S(1)} %get-tuple-element.52), channel_id=1, source_target_pairs={{4,0},{8,4},{12,8},{16,12},{20,16},{24,20},{28,24},{0,28},{5,1},{9... | collective-permute-start | bytes 516104 | tf_op jit(solution)/shard_map/ppermute | solution.py:786
  8.1 0.0 copy-done
  8.2 0.7 %collective-permute-start.4 = (bf16[720,128]{1,0:T(8,128)(2,1)S(1)}, bf16[720,128]{1,0:T(8,128)(2,1)S(1)}, u32[]{:S(2)}, u32[]{:S(2)}) collective-permute-start(bf16[720,128]{1,0:T(8,128)(2,1)S(1)} %get-tuple-element.74), channel_id=1, source_target_pairs={{0,3},{1,2},{2,1},{3,0},{4,7},{5,6},{6,5},{7,4},{8,11},{9,10},{10,... | collective-permute-start | bytes 552968 | tf_op jit(solution)/shard_map/ppermute | solution.py:801
  8.9 1.1 %collective-permute-start.2 = (bf16[720,128]{1,0:T(8,128)(2,1)S(1)}, bf16[720,128]{1,0:T(8,128)(2,1)S(1)}, u32[]{:S(2)}, u32[]{:S(2)}) collective-permute-start(bf16[720,128]{1,0:T(8,128)(2,1)S(1)} %get-tuple-element.56), channel_id=1, source_target_pairs={{0,1},{1,0},{2,3},{3,2},{4,5},{5,4},{6,7},{7,6},{8,9},{9,8},{10,11... | collective-permute-start | bytes 552968 | tf_op jit(solution)/shard_map/ppermute | solution.py:802
  9.9 0.0 copy-done.3
  9.9 0.0 copy-done.4
  9.9 0.0 copy-done.2
  9.9 0.2 setup.1
  10.1 0.0 copy-done.1
  10.1 0.8 %nest.3.inner = f32[1296,128]{1,0:T(8,128)S(1)} custom-call(f32[1296,128]{1,0:T(8,128)S(1)} %bitcast.17, f32[3,144,128]{2,1,0:T(8,128)S(1)} %get-tuple-element.61.moves), custom_call_target="tpu_custom_call" | custom-call | flops 30000001024 | tf_op jit(solution)/shard_map/nest/pallas_call | solution.py:812
  11.0 0.0 copy-start.5
  11.0 0.0 copy-start.6
  11.0 0.0 copy-start.7
  11.0 0.0 copy-start.8
  11.0 0.9 %local.1 = (f32[1296,128]{1,0:T(8,128)S(1)}, f32[8,128]{1,0:T(8,128)S(1)}) custom-call(f32[1296,128]{1,0:T(8,128)S(1)} %bitcast.14, f32[3,144,128]{2,1,0:T(8,128)S(1)} %get-tuple-element.62.moves, f32[8,128]{1,0:T(8,128)S(1)} %get-tuple-element.63.sea), custom_call_target="tpu_custom_call" | custom-call | flops 30000001024 | tf_op jit(solution)/shard_map/local/pallas_call | solution.py:814
  11.9 0.0 copy-done.5
  11.9 0.0 copy-done.6
  11.9 0.0 copy-done.7
  11.9 0.0 copy-done.8
  11.9 0.4 %rim.1.mix = bf16[256,768]{1,0:T(8,128)(2,1)S(1)} custom-call(s32[2,128]{1,0:T(2,128)S(1)} %bitcast.20, s32[1,128]{1,0:T(1,128)S(1)} %bitcast.21, s32[1,128]{1,0:T(1,128)S(1)} %bitcast.22, f32[3,128]{1,0:T(4,128)S(1)} %bitcast.19), custom_call_target="tpu_custom_call" | custom-call | tf_op jit(solution)/shard_map/rim/pallas_call | solution.py:805
  12.3 0.0 collective-permute-done.2.raw_a
  12.4 0.5 %beside.1.plain_in = f32[19,144,128]{2,1,0:T(8,128)S(1)} custom-call(bf16[720,128]{1,0:T(8,128)(2,1)S(1)} %collective-permute-done.2.raw_a, f32[3,144,128]{2,1,0:T(8,128)S(1)} %get-tuple-element.62.moves, f32[8,128]{1,0:T(8,128)S(1)} %get-tuple-element.63.sea), custom_call_target="tpu_custom_call" | custom-call | flops 10000000000 | tf_op jit(solution)/shard_map/beside/pallas_call | solution.py:818
  12.9 0.0 collective-permute-done.1.from_w
  12.9 0.0 collective-permute-done.from_e
  12.9 0.3 edges.1
  13.2 0.1 collective-permute-start.3
  13.2 0.1 pass.1
  13.3 0.5 %collective-permute-start.5 = (bf16[400,128]{1,0:T(8,128)(2,1)S(1)}, bf16[400,128]{1,0:T(8,128)(2,1)S(1)}, u32[]{:S(2)}, u32[]{:S(2)}) collective-permute-start(bf16[400,128]{1,0:T(8,128)(2,1)S(1)} %pass.1), channel_id=1, source_target_pairs={{0,4},{1,2},{2,1},{3,7},{4,0},{5,6},{6,5},{7,3},{8,12},{9,10},{10,... | collective-permute-start | bytes 307208 | tf_op jit(solution)/shard_map/ppermute | solution.py:843
  13.8 1.3 %collective-permute-done.4.raw_b = bf16[720,128]{1,0:T(8,128)(2,1)S(1)} collective-permute-done((bf16[720,128]{1,0:T(8,128)(2,1)S(1)}, bf16[720,128]{1,0:T(8,128)(2,1)S(1)}, u32[]{:S(2)}, u32[]{:S(2)}) %collective-permute-start.4) | collective-permute-done | bytes 184352 | tf_op jit(solution)/shard_map/ppermute | solution.py:801
  15.0 0.0 collective-permute-done.3.recv_a
  15.0 0.9 %collective-permute-start.6 = (f32[8,128]{1,0:T(8,128)S(1)}, f32[8,128]{1,0:T(8,128)S(1)}, u32[]{:S(2)}, u32[]{:S(2)}) collective-permute-start(f32[8,128]{1,0:T(8,128)S(1)} %add.3.pair), channel_id=1, source_target_pairs={{0,3},{1,2},{2,1},{3,0},{4,7},{5,6},{6,5},{7,4},{8,11},{9,10},{10,... | collective-permute-start | bytes 12296 | tf_op jit(solution)/shard_map/ppermute | solution.py:860
  15.9 0.5 %beyond.1 = (f32[19,144,128]{2,1,0:T(8,128)S(1)}, f32[200,128]{1,0:T(8,128)S(1)}) custom-call(bf16[720,128]{1,0:T(8,128)(2,1)S(1)} %collective-permute-done.4.raw_b, f32[3,144,128]{2,1,0:T(8,128)S(1)} %get-tuple-element.62.moves, f32[8,128]{1,0:T(8,128)S(1)} %get-tuple-element.63.sea, ...), custom_call_target="tpu_custom_call", output_to_operand_aliasing={{0}: (3, {})} | custom-call | flops 30000001024 | tf_op jit(solution)/shard_map/beyond/pallas_call | solution.py:728
  16.4 0.9 %inner.1 = (f32[19,144,128]{2,1,0:T(8,128)S(1)}, f32[19,168,128]{2,1,0:T(8,128)S(1)}, f32[14,168,128]{2,1,0:T(8,128)S(1)}, f32[14,168,128]{2,1,0:T(8,128)S(1)}, ...) custom-call(f32[1296,128]{1,0:T(8,128)S(1)} %get-tuple-element.70.ad, ...), custom_call_target="tpu_custom_call", output_to_operand_aliasing={{0}: (4, {})} | custom-call | tf_op jit(solution)/shard_map/inner/pallas_call | solution.py:728
  17.4 0.1 nest_edge.1
  17.5 0.5 %collective-permute-done.5.recv_b = bf16[400,128]{1,0:T(8,128)(2,1)S(1)} collective-permute-done((bf16[400,128]{1,0:T(8,128)(2,1)S(1)}, bf16[400,128]{1,0:T(8,128)(2,1)S(1)}, u32[]{:S(2)}, u32[]{:S(2)}) %collective-permute-start.5) | collective-permute-done | bytes 102432 | tf_op jit(solution)/shard_map/ppermute | solution.py:843
  18.0 0.8 %outer.1 = (f32[1296,128]{1,0:T(8,128)S(1)}, f32[19,144,128]{2,1,0:T(8,128)S(1)}, f32[19,168,128]{2,1,0:T(8,128)S(1)}, f32[14,168,128]{2,1,0:T(8,128)S(1)}, f32[...) custom-call(f32[1296,128]{1,0:T(8,128)S(1)} %get-tuple-element.70.ad, ...), custom_call_target="tpu_custom_call", output_to_operand_aliasing={{0}: (9, {}), {1}: (10, {}), {2}: (11, {}), {3}: (12, {}), ... | custom-call | tf_op jit(solution)/shard_map/outer/pallas_call | solution.py:728
  18.8 0.0 collective-permute-done.6.other
  18.8 0.5 %sources.1 = (f32[1296,128]{1,0:T(8,128)S(1)}, bf16[256,384]{1,0:T(8,128)(2,1)S(1)}) custom-call(f32[1296,128]{1,0:T(8,128)S(1)} %get-tuple-element.93.num, f32[360,128]{1,0:T(8,128)S(1)} %get-tuple-element.94.s_num, f32[8,128]{1,0:T(8,128)S(1)} %add.3.pair, f32[8,128]{1,0:T(8,128)S(1)} %collective-permute-done.6.other, bf16[256,768]{1,0:T(8,128)(2,1)S(1)} %rim.1.mix), custom_call_target="tpu_custom_call" | custom-call | tf_op jit(solution)/shard_map/sources/pallas_call | solution.py:899
  19.4 13.4 %all_to_all.11 = bf16[8,32,384]{2,1,0:T(8,128)(2,1)S(1)} all-to-all(bf16[8,32,384]{2,1,0:T(8,128)(2,1)S(1)} %bitcast.18), channel_id=1, replica_groups=mesh['grid'=8,'spec'=4] {'grid'}, dimensions={0} | all-to-all | bytes 393216 | tf_op jit(solution)/shard_map/all_to_all | solution.py:907
  32.7 1.3 %blend.1 = (f32[1296,128]{1,0:T(8,128)}, f32[1296,128]{1,0:T(8,128)}) custom-call(bf16[256,384]{1,0:T(8,128)(2,1)S(1)} %bitcast.16, f32[4,332,128]{2,1,0:T(8,128)S(1)} %get-tuple-element.98.nest_adv, f32[1296,128]{1,0:T(8,128)S(1)} %get-tuple-element.99.spectra), custom_call_target="tpu_custom_call" | custom-call | tf_op jit(solution)/shard_map/blend/pallas_call | solution.py:908
  (3 shorter events, 0.0 us)
Async XLA Ops:
  0.6 9.3 %copy-start.3 = (f32[2,4,128]{2,1,0:T(4,128)S(1)}, f32[2,4,128]{2,1,0:T(4,128)}, u32[]{:S(2)}) copy-start(f32[2,4,128]{2,1,0:T(4,128)} %wind.3) | copy-start | bytes 12292
  0.6 9.3 %copy-start.4 = (s32[4,128]{1,0:T(4,128)S(1)}, s32[4,128]{1,0:T(4,128)}, u32[]{:S(2)}) copy-start(s32[4,128]{1,0:T(4,128)} %mask.3) | copy-start | bytes 6148
  0.7 9.5 %copy-start.1 = (f32[9,36,4,128]{3,2,1,0:T(4,128)S(1)}, f32[9,36,4,128]{3,2,1,0:T(4,128)}, u32[]{:S(2)}) copy-start(f32[9,36,4,128]{3,2,1,0:T(4,128)} %nest.2) | copy-start | bytes 1990660
  0.7 7.5 %copy-start = (f32[9,36,4,128]{3,2,1,0:T(4,128)S(1)}, f32[9,36,4,128]{3,2,1,0:T(4,128)}, u32[]{:S(2)}) copy-start(f32[9,36,4,128]{3,2,1,0:T(4,128)} %energy.1) | copy-start | bytes 1990660
  0.7 9.3 %copy-start.2 = (f32[192,128]{1,0:T(8,128)S(1)}, f32[192,128]{1,0:T(8,128)}, u32[]{:S(2)}) copy-start(f32[192,128]{1,0:T(8,128)} %constant.4.clone.table) | copy-start | bytes 294916
  2.0 10.9 %collective-permute-start.1 = (bf16[336,128]{1,0:T(8,128)(2,1)S(1)}, bf16[336,128]{1,0:T(8,128)(2,1)S(1)}, u32[]{:S(2)}, u32[]{:S(2)}) collective-permute-start(bf16[336,128]{1,0:T(8,128)(2,1)S(1)} %get-tuple-element.53), channel_id=1, source_target_pairs={{0,4},{4,8},{8,12},{12,16},{16,20},{20,24},{24,28},{28,0},{1,5},{5... | collective-permute-start | bytes 258056 | tf_op jit(solution)/shard_map/ppermute | solution.py:787
  5.0 7.8 %collective-permute-start = (bf16[672,128]{1,0:T(8,128)(2,1)S(1)}, bf16[672,128]{1,0:T(8,128)(2,1)S(1)}, u32[]{:S(2)}, u32[]{:S(2)}) collective-permute-start(bf16[672,128]{1,0:T(8,128)(2,1)S(1)} %get-tuple-element.52), channel_id=1, source_target_pairs={{4,0},{8,4},{12,8},{16,12},{20,16},{24,20},{28,24},{0,28},{5,1},{9... | collective-permute-start | bytes 516104 | tf_op jit(solution)/shard_map/ppermute | solution.py:786
  8.2 6.9 %collective-permute-start.4 = (bf16[720,128]{1,0:T(8,128)(2,1)S(1)}, bf16[720,128]{1,0:T(8,128)(2,1)S(1)}, u32[]{:S(2)}, u32[]{:S(2)}) collective-permute-start(bf16[720,128]{1,0:T(8,128)(2,1)S(1)} %get-tuple-element.74), channel_id=1, source_target_pairs={{0,3},{1,2},{2,1},{3,0},{4,7},{5,6},{6,5},{7,4},{8,11},{9,10},{10,... | collective-permute-start | bytes 552968 | tf_op jit(solution)/shard_map/ppermute | solution.py:801
  8.9 3.5 %collective-permute-start.2 = (bf16[720,128]{1,0:T(8,128)(2,1)S(1)}, bf16[720,128]{1,0:T(8,128)(2,1)S(1)}, u32[]{:S(2)}, u32[]{:S(2)}) collective-permute-start(bf16[720,128]{1,0:T(8,128)(2,1)S(1)} %get-tuple-element.56), channel_id=1, source_target_pairs={{0,1},{1,0},{2,3},{3,2},{4,5},{5,4},{6,7},{7,6},{8,9},{9,8},{10,11... | collective-permute-start | bytes 552968 | tf_op jit(solution)/shard_map/ppermute | solution.py:802
  11.0 0.9 %copy-start.5 = (f32[128,3]{0,1:T(4,128)S(1)}, f32[128,3]{0,1:T(4,128)}, u32[]{:S(2)}) copy-start(f32[128,3]{0,1:T(4,128)} %param.16) | copy-start | bytes 4612
  11.0 0.9 %copy-start.6 = (s32[128,2]{0,1:T(2,128)S(1)}, s32[128,2]{0,1:T(2,128)}, u32[]{:S(2)}) copy-start(s32[128,2]{0,1:T(2,128)} %param.13) | copy-start | bytes 3076
  11.0 0.9 %copy-start.7 = (s32[128,1]{0,1:T(1,128)S(1)}, s32[128,1]{0,1:T(1,128)}, u32[]{:S(2)}) copy-start(s32[128,1]{0,1:T(1,128)} %param.14) | copy-start | bytes 1540
  11.0 0.9 %copy-start.8 = (s32[128]{0:T(128)S(1)}, s32[128]{0:T(128)}, u32[]{:S(2)}) copy-start(s32[128]{0:T(128)} %param.15) | copy-start | bytes 1540
  13.2 1.9 %collective-permute-start.3 = (bf16[384,128]{1,0:T(8,128)(2,1)S(1)}, bf16[384,128]{1,0:T(8,128)(2,1)S(1)}, u32[]{:S(2)}, u32[]{:S(2)}) collective-permute-start(bf16[384,128]{1,0:T(8,128)(2,1)S(1)} %get-tuple-element.73), channel_id=1, source_target_pairs={{0,1},{1,0},{2,3},{3,2},{4,5},{5,4},{6,7},{7,6},{8,9},{9,8},{10,11... | collective-permute-start | bytes 294920 | tf_op jit(solution)/shard_map/ppermute | solution.py:842
  13.3 4.7 %collective-permute-start.5 = (bf16[400,128]{1,0:T(8,128)(2,1)S(1)}, bf16[400,128]{1,0:T(8,128)(2,1)S(1)}, u32[]{:S(2)}, u32[]{:S(2)}) collective-permute-start(bf16[400,128]{1,0:T(8,128)(2,1)S(1)} %pass.1), channel_id=1, source_target_pairs={{0,4},{1,2},{2,1},{3,7},{4,0},{5,6},{6,5},{7,3},{8,12},{9,10},{10,... | collective-permute-start | bytes 307208 | tf_op jit(solution)/shard_map/ppermute | solution.py:843
  15.0 3.8 %collective-permute-start.6 = (f32[8,128]{1,0:T(8,128)S(1)}, f32[8,128]{1,0:T(8,128)S(1)}, u32[]{:S(2)}, u32[]{:S(2)}) collective-permute-start(f32[8,128]{1,0:T(8,128)S(1)} %add.3.pair), channel_id=1, source_target_pairs={{0,3},{1,2},{2,1},{3,0},{4,7},{5,6},{6,5},{7,4},{8,11},{9,10},{10,... | collective-permute-start | bytes 12296 | tf_op jit(solution)/shard_map/ppermute | solution.py:860

commit v10 on v9

--- a/solution.py
+++ b/solution.py
@@ -192,7 +192,10 @@
 def pass_kernel(sz, from_w, from_e, msg, wide_w, wide_e, tmp):
     wide_w[...] = from_w[...].astype(F32)
     wide_e[...] = from_e[...].astype(F32)
-    tmp[...] = jnp.zeros_like(tmp)
+    for row, end in ((reach * sz.half, sz.pass_thick), (sz.pass_thick + reach * sz.thick, sz.pass_rows)):
+        row = row // VREG * VREG
+        if end > row:
+            tmp[pl.ds(row, end - row), :] = jnp.zeros((end - row, sz.lat), F32)
     first = far_band(sz)
     count = reach * sz.half
     tmp[pl.ds(0, count), :] = wide_w[pl.ds(first * sz.half, count), :]

time: 34.2 us -> 34.2 us (level)
  no operation moved by 1% of the time
where the time goes in v10:
time: 34.2 us; the launch traced here: 34 us
  blocking collectives  13.4 us (39%)
  starting transfers between devices  9.31 us (27%)
  Pallas kernels  8.58 us (25%)
  waiting for transfers between devices  1.82 us (5%)
  between operations  0.86 us (3%)
    all_to_all x1, blocking collectives, per_device(): recv = lax.all_to_all(msg, 'grid', split_axis=0, concat_axis=0, tiled=True)  13.4 us
    ppermute x1, starting transfers between devices, per_device(): from_e = lax.ppermute(thick, 'grid', down)  3.1 us
    ppermute x1, starting transfers between devices, per_device(): from_w = lax.ppermute(thin, 'grid', up)  3.02 us
    pallas_call x5, Pallas kernels, in_place(): return call(*[pin(a) if i in aliases else a for i, a in enumerate(args)])  2.61 us
    pallas_call x1, Pallas kernels, per_device(): kernel_call(functools.partial(pack_kernel, sz), (half(sz.thin_rows), half...  1.31 us
    pallas_call x1, Pallas kernels, per_device(): kernel_call(functools.partial(blend_kernel, sz), (field, field), 3, out_h...  1.27 us
    ppermute x1, waiting for transfers between devices, per_device(): lax.ppermute(raw_b, 'spec', [(i, (i + 1 if i % 2 else i - 1) % sz.spec) f...  1.26 us
    ppermute x1, starting transfers between devices, per_device(): recv_raw_a = lax.ppermute(raw_a, 'spec', pairs)  1.06 us
  transfers between devices with their start and end apart: 7, of which 2 were waited for; matrix products, arithmetic and copies ran while one was open for 0% of the time, Pallas kernels for 16%

profile of v10, /device:TPU:0, one launch (start us, length us, event | category | flops | bytes accessed | tf_op | source)
XLA Modules:
  0.0 34.0 jit_solution(8775572305976625385)
XLA Ops:
  0.6 0.0 copy-start.3
  0.6 0.0 copy-start.4
  0.7 0.0 copy-start.1
  0.7 0.0 copy-start
  0.7 0.0 copy-start.2
  0.7 1.3 %pack.1 = (bf16[336,128]{1,0:T(8,128)(2,1)S(1)}, bf16[672,128]{1,0:T(8,128)(2,1)S(1)}) custom-call(f32[9,36,4,128]{3,2,1,0:T(4,128)} %energy.1, f32[9,36,4,128]{3,2,1,0:T(4,128)} %nest.2, s32[4,128]{1,0:T(4,128)} %mask.3, f32[2,4,128]{2,1,0:T(4,128)} %wind.3), custom_call_target="tpu_custom_call" | custom-call | tf_op jit(solution)/shard_map/pack/pallas_call | solution.py:769
  2.0 3.0 %collective-permute-start.1 = (bf16[336,128]{1,0:T(8,128)(2,1)S(1)}, bf16[336,128]{1,0:T(8,128)(2,1)S(1)}, u32[]{:S(2)}, u32[]{:S(2)}) collective-permute-start(bf16[336,128]{1,0:T(8,128)(2,1)S(1)} %get-tuple-element.53), channel_id=1, source_target_pairs={{0,4},{4,8},{8,12},{12,16},{16,20},{20,24},{24,28},{28,0},{1,5},{5... | collective-permute-start | bytes 258056 | tf_op jit(solution)/shard_map/ppermute | solution.py:790
  5.0 3.1 %collective-permute-start = (bf16[672,128]{1,0:T(8,128)(2,1)S(1)}, bf16[672,128]{1,0:T(8,128)(2,1)S(1)}, u32[]{:S(2)}, u32[]{:S(2)}) collective-permute-start(bf16[672,128]{1,0:T(8,128)(2,1)S(1)} %get-tuple-element.52), channel_id=1, source_target_pairs={{4,0},{8,4},{12,8},{16,12},{20,16},{24,20},{28,24},{0,28},{5,1},{9... | collective-permute-start | bytes 516104 | tf_op jit(solution)/shard_map/ppermute | solution.py:789
  8.1 0.0 copy-done
  8.2 0.7 %collective-permute-start.4 = (bf16[720,128]{1,0:T(8,128)(2,1)S(1)}, bf16[720,128]{1,0:T(8,128)(2,1)S(1)}, u32[]{:S(2)}, u32[]{:S(2)}) collective-permute-start(bf16[720,128]{1,0:T(8,128)(2,1)S(1)} %get-tuple-element.74), channel_id=1, source_target_pairs={{0,3},{1,2},{2,1},{3,0},{4,7},{5,6},{6,5},{7,4},{8,11},{9,10},{10,... | collective-permute-start | bytes 552968 | tf_op jit(solution)/shard_map/ppermute | solution.py:804
  8.9 1.1 %collective-permute-start.2 = (bf16[720,128]{1,0:T(8,128)(2,1)S(1)}, bf16[720,128]{1,0:T(8,128)(2,1)S(1)}, u32[]{:S(2)}, u32[]{:S(2)}) collective-permute-start(bf16[720,128]{1,0:T(8,128)(2,1)S(1)} %get-tuple-element.56), channel_id=1, source_target_pairs={{0,1},{1,0},{2,3},{3,2},{4,5},{5,4},{6,7},{7,6},{8,9},{9,8},{10,11... | collective-permute-start | bytes 552968 | tf_op jit(solution)/shard_map/ppermute | solution.py:805
  9.9 0.0 copy-done.3
  9.9 0.0 copy-done.4
  9.9 0.0 copy-done.2
  9.9 0.2 setup.1
  10.1 0.0 copy-done.1
  10.1 0.8 %nest.3.inner = f32[1296,128]{1,0:T(8,128)S(1)} custom-call(f32[1296,128]{1,0:T(8,128)S(1)} %bitcast.17, f32[3,144,128]{2,1,0:T(8,128)S(1)} %get-tuple-element.61.moves), custom_call_target="tpu_custom_call" | custom-call | flops 30000001024 | tf_op jit(solution)/shard_map/nest/pallas_call | solution.py:815
  11.0 0.0 copy-start.5
  11.0 0.0 copy-start.6
  11.0 0.0 copy-start.7
  11.0 0.0 copy-start.8
  11.0 0.9 %local.1 = (f32[1296,128]{1,0:T(8,128)S(1)}, f32[8,128]{1,0:T(8,128)S(1)}) custom-call(f32[1296,128]{1,0:T(8,128)S(1)} %bitcast.14, f32[3,144,128]{2,1,0:T(8,128)S(1)} %get-tuple-element.62.moves, f32[8,128]{1,0:T(8,128)S(1)} %get-tuple-element.63.sea), custom_call_target="tpu_custom_call" | custom-call | flops 30000001024 | tf_op jit(solution)/shard_map/local/pallas_call | solution.py:817
  11.9 0.0 copy-done.5
  11.9 0.0 copy-done.6
  11.9 0.0 copy-done.7
  11.9 0.0 copy-done.8
  11.9 0.4 %rim.1.mix = bf16[256,768]{1,0:T(8,128)(2,1)S(1)} custom-call(s32[2,128]{1,0:T(2,128)S(1)} %bitcast.20, s32[1,128]{1,0:T(1,128)S(1)} %bitcast.21, s32[1,128]{1,0:T(1,128)S(1)} %bitcast.22, f32[3,128]{1,0:T(4,128)S(1)} %bitcast.19), custom_call_target="tpu_custom_call" | custom-call | tf_op jit(solution)/shard_map/rim/pallas_call | solution.py:808
  12.3 0.0 collective-permute-done.2.raw_a
  12.4 0.5 %beside.1.plain_in = f32[19,144,128]{2,1,0:T(8,128)S(1)} custom-call(bf16[720,128]{1,0:T(8,128)(2,1)S(1)} %collective-permute-done.2.raw_a, f32[3,144,128]{2,1,0:T(8,128)S(1)} %get-tuple-element.62.moves, f32[8,128]{1,0:T(8,128)S(1)} %get-tuple-element.63.sea), custom_call_target="tpu_custom_call" | custom-call | flops 10000000000 | tf_op jit(solution)/shard_map/beside/pallas_call | solution.py:821
  12.9 0.0 collective-permute-done.1.from_w
  12.9 0.0 collective-permute-done.from_e
  12.9 0.3 edges.1
  13.2 0.1 collective-permute-start.3
  13.2 0.1 pass.1
  13.3 0.5 %collective-permute-start.5 = (bf16[400,128]{1,0:T(8,128)(2,1)S(1)}, bf16[400,128]{1,0:T(8,128)(2,1)S(1)}, u32[]{:S(2)}, u32[]{:S(2)}) collective-permute-start(bf16[400,128]{1,0:T(8,128)(2,1)S(1)} %pass.1), channel_id=1, source_target_pairs={{0,4},{1,2},{2,1},{3,7},{4,0},{5,6},{6,5},{7,3},{8,12},{9,10},{10,... | collective-permute-start | bytes 307208 | tf_op jit(solution)/shard_map/ppermute | solution.py:846
  13.8 1.3 %collective-permute-done.4.raw_b = bf16[720,128]{1,0:T(8,128)(2,1)S(1)} collective-permute-done((bf16[720,128]{1,0:T(8,128)(2,1)S(1)}, bf16[720,128]{1,0:T(8,128)(2,1)S(1)}, u32[]{:S(2)}, u32[]{:S(2)}) %collective-permute-start.4) | collective-permute-done | bytes 184352 | tf_op jit(solution)/shard_map/ppermute | solution.py:804
  15.0 0.0 collective-permute-done.3.recv_a
  15.0 0.9 %collective-permute-start.6 = (f32[8,128]{1,0:T(8,128)S(1)}, f32[8,128]{1,0:T(8,128)S(1)}, u32[]{:S(2)}, u32[]{:S(2)}) collective-permute-start(f32[8,128]{1,0:T(8,128)S(1)} %add.3.pair), channel_id=1, source_target_pairs={{0,3},{1,2},{2,1},{3,0},{4,7},{5,6},{6,5},{7,4},{8,11},{9,10},{10,... | collective-permute-start | bytes 12296 | tf_op jit(solution)/shard_map/ppermute | solution.py:863
  15.9 0.5 %beyond.1 = (f32[19,144,128]{2,1,0:T(8,128)S(1)}, f32[200,128]{1,0:T(8,128)S(1)}) custom-call(bf16[720,128]{1,0:T(8,128)(2,1)S(1)} %collective-permute-done.4.raw_b, f32[3,144,128]{2,1,0:T(8,128)S(1)} %get-tuple-element.62.moves, f32[8,128]{1,0:T(8,128)S(1)} %get-tuple-element.63.sea, ...), custom_call_target="tpu_custom_call", output_to_operand_aliasing={{0}: (3, {})} | custom-call | flops 30000001024 | tf_op jit(solution)/shard_map/beyond/pallas_call | solution.py:731
  16.4 0.9 %inner.1 = (f32[19,144,128]{2,1,0:T(8,128)S(1)}, f32[19,168,128]{2,1,0:T(8,128)S(1)}, f32[14,168,128]{2,1,0:T(8,128)S(1)}, f32[14,168,128]{2,1,0:T(8,128)S(1)}, ...) custom-call(f32[1296,128]{1,0:T(8,128)S(1)} %get-tuple-element.70.ad, ...), custom_call_target="tpu_custom_call", output_to_operand_aliasing={{0}: (4, {})} | custom-call | tf_op jit(solution)/shard_map/inner/pallas_call | solution.py:731
  17.4 0.1 nest_edge.1
  17.5 0.5 %collective-permute-done.5.recv_b = bf16[400,128]{1,0:T(8,128)(2,1)S(1)} collective-permute-done((bf16[400,128]{1,0:T(8,128)(2,1)S(1)}, bf16[400,128]{1,0:T(8,128)(2,1)S(1)}, u32[]{:S(2)}, u32[]{:S(2)}) %collective-permute-start.5) | collective-permute-done | bytes 102432 | tf_op jit(solution)/shard_map/ppermute | solution.py:846
  18.0 0.8 %outer.1 = (f32[1296,128]{1,0:T(8,128)S(1)}, f32[19,144,128]{2,1,0:T(8,128)S(1)}, f32[19,168,128]{2,1,0:T(8,128)S(1)}, f32[14,168,128]{2,1,0:T(8,128)S(1)}, f32[...) custom-call(f32[1296,128]{1,0:T(8,128)S(1)} %get-tuple-element.70.ad, ...), custom_call_target="tpu_custom_call", output_to_operand_aliasing={{0}: (9, {}), {1}: (10, {}), {2}: (11, {}), {3}: (12, {}), ... | custom-call | tf_op jit(solution)/shard_map/outer/pallas_call | solution.py:731
  18.8 0.0 collective-permute-done.6.other
  18.8 0.5 %sources.1 = (f32[1296,128]{1,0:T(8,128)S(1)}, bf16[256,384]{1,0:T(8,128)(2,1)S(1)}) custom-call(f32[1296,128]{1,0:T(8,128)S(1)} %get-tuple-element.93.num, f32[360,128]{1,0:T(8,128)S(1)} %get-tuple-element.94.s_num, f32[8,128]{1,0:T(8,128)S(1)} %add.3.pair, f32[8,128]{1,0:T(8,128)S(1)} %collective-permute-done.6.other, bf16[256,768]{1,0:T(8,128)(2,1)S(1)} %rim.1.mix), custom_call_target="tpu_custom_call" | custom-call | tf_op jit(solution)/shard_map/sources/pallas_call | solution.py:902
  19.4 13.4 %all_to_all.11 = bf16[8,32,384]{2,1,0:T(8,128)(2,1)S(1)} all-to-all(bf16[8,32,384]{2,1,0:T(8,128)(2,1)S(1)} %bitcast.18), channel_id=1, replica_groups=mesh['grid'=8,'spec'=4] {'grid'}, dimensions={0} | all-to-all | bytes 393216 | tf_op jit(solution)/shard_map/all_to_all | solution.py:910
  32.7 1.3 %blend.1 = (f32[1296,128]{1,0:T(8,128)}, f32[1296,128]{1,0:T(8,128)}) custom-call(bf16[256,384]{1,0:T(8,128)(2,1)S(1)} %bitcast.16, f32[4,332,128]{2,1,0:T(8,128)S(1)} %get-tuple-element.98.nest_adv, f32[1296,128]{1,0:T(8,128)S(1)} %get-tuple-element.99.spectra), custom_call_target="tpu_custom_call" | custom-call | tf_op jit(solution)/shard_map/blend/pallas_call | solution.py:911
  (3 shorter events, 0.0 us)
Async XLA Ops:
  0.6 9.3 %copy-start.3 = (f32[2,4,128]{2,1,0:T(4,128)S(1)}, f32[2,4,128]{2,1,0:T(4,128)}, u32[]{:S(2)}) copy-start(f32[2,4,128]{2,1,0:T(4,128)} %wind.3) | copy-start | bytes 12292
  0.6 9.3 %copy-start.4 = (s32[4,128]{1,0:T(4,128)S(1)}, s32[4,128]{1,0:T(4,128)}, u32[]{:S(2)}) copy-start(s32[4,128]{1,0:T(4,128)} %mask.3) | copy-start | bytes 6148
  0.7 9.5 %copy-start.1 = (f32[9,36,4,128]{3,2,1,0:T(4,128)S(1)}, f32[9,36,4,128]{3,2,1,0:T(4,128)}, u32[]{:S(2)}) copy-start(f32[9,36,4,128]{3,2,1,0:T(4,128)} %nest.2) | copy-start | bytes 1990660
  0.7 7.5 %copy-start = (f32[9,36,4,128]{3,2,1,0:T(4,128)S(1)}, f32[9,36,4,128]{3,2,1,0:T(4,128)}, u32[]{:S(2)}) copy-start(f32[9,36,4,128]{3,2,1,0:T(4,128)} %energy.1) | copy-start | bytes 1990660
  0.7 9.3 %copy-start.2 = (f32[192,128]{1,0:T(8,128)S(1)}, f32[192,128]{1,0:T(8,128)}, u32[]{:S(2)}) copy-start(f32[192,128]{1,0:T(8,128)} %constant.4.clone.table) | copy-start | bytes 294916
  2.0 10.9 %collective-permute-start.1 = (bf16[336,128]{1,0:T(8,128)(2,1)S(1)}, bf16[336,128]{1,0:T(8,128)(2,1)S(1)}, u32[]{:S(2)}, u32[]{:S(2)}) collective-permute-start(bf16[336,128]{1,0:T(8,128)(2,1)S(1)} %get-tuple-element.53), channel_id=1, source_target_pairs={{0,4},{4,8},{8,12},{12,16},{16,20},{20,24},{24,28},{28,0},{1,5},{5... | collective-permute-start | bytes 258056 | tf_op jit(solution)/shard_map/ppermute | solution.py:790
  5.0 7.8 %collective-permute-start = (bf16[672,128]{1,0:T(8,128)(2,1)S(1)}, bf16[672,128]{1,0:T(8,128)(2,1)S(1)}, u32[]{:S(2)}, u32[]{:S(2)}) collective-permute-start(bf16[672,128]{1,0:T(8,128)(2,1)S(1)} %get-tuple-element.52), channel_id=1, source_target_pairs={{4,0},{8,4},{12,8},{16,12},{20,16},{24,20},{28,24},{0,28},{5,1},{9... | collective-permute-start | bytes 516104 | tf_op jit(solution)/shard_map/ppermute | solution.py:789
  8.2 6.9 %collective-permute-start.4 = (bf16[720,128]{1,0:T(8,128)(2,1)S(1)}, bf16[720,128]{1,0:T(8,128)(2,1)S(1)}, u32[]{:S(2)}, u32[]{:S(2)}) collective-permute-start(bf16[720,128]{1,0:T(8,128)(2,1)S(1)} %get-tuple-element.74), channel_id=1, source_target_pairs={{0,3},{1,2},{2,1},{3,0},{4,7},{5,6},{6,5},{7,4},{8,11},{9,10},{10,... | collective-permute-start | bytes 552968 | tf_op jit(solution)/shard_map/ppermute | solution.py:804
  8.9 3.5 %collective-permute-start.2 = (bf16[720,128]{1,0:T(8,128)(2,1)S(1)}, bf16[720,128]{1,0:T(8,128)(2,1)S(1)}, u32[]{:S(2)}, u32[]{:S(2)}) collective-permute-start(bf16[720,128]{1,0:T(8,128)(2,1)S(1)} %get-tuple-element.56), channel_id=1, source_target_pairs={{0,1},{1,0},{2,3},{3,2},{4,5},{5,4},{6,7},{7,6},{8,9},{9,8},{10,11... | collective-permute-start | bytes 552968 | tf_op jit(solution)/shard_map/ppermute | solution.py:805
  11.0 0.9 %copy-start.5 = (f32[128,3]{0,1:T(4,128)S(1)}, f32[128,3]{0,1:T(4,128)}, u32[]{:S(2)}) copy-start(f32[128,3]{0,1:T(4,128)} %param.16) | copy-start | bytes 4612
  11.0 0.9 %copy-start.6 = (s32[128,2]{0,1:T(2,128)S(1)}, s32[128,2]{0,1:T(2,128)}, u32[]{:S(2)}) copy-start(s32[128,2]{0,1:T(2,128)} %param.13) | copy-start | bytes 3076
  11.0 0.9 %copy-start.7 = (s32[128,1]{0,1:T(1,128)S(1)}, s32[128,1]{0,1:T(1,128)}, u32[]{:S(2)}) copy-start(s32[128,1]{0,1:T(1,128)} %param.14) | copy-start | bytes 1540
  11.0 0.9 %copy-start.8 = (s32[128]{0:T(128)S(1)}, s32[128]{0:T(128)}, u32[]{:S(2)}) copy-start(s32[128]{0:T(128)} %param.15) | copy-start | bytes 1540
  13.2 1.9 %collective-permute-start.3 = (bf16[384,128]{1,0:T(8,128)(2,1)S(1)}, bf16[384,128]{1,0:T(8,128)(2,1)S(1)}, u32[]{:S(2)}, u32[]{:S(2)}) collective-permute-start(bf16[384,128]{1,0:T(8,128)(2,1)S(1)} %get-tuple-element.73), channel_id=1, source_target_pairs={{0,1},{1,0},{2,3},{3,2},{4,5},{5,4},{6,7},{7,6},{8,9},{9,8},{10,11... | collective-permute-start | bytes 294920 | tf_op jit(solution)/shard_map/ppermute | solution.py:845
  13.3 4.7 %collective-permute-start.5 = (bf16[400,128]{1,0:T(8,128)(2,1)S(1)}, bf16[400,128]{1,0:T(8,128)(2,1)S(1)}, u32[]{:S(2)}, u32[]{:S(2)}) collective-permute-start(bf16[400,128]{1,0:T(8,128)(2,1)S(1)} %pass.1), channel_id=1, source_target_pairs={{0,4},{1,2},{2,1},{3,7},{4,0},{5,6},{6,5},{7,3},{8,12},{9,10},{10,... | collective-permute-start | bytes 307208 | tf_op jit(solution)/shard_map/ppermute | solution.py:846
  15.0 3.8 %collective-permute-start.6 = (f32[8,128]{1,0:T(8,128)S(1)}, f32[8,128]{1,0:T(8,128)S(1)}, u32[]{:S(2)}, u32[]{:S(2)}) collective-permute-start(f32[8,128]{1,0:T(8,128)S(1)} %add.3.pair), channel_id=1, source_target_pairs={{0,3},{1,2},{2,1},{3,0},{4,7},{5,6},{6,5},{7,4},{8,11},{9,10},{10,... | collective-permute-start | bytes 12296 | tf_op jit(solution)/shard_map/ppermute | solution.py:863
